TPU v7x, 32 devices: a whole 2x2x4 slice. The times are simulated.
32 devices in a mesh: dp: 8 (over z, y), tensor: 4 (over x, core).
Axes of the slice: x: 2, y: 2, z: 4, core: 2. Of those that a mesh axis runs over, the one named last changes fastest.
Arguments:
- tokens: bfloat16 [4096, 4096], P(('dp', 'tensor')), may hold values from -6 to 6
- weight: bfloat16 [4096, 4096], P('tensor', 'dp'), may hold values from -0.09375 to 0.09375
Outputs:
- projected: bfloat16 [4096, 4096], P('dp', 'tensor')
All inputs are finite; a program needn't handle non-finite values.
Results may differ from a plain program's by a relative error of at most 0.0057.
Values may be sent and summed in bfloat16 or wider, within the bound.
No kernel may reach another device: no remote copies, remote signals or barrier semaphores. Data moves between devices by JAX's collectives and lax.ppermute only.
A program may use at most 64 MiB of HBM per device.

v0:
```python
import jax
import jax.numpy as jnp
from jax import lax
from jax.sharding import PartitionSpec as P


def contract_last(left, right):
    return lax.dot_general(
        left, right, (((1,), (1,)), ((), ())), preferred_element_type=jnp.float32
    )


def contract_first(left, right):
    return lax.dot_general(
        left, right, (((0,), (0,)), ((), ())), preferred_element_type=jnp.float32
    )


def on_device(tokens, weight):
    col_slab = lax.all_gather(weight, "tensor", axis=0, tiled=True)
    term = contract_last(col_slab, weight)
    gram_cols = lax.psum(term, "dp").astype(jnp.bfloat16)
    update = 1.5 * weight.astype(jnp.float32) - 0.5 * contract_first(gram_cols, col_slab)
    ortho = update.astype(jnp.bfloat16)
    full_rows = lax.all_gather(ortho, "dp", axis=1, tiled=True)
    result = contract_last(lax.all_gather(tokens, "tensor", axis=0, tiled=True), full_rows)
    return result.astype(jnp.bfloat16)


def solution(mesh):
    placed = (P(("dp", "tensor"), None), P("tensor", "dp"))
    return jax.shard_map(
        on_device, mesh=mesh, in_specs=placed, out_specs=P("dp", "tensor"), check_vma=False
    )
```

profile of v0, /device:TPU:0, one launch (start us, length us, event | category | flops | bytes accessed | tf_op | source)
XLA Modules:
  0.0 855.3 jit_solution(1601401629869962513)
XLA Ops:
  6.5 0.0 all-gather.4.cloned.1.call-start
  6.5 0.7 all-gather.4.cloned.1.call-update
  7.3 0.0 all-gather.8.cloned.1.call-start
  7.3 0.7 all-gather.8.cloned.1.call-update
  8.0 0.0 all-gather.6.cloned.1.call-start
  8.1 38.1 %all-gather.4.cloned.1.call-done = bf16[4096,512]{1,0:T(8,128)(2,1)} async-done(((bf16[1024,512]{1,0:T(8,128)(2,1)}), bf16[4096,512]{1,0:T(8,128)(2,1)}) %all-gather.4.cloned.1.call-update) | async-done | bytes 4194320 | tf_op jit(solution)/shard_map/all_gather | solution.py:20
  46.1 13.8 %fusion.5 = f32[4096,1024]{1,0:T(8,128)} fusion(bf16[4096,512]{1,0:T(8,128)(2,1)} %all-gather.4.cloned.1.call-done, bf16[1024,512]{1,0:T(8,128)(2,1)} %param.3), kind=kOutput, calls=%fused_computation.5 | convolution fusion | flops 4294967296 | bytes 22020096 | tf_op jit(solution)/shard_map/dot_general | solution.py:8
  60.0 0.0 copy-start
  60.0 645.1 %all-reduce.1 = bf16[4096,1024]{1,0:T(8,128)(2,1)} all-reduce(f32[4096,1024]{1,0:T(8,128)} %fusion.5), channel_id=1, replica_groups=mesh['dp'=8,'tensor'=4] {'dp'}, use_global_device_ids=true, to_apply=%region_0.0 | all-reduce | flops 4194304 | bytes 25165824 | tf_op jit(solution)/shard_map/psum | solution.py:22
  705.1 0.0 copy-done
  705.1 10.1 %subtract_convert_fusion = bf16[1024,512]{1,0:T(8,128)(2,1)} fusion(bf16[1024,512]{1,0:T(8,128)(2,1)S(1)} %copy-done, bf16[4096,512]{1,0:T(8,128)(2,1)} %all-gather.4.cloned.1.call-done, bf16[4096,1024]{1,0:T(8,128)(2,1)} %all-reduce.1), kind=kOutput, calls=%fused_computation.2 | convolution fusion | flops 4297588736 | bytes 14680064 | tf_op jit(solution)/shard_map/dot_general | solution.py:14
  715.1 0.0 all-gather.6.cloned.1.call-update
  715.2 0.0 all-gather.8.cloned.1.call-done
  715.2 123.1 %all-gather.6.cloned.1.call-done = bf16[1024,4096]{1,0:T(8,128)(2,1)} async-done(((bf16[1024,512]{1,0:T(8,128)(2,1)}), bf16[1024,4096]{1,0:T(8,128)(2,1)}) %all-gather.6.cloned.1.call-update) | async-done | bytes 8388624 | tf_op jit(solution)/shard_map/all_gather | solution.py:25
  838.3 9.1 %fusion.4 = bf16[512,1024]{0,1:T(8,128)(2,1)S(1)} fusion(bf16[1024,4096]{1,0:T(8,128)(2,1)} %all-gather.6.cloned.1.call-done, bf16[512,4096]{1,0:T(8,128)(2,1)} %all-gather.8.cloned.1.call-done), kind=kOutput, calls=%fused_computation.4 | convolution fusion | flops 4295491584 | bytes 13631488 | tf_op jit(solution)/shard_map/dot_general | solution.py:8
  847.4 1.3 copy.3
Async XLA Ops:
  6.5 39.6 %all-gather.4.cloned.1.call-start = ((), (), s32[]{:S(2)}) async-start(), calls=%async_computation | async-start | bytes 5242880 | tf_op jit(solution)/shard_map/all_gather | solution.py:20
  7.3 707.9 %all-gather.8.cloned.1.call-start = ((), (), s32[]{:S(2)}) async-start(), calls=%async_computation.2 | async-start | bytes 5242880 | tf_op jit(solution)/shard_map/all_gather | solution.py:26
  8.0 830.3 %all-gather.6.cloned.1.call-start = ((), (), s32[]{:S(2)}) async-start(), calls=%async_computation.1 | async-start | bytes 9437184 | tf_op jit(solution)/shard_map/all_gather | solution.py:25
  60.0 645.1 %copy-start = (bf16[1024,512]{1,0:T(8,128)(2,1)S(1)}, bf16[1024,512]{1,0:T(8,128)(2,1)}, u32[]{:S(2)}) copy-start(bf16[1024,512]{1,0:T(8,128)(2,1)} %param.3) | copy-start | bytes 3145732
Sparse Core Ops, SparseCore 0:
  8.9 37.1 all-gather.3
  47.7 34.4 all-gather.7
  715.3 122.9 all-gather.5
where the time goes:
time: 855 us
  blocking collectives  645 us (75%)
  waiting for transfers between devices  163 us (19%)
  matrix products  33 us (4%)
  between operations  13.1 us (2%)
    psum x1, blocking collectives, on_device(): gram_cols = lax.psum(term, 'dp').astype(jnp.bfloat16)  645 us
    all_gather x1, waiting for transfers between devices, on_device(): full_rows = lax.all_gather(ortho, 'dp', axis=1, tiled=True)  123 us
    all_gather x1, waiting for transfers between devices, on_device(): col_slab = lax.all_gather(weight, 'tensor', axis=0, tiled=True)  38.1 us
    dot_general x2, matrix products, contract_last(): lax.dot_general(left, right, (((1,), (1,)), ((), ())), preferred_element_...  22.9 us
  transfers between devices with their start and end apart: 3, of which 2 were waited for; matrix products, arithmetic and copies ran while one was open for 3% of the time, Pallas kernels for 0%

commit v1 on v0

v1 whole, which is shorter than its diff:
```python
import functools

import jax
import jax.numpy as jnp
from jax import lax
from jax.experimental import pallas as pl
from jax.experimental.pallas import tpu as pltpu
from jax.sharding import PartitionSpec as P

BF = jnp.bfloat16
F32 = jnp.float32
ANY = pl.BlockSpec(memory_space=pl.ANY)
SMEM = pl.BlockSpec(memory_space=pltpu.SMEM)
VMEM = pl.BlockSpec(memory_space=pltpu.VMEM)


def contract_last(left, right):
    return lax.dot_general(left, right, (((1,), (1,)), ((), ())), preferred_element_type=F32)


def contract(left, right):
    return lax.dot_general(left, right, (((1,), (0,)), ((), ())), preferred_element_type=F32)


def gathered_form(tokens, weight):
    rows = lax.all_gather(weight, "dp", axis=1, tiled=True)
    toks = lax.all_gather(tokens, "tensor", axis=0, tiled=True)
    first = contract_last(toks, rows)
    part = contract(first.astype(BF), rows).astype(BF)
    second = lax.psum(part, "tensor")
    return (1.5 * first - 0.5 * contract_last(second, rows)).astype(BF)


def call(body, ins, outs, scratch, flops):
    nbytes = sum(v.size * v.dtype.itemsize for v in ins) + sum(
        v.size * v.dtype.itemsize for v in outs
    )
    return pl.pallas_call(
        body,
        out_shape=outs,
        in_specs=[SMEM] + [ANY] * (len(ins) - 1),
        out_specs=[VMEM] * len(outs),
        scratch_shapes=scratch,
        compiler_params=pltpu.CompilerParams(vmem_limit_bytes=48 << 20),
        cost_estimate=pl.CostEstimate(flops=flops, bytes_accessed=nbytes, transcendentals=0),
    )(*ins)


def shape(dims, dtype):
    return jax.ShapeDtypeStruct(dims, dtype)


def tiles(extent, step=256):
    return [(at, min(step, extent - at)) for at in range(0, extent, step)]


def project(where, toks, parts, acc, width, rows, last):
    count = toks.shape[0]
    depth = width * len(parts)
    flat = [piece for _, pieces in parts for piece in pieces]

    def body(where_ref, t_ref, *refs):
        pieces = refs[: len(flat)]
        refs = refs[len(flat) :]
        if acc is not None:
            acc_ref, refs = refs[0], refs[1:]
        outs, (t_buf, w_buf, sem) = refs[: 2 if last else 1], refs[2 if last else 1 :]
        copies = []
        at = 0
        for k, (slot, own) in enumerate(parts):
            cols = pl.ds(k * width, width)
            src = pl.multiple_of(where_ref[slot] * width, width)
            copies.append((t_ref.at[:, pl.ds(src, width)], t_buf.at[:, cols]))
            row = 0
            for piece in own:
                height = piece.shape[0]
                copies.append((pieces[at], w_buf.at[pl.ds(row, height), cols]))
                row += height
                at += 1
        if acc is not None:
            copies.append((acc_ref, outs[0]))
        copies = [pltpu.make_async_copy(a, b, sem.at[i]) for i, (a, b) in enumerate(copies)]
        for c in copies:
            c.start()
        for c in copies:
            c.wait()
        for at, size in tiles(rows):
            term = contract_last(t_buf[...], w_buf[at : at + size, :])
            if acc is not None:
                term += outs[0][:, at : at + size]
            outs[0][:, at : at + size] = term
            if last:
                outs[1][:, at : at + size] = term.astype(BF)

    outs = [shape((count, rows), F32)] + ([shape((count, rows), BF)] if last else [])
    ins = [where, toks] + flat + ([acc] if acc is not None else [])
    scratch = [
        pltpu.VMEM((count, depth), BF),
        pltpu.VMEM((rows, depth), BF),
        pltpu.SemaphoreType.DMA((len(parts) + len(flat) + 1,)),
    ]
    return call(body, ins, outs, scratch, 2 * count * rows * depth)


def spread(where, p, chunks, width, rows, keep):
    count = p.shape[0]
    half = width // 2
    flat = [piece for pieces in chunks for piece in pieces]
    dtype = F32 if keep else BF

    def body(where_ref, p_ref, *refs):
        pieces, (out, p_buf, w_buf, sem) = refs[: len(flat)], refs[len(flat) :]
        core = where_ref[where.shape[0] - 1]
        src = pl.multiple_of((core if keep else 1 - core) * half, half)
        copies = [(p_ref, p_buf)]
        at = 0
        for k, own in enumerate(chunks):
            row = 0
            for piece in own:
                height = piece.shape[0]
                copies.append(
                    (pieces[at].at[:, pl.ds(src, half)], w_buf.at[k, pl.ds(row, height), :])
                )
                row += height
                at += 1
        copies = [pltpu.make_async_copy(a, b, sem.at[i]) for i, (a, b) in enumerate(copies)]
        for c in copies:
            c.start()
        for c in copies:
            c.wait()
        for k in range(len(chunks)):
            out[:, k * half : (k + 1) * half] = contract(p_buf[...], w_buf[k]).astype(dtype)

    scratch = [
        pltpu.VMEM((count, rows), BF),
        pltpu.VMEM((len(chunks), rows, half), BF),
        pltpu.SemaphoreType.DMA((1 + len(flat),)),
    ]
    flops = 2 * count * rows * half * len(chunks)
    return call(
        body, [where, p] + flat, [shape((count, half * len(chunks)), dtype)], scratch, flops
    )[0]


def collect(where, mine, theirs, chunks, acc, p, width, rows):
    count = mine.shape[0]
    half = width // 2
    flat = [piece for pieces in chunks for piece in pieces]
    extra = [v for v in (acc, p) if v is not None]

    def body(where_ref, mine_ref, theirs_ref, *refs):
        pieces, refs = refs[: len(flat)], refs[len(flat) :]
        more, (out, q_buf, w_buf, more_buf, sem) = refs[: len(extra)], refs[len(extra) :]
        core = where_ref[where.shape[0] - 1]
        copies = []
        at = 0
        for k, own in enumerate(chunks):
            for ref, side in ((mine_ref, core), (theirs_ref, 1 - core)):
                dst = pl.multiple_of(k * width + side * half, half)
                copies.append((ref.at[:, pl.ds(k * half, half)], q_buf.at[:, pl.ds(dst, half)]))
            row = 0
            for piece in own:
                height = piece.shape[0]
                copies.append(
                    (pieces[at], w_buf.at[pl.ds(row, height), pl.ds(k * width, width)])
                )
                row += height
                at += 1
        for i, ref in enumerate(more):
            copies.append((ref, more_buf.at[i]))
        copies = [pltpu.make_async_copy(a, b, sem.at[i]) for i, (a, b) in enumerate(copies)]
        for c in copies:
            c.start()
        for c in copies:
            c.wait()
        for at, size in tiles(rows):
            cols = slice(at, at + size)
            term = contract_last(q_buf[...], w_buf[cols, :])
            if acc is not None:
                term += more_buf[0, :, cols]
            if p is not None:
                term = 1.5 * more_buf[len(extra) - 1, :, cols] - 0.5 * term
            out[:, cols] = term.astype(out.dtype)

    depth = width * len(chunks)
    scratch = [
        pltpu.VMEM((count, depth), BF),
        pltpu.VMEM((rows, depth), BF),
        pltpu.VMEM((max(1, len(extra)), count, rows), F32),
        pltpu.SemaphoreType.DMA((2 * len(chunks) + len(flat) + len(extra),)),
    ]
    out = shape((count, rows), F32 if p is None else BF)
    ins = [where, mine, theirs] + flat + extra
    return call(body, ins, [out], scratch, 2 * count * rows * depth)[0]


def ring_form(n, tokens, weight):
    rows, width = weight.shape
    t = lax.axis_index("tensor")
    i = lax.axis_index("dp")
    steps = n // 2 - 1
    offsets = [0] + [o for s in range(1, steps + 1) for o in (-s, s)] + [steps + 1]
    ring = list(range(0, n, 2)) + list(range(n - 1, 0, -2))
    place = jnp.where(i % 2 == 0, i // 2, n - 1 - i // 2)
    spots = (place + jnp.array(offsets, jnp.int32) + n) % n
    source = jnp.where(spots < n // 2, 2 * spots, 2 * (n - 1 - spots) + 1)
    where = jnp.concatenate([source, (t % 2)[None]]).astype(jnp.int32)

    def up(v):
        return lax.ppermute(v, "dp", [(ring[i], ring[(i + 1) % n]) for i in range(n)])

    def down(v):
        return lax.ppermute(v, "dp", [(ring[(i + 1) % n], ring[i]) for i in range(n)])

    def over_x(v):
        return lax.ppermute(v, "tensor", [(t, t ^ 2) for t in range(4)])

    def over_core(v):
        return lax.ppermute(v, "tensor", [(t, t ^ 1) for t in range(4)])

    def gather(block):
        found = {0: [block]}
        u = d = block
        for s in range(1, steps + 1):
            u, d = up(u), down(d)
            found[-s], found[s] = [u], [d]
        half = block.shape[0] // 2
        found[steps + 1] = [up(u[:half]), down(d[half:])]
        return [found[o] for o in offsets]

    chunks = gather(weight)
    far = over_x(tokens)
    pair = jnp.where(t < 2, jnp.stack([tokens, far]), jnp.stack([far, tokens]))
    other = over_core(pair)
    quad = jnp.where(t % 2 == 0, jnp.stack([pair, other], 1), jnp.stack([other, pair], 1))
    toks = quad.reshape(4 * tokens.shape[0], tokens.shape[1])

    near = n - 3
    parts = list(enumerate(chunks))
    acc = project(where, toks, parts[:near], None, width, rows, False)[0]
    p, p_b = project(where, toks, parts[near:], acc, width, rows, True)

    groups = [chunks[0:2], chunks[2:4], chunks[4:6], chunks[6:8]]
    sums = []
    for bundle in (groups[:1], groups[1:]):
        joined = [c for g in bundle for c in g]
        give = over_core(spread(where, p_b, joined, width, rows, False))
        keep = spread(where, p_b, joined, width, rows, True)
        chip = keep + give.astype(F32)
        for k in range(len(bundle)):
            mine = chip[:, k * width : (k + 1) * width]
            sums.append((mine, over_x(mine.astype(BF))))
    out = None
    for g, (chip, far) in enumerate(sums):
        whole = (chip + far.astype(F32)).astype(BF)
        final = p if g == len(sums) - 1 else None
        out = collect(where, whole, over_core(whole), groups[g], out, final, width, rows)
    return out


def solution(mesh):
    n = mesh.shape["dp"]

    def on_device(tokens, weight):
        if mesh.shape["tensor"] == 4 and n == 8:
            return ring_form(n, tokens, weight)
        return gathered_form(tokens, weight)

    placed = (P(("dp", "tensor"), None), P("tensor", "dp"))
    return jax.shard_map(
        on_device, mesh=mesh, in_specs=placed, out_specs=P("dp", "tensor"), check_vma=False
    )
```

time: 855 us -> 177 us (0.21)
  blocking collectives: 645 us -> 0 us
  waiting for transfers between devices: 163 us -> 99.6 us
  Pallas kernels: 0 us -> 42.4 us
  matrix products: 33 us -> 0 us
  starting transfers between devices: 0.08 us -> 16.7 us
  other arithmetic: 0 us -> 14.2 us
  between operations: 13.1 us -> 0.24 us
    psum x1 -> x0, blocking collectives: 645 us -> none  [on_device(): gram_cols = lax.psum(term, 'dp').astype(jnp.bfloat16)]
    all_gather x3 -> x0, waiting for transfers between devices: 161 us -> none  [the longest x1 123 us: on_device(): full_rows = lax.all_gather(ortho, 'dp', axis=1, tiled=True)]
    ppermute x0 -> x20, waiting for transfers between devices: none -> 99.6 us  [the longest x4 59.1 us: down(): lax.ppermute(v, 'dp', [(ring[(i + 1) % n], ring[i]) for i in range(n)])]
    pallas_call x0 -> x10, Pallas kernels: none -> 42.4 us  [call(): pl.pallas_call(body, out_shape=outs, in_specs=[SMEM] + [ANY] * (len(ins)...]
    dot_general x3 -> x0, matrix products: 33 us -> none  [the longest x2 22.9 us: contract_last(): lax.dot_general(left, right, (((1,), (1,)), ((), ())), preferred_element_...]
    ppermute x0 -> x20, starting transfers between devices: none -> 16.7 us  [the longest x4 7.25 us: down(): lax.ppermute(v, 'dp', [(ring[(i + 1) % n], ring[i]) for i in range(n)])]
    select_n x0 -> x4, other arithmetic: none -> 10.8 us  [the longest x2 6.22 us: ring_form(): pair = jnp.where(t < 2, jnp.stack([tokens, far]), jnp.stack([far, tokens]))]
  transfers between devices with their start and end apart: 3 -> 20, of which waited for: 2 -> 7; matrix products, arithmetic and copies ran while one was open for 3% -> 8% of each run, Pallas kernels for 0% -> 15%
where the time goes in v1:
time: 177 us; the launch traced here: 176 us
  waiting for transfers between devices  99.6 us (56%)
  Pallas kernels  42.4 us (24%)
  starting transfers between devices  16.7 us (9%)
  other arithmetic  14.2 us (8%)
  local copies, waits for them, and re-layouts  3 us (2%)
    ppermute x4, waiting for transfers between devices, down(): lax.ppermute(v, 'dp', [(ring[(i + 1) % n], ring[i]) for i in range(n)])  59.1 us
    pallas_call x10, Pallas kernels, call(): pl.pallas_call(body, out_shape=outs, in_specs=[SMEM] + [ANY] * (len(ins)...  42.4 us
    ppermute x5, waiting for transfers between devices, over_x(): return lax.ppermute(v, 'tensor', [(t, t ^ 2) for t in range(4)])  40.5 us
    ppermute x4, starting transfers between devices, down(): lax.ppermute(v, 'dp', [(ring[(i + 1) % n], ring[i]) for i in range(n)])  7.25 us
    select_n x2, other arithmetic, ring_form(): pair = jnp.where(t < 2, jnp.stack([tokens, far]), jnp.stack([far, tokens]))  6.22 us
    ppermute x5, starting transfers between devices, over_x(): return lax.ppermute(v, 'tensor', [(t, t ^ 2) for t in range(4)])  6.12 us
    select_n x1, other arithmetic, ring_form(): jnp.where(t % 2 == 0, jnp.stack([pair, other], 1), jnp.stack([other, pair...  4.56 us
  transfers between devices with their start and end apart: 20, of which 7 were waited for; matrix products, arithmetic and copies ran while one was open for 8% of the time, Pallas kernels for 15%

profile of v1, /device:TPU:0, one launch (start us, length us, event | category | flops | bytes accessed | tf_op | source)
XLA Modules:
  0.0 176.2 jit_solution(8889423664453907039)
XLA Ops:
  0.0 3.0 %collective-permute-start.5 = (bf16[1024,512]{1,0:T(8,128)(2,1)}, bf16[1024,512]{1,0:T(8,128)(2,1)S(1)}, u32[]{:S(2)}, u32[]{:S(2)}) collective-permute-start(bf16[1024,512]{1,0:T(8,128)(2,1)} %refs_0_.7), channel_id=1, source_target_pairs={{8,0},{16,8},{24,16},{28,24},{20,28},{12,20},{4,12},{0,4},{9,1},{1... | collective-permute-start | bytes 3145736 | tf_op jit(solution)/shard_map/ppermute | solution.py:213
  3.0 1.9 %collective-permute-start = (bf16[128,4096]{1,0:T(8,128)(2,1)}, bf16[128,4096]{1,0:T(8,128)(2,1)S(1)}, u32[]{:S(2)}, u32[]{:S(2)}) collective-permute-start(bf16[128,4096]{1,0:T(8,128)(2,1)} %param.3), channel_id=1, source_target_pairs={{0,2},{1,3},{2,0},{3,1},{4,6},{5,7},{6,4},{7,5},{8,10},{9,11},{10,... | collective-permute-start | bytes 3145736 | tf_op jit(solution)/shard_map/ppermute | solution.py:216
  5.0 21.4 %collective-permute-done.5.refs_2_.refs_0_ = bf16[1024,512]{1,0:T(8,128)(2,1)S(1)} collective-permute-done((bf16[1024,512]{1,0:T(8,128)(2,1)}, bf16[1024,512]{1,0:T(8,128)(2,1)S(1)}, u32[]{:S(2)}, u32[]{:S(2)}) %collective-permute-start.5) | collective-permute-done | bytes 1048608 | tf_op jit(solution)/shard_map/ppermute | solution.py:213
  26.4 1.7 collective-permute-start.6
  28.4 3.6 %maximum_select_fusion.2 = bf16[2,128,4096]{2,1,0:T(8,128)(2,1)} fusion(bf16[1,128,4096]{2,1,0:T(8,128)(2,1)S(1)} %bitcast.11, bf16[1,128,4096]{2,1,0:T(8,128)(2,1)} %bitcast.9, pred[]{:T(512)S(6)} %lt.28), kind=kLoop, calls=%fused_computation.3 | loop fusion | flops 3145728 | bytes 4194305 | tf_op jit(solution)/shard_map/jit(_where)/select_n | solution.py:233
  32.1 18.8 %collective-permute-done.6.refs_4_.refs_2_.refs_0_ = bf16[1024,512]{1,0:T(8,128)(2,1)} collective-permute-done((bf16[1024,512]{1,0:T(8,128)(2,1)S(1)}, bf16[1024,512]{1,0:T(8,128)(2,1)}, u32[]{:S(2)}, u32[]{:S(2)}) %collective-permute-start.6) | collective-permute-done | bytes 1048608 | tf_op jit(solution)/shard_map/ppermute | solution.py:213
  53.0 2.6 %maximum_select_fusion.1 = bf16[2,1,128,4096]{3,2,1,0:T(8,128)(2,1)S(1)} fusion(bf16[1,1,128,4096]{3,2,1,0:T(8,128)(2,1)} %bitcast.12, bf16[1,1,128,4096]{3,2,1,0:T(8,128)(2,1)} %bitcast.10, pred[]{:T(512)S(6)} %lt.28), kind=kLoop, calls=%fused_computation.2 | loop fusion | flops 3145728 | bytes 4194305 | tf_op jit(solution)/shard_map/jit(_where)/select_n | solution.py:233
  55.6 18.9 %collective-permute-done.7.refs_1_.refs_4_.refs_0_ = bf16[1024,512]{1,0:T(8,128)(2,1)S(1)} collective-permute-done((bf16[1024,512]{1,0:T(8,128)(2,1)}, bf16[1024,512]{1,0:T(8,128)(2,1)S(1)}, u32[]{:S(2)}, u32[]{:S(2)}) %collective-permute-start.7) | collective-permute-done | bytes 1048608 | tf_op jit(solution)/shard_map/ppermute | solution.py:213
  76.7 4.6 %maximum_select_fusion = bf16[2,2,128,4096]{3,2,1,0:T(8,128)(2,1)} fusion(bf16[2,1,128,4096]{3,2,1,0:T(8,128)(2,1)} %bitcast.5, bf16[2,1,128,4096]{3,2,1,0:T(8,128)(2,1)S(1)} %maximum_select_fusion.1, pred[]{:T(512)S(6)} %eq.13), kind=kLoop, calls=%fused_computation | loop fusion | flops 6291456 | bytes 8388609 | tf_op jit(solution)/shard_map/jit(_where)/select_n | solution.py:235
  81.3 7.3 %shard_map.37.refs_4_ = f32[512,1024]{1,0:T(8,128)} custom-call(s32[9]{0:T(128)S(1)} %pad_add_fusion.where_ref, bf16[512,4096]{1,0:T(8,128)(2,1)} %bitcast.7, bf16[1024,512]{1,0:T(8,128)(2,1)S(1)} %copy-done.4, bf16[1024,512]{1,0:T(8,128)(2,1)S(1)} %collective-permute-done.2.refs_1_, bf16[1024,512]{1,0:T(8,128)(2,1)S(1)} %copy-done.6, ...), custom_call_target="tpu_custom_call" | custom-call | flops 2684354560 | bytes 11534372 | tf_op jit(solution)/shard_map/pallas_call | solution.py:38
  88.7 6.0 %shard_map.38 = (f32[512,1024]{1,0:T(8,128)}, bf16[512,1024]{1,0:T(8,128)(2,1)S(1)}) custom-call(s32[9]{0:T(128)S(1)} %pad_add_fusion.where_ref, bf16[512,4096]{1,0:T(8,128)(2,1)} %bitcast.8, bf16[1024,512]{1,0:T(8,128)(2,1)S(1)} %collective-permute-done.4.refs_0_.refs_3_.refs_1_, bf16[1024,512]{1,0:T(8,128)(2,1)S(1)} %collective-permute-done.7.refs_1_.refs_4_.refs_0_, ...), custom_call_target="tpu_custom_call" | custom-call | flops 1610612736 | bytes 12582948 | tf_op jit(solution)/shard_map/pallas_call | solution.py:38
  94.6 5.2 %shard_map.40 = bf16[512,1536]{1,0:T(8,128)(2,1)} custom-call(s32[9]{0:T(128)S(1)} %pad_add_fusion.where_ref, bf16[512,1024]{1,0:T(8,128)(2,1)S(1)} %get-tuple-element.7.p_ref, bf16[1024,512]{1,0:T(8,128)(2,1)S(1)} %copy-done.6, bf16[1024,512]{1,0:T(8,128)(2,1)} %collective-permute-done.3.refs_3_.refs_1_, ...), custom_call_target="tpu_custom_call" | custom-call | flops 1610612736 | bytes 8912932 | tf_op jit(solution)/shard_map/pallas_call | solution.py:38
  99.9 1.4 shard_map.42
  101.9 1.4 shard_map.41
  103.3 5.7 %shard_map.39 = f32[512,1536]{1,0:T(8,128)} custom-call(s32[9]{0:T(128)S(1)} %pad_add_fusion.where_ref, bf16[512,1024]{1,0:T(8,128)(2,1)S(1)} %get-tuple-element.7.p_ref, bf16[1024,512]{1,0:T(8,128)(2,1)S(1)} %copy-done.6, bf16[1024,512]{1,0:T(8,128)(2,1)} %collective-permute-done.3.refs_3_.refs_1_, ...), custom_call_target="tpu_custom_call" | custom-call | flops 1610612736 | bytes 10485796 | tf_op jit(solution)/shard_map/pallas_call | solution.py:38
  110.4 2.4 %convert_add_fusion = f32[512,1536]{1,0:T(8,128)S(1)} fusion(f32[512,1536]{1,0:T(8,128)} %shard_map.39, bf16[512,1536]{1,0:T(8,128)(2,1)S(1)} %collective-permute-done.10), kind=kLoop, calls=%fused_computation.1 | loop fusion | flops 1572864 | bytes 7864320 | tf_op jit(solution)/shard_map/add | solution.py:249
  116.0 8.0 %collective-permute-done.18 = bf16[512,512]{1,0:T(8,128)(2,1)S(1)} collective-permute-done((bf16[512,512]{1,0:T(8,128)(2,1)S(1)}, bf16[512,512]{1,0:T(8,128)(2,1)S(1)}, u32[]{:S(2)}, u32[]{:S(2)}) %collective-permute-start.18) | collective-permute-done | bytes 524320 | tf_op jit(solution)/shard_map/ppermute | solution.py:216
  124.3 10.9 %collective-permute-done.15 = bf16[512,512]{1,0:T(8,128)(2,1)S(1)} collective-permute-done((bf16[512,512]{1,0:T(8,128)(2,1)S(1)}, bf16[512,512]{1,0:T(8,128)(2,1)S(1)}, u32[]{:S(2)}, u32[]{:S(2)}) %collective-permute-start.15) | collective-permute-done | bytes 524320 | tf_op jit(solution)/shard_map/ppermute | solution.py:216
  135.3 11.2 %collective-permute-done.13 = bf16[512,512]{1,0:T(8,128)(2,1)S(1)} collective-permute-done((bf16[512,512]{1,0:T(8,128)(2,1)S(1)}, bf16[512,512]{1,0:T(8,128)(2,1)S(1)}, u32[]{:S(2)}, u32[]{:S(2)}) %collective-permute-start.13) | collective-permute-done | bytes 524320 | tf_op jit(solution)/shard_map/ppermute | solution.py:216
  146.5 10.3 %collective-permute-done.11 = bf16[512,512]{1,0:T(8,128)(2,1)S(1)} collective-permute-done((bf16[512,512]{1,0:T(8,128)(2,1)S(1)}, bf16[512,512]{1,0:T(8,128)(2,1)S(1)}, u32[]{:S(2)}, u32[]{:S(2)}) %collective-permute-start.11) | collective-permute-done | bytes 524320 | tf_op jit(solution)/shard_map/ppermute | solution.py:216
  158.0 2.3 %shard_map.43.refs_2_ = f32[512,1024]{1,0:T(8,128)S(1)} custom-call(s32[9]{0:T(128)S(1)} %pad_add_fusion.where_ref, bf16[512,512]{1,0:T(8,128)(2,1)S(1)} %add_convert_fusion.mine_ref, bf16[512,512]{1,0:T(8,128)(2,1)S(1)} %collective-permute-done.19.theirs_ref, bf16[1024,512]{1,0:T(8,128)(2,1)S(1)} %copy-done.4, ...), custom_call_target="tpu_custom_call" | custom-call | flops 1073741824 | bytes 5242916 | tf_op jit(solution)/shard_map/pallas_call | solution.py:38
  161.7 4.1 %shard_map.44.refs_2_ = f32[512,1024]{1,0:T(8,128)S(1)} custom-call(s32[9]{0:T(128)S(1)} %pad_add_fusion.where_ref, bf16[512,512]{1,0:T(8,128)(2,1)S(1)} %get-tuple-element.9.mine_ref, bf16[512,512]{1,0:T(8,128)(2,1)S(1)} %collective-permute-done.16.theirs_ref, bf16[1024,512]{1,0:T(8,128)(2,1)S(1)} %copy-done.6, ...), custom_call_target="tpu_custom_call" | custom-call | flops 1073741824 | bytes 7340068 | tf_op jit(solution)/shard_map/pallas_call | solution.py:38
  167.2 3.9 %shard_map.45.refs_3_ = f32[512,1024]{1,0:T(8,128)S(1)} custom-call(s32[9]{0:T(128)S(1)} %pad_add_fusion.where_ref, bf16[512,512]{1,0:T(8,128)(2,1)S(1)} %get-tuple-element.11.mine_ref, bf16[512,512]{1,0:T(8,128)(2,1)S(1)} %collective-permute-done.14.theirs_ref, bf16[1024,512]{1,0:T(8,128)(2,1)} %collective-permute-done.6.refs_4_.refs_2_.refs_0_, ...), custom_call_target="tpu_custom_call" | custom-call | flops 1073741824 | bytes 7340068 | tf_op jit(solution)/shard_map/pallas_call | solution.py:38
  171.2 5.1 %shard_map.46 = bf16[512,1024]{1,0:T(8,128)(2,1)} custom-call(s32[9]{0:T(128)S(1)} %pad_add_fusion.where_ref, bf16[512,512]{1,0:T(8,128)(2,1)S(1)} %get-tuple-element.10.mine_ref, bf16[512,512]{1,0:T(8,128)(2,1)S(1)} %collective-permute-done.12.theirs_ref, bf16[1024,512]{1,0:T(8,128)(2,1)S(1)} %copy-done.1, ...), custom_call_target="tpu_custom_call" | custom-call | flops 1073741824 | bytes 8388644 | tf_op jit(solution)/shard_map/pallas_call | solution.py:38
  (60 shorter events, 14.2 us)
Async XLA Ops:
  0.0 26.4 %collective-permute-start.5 = (bf16[1024,512]{1,0:T(8,128)(2,1)}, bf16[1024,512]{1,0:T(8,128)(2,1)S(1)}, u32[]{:S(2)}, u32[]{:S(2)}) collective-permute-start(bf16[1024,512]{1,0:T(8,128)(2,1)} %refs_0_.7), channel_id=1, source_target_pairs={{8,0},{16,8},{24,16},{28,24},{20,28},{12,20},{4,12},{0,4},{9,1},{1... | collective-permute-start | bytes 3145736 | tf_op jit(solution)/shard_map/ppermute | solution.py:213
  3.0 25.1 %collective-permute-start.2 = (bf16[1024,512]{1,0:T(8,128)(2,1)}, bf16[1024,512]{1,0:T(8,128)(2,1)S(1)}, u32[]{:S(2)}, u32[]{:S(2)}) collective-permute-start(bf16[1024,512]{1,0:T(8,128)(2,1)} %refs_0_.7), channel_id=1, source_target_pairs={{0,8},{8,16},{16,24},{24,28},{28,20},{20,12},{12,4},{4,0},{1,9},{9... | collective-permute-start | bytes 3145736 | tf_op jit(solution)/shard_map/ppermute | solution.py:210
  3.0 25.4 %collective-permute-start = (bf16[128,4096]{1,0:T(8,128)(2,1)}, bf16[128,4096]{1,0:T(8,128)(2,1)S(1)}, u32[]{:S(2)}, u32[]{:S(2)}) collective-permute-start(bf16[128,4096]{1,0:T(8,128)(2,1)} %param.3), channel_id=1, source_target_pairs={{0,2},{1,3},{2,0},{3,1},{4,6},{5,7},{6,4},{7,5},{8,10},{9,11},{10,... | collective-permute-start | bytes 3145736 | tf_op jit(solution)/shard_map/ppermute | solution.py:216
  26.4 5.6 %copy-start.5 = (bf16[1024,512]{1,0:T(8,128)(2,1)}, bf16[1024,512]{1,0:T(8,128)(2,1)S(1)}, u32[]{:S(2)}) copy-start(bf16[1024,512]{1,0:T(8,128)(2,1)S(1)} %collective-permute-done.5.refs_2_.refs_0_) | copy-start | bytes 3145732
  26.4 24.5 %collective-permute-start.6 = (bf16[1024,512]{1,0:T(8,128)(2,1)S(1)}, bf16[1024,512]{1,0:T(8,128)(2,1)}, u32[]{:S(2)}, u32[]{:S(2)}) collective-permute-start(bf16[1024,512]{1,0:T(8,128)(2,1)S(1)} %collective-permute-done.5.refs_2_.refs_0_), channel_id=1, source_target_pairs={{8,0},{16,8},{24,16},{28,24},{20,28},{12,20},{4,12},{0,4},{9,1},{1... | collective-permute-start | bytes 3145736 | tf_op jit(solution)/shard_map/ppermute | solution.py:213
  28.1 24.1 %collective-permute-start.3 = (bf16[1024,512]{1,0:T(8,128)(2,1)S(1)}, bf16[1024,512]{1,0:T(8,128)(2,1)}, u32[]{:S(2)}, u32[]{:S(2)}) collective-permute-start(bf16[1024,512]{1,0:T(8,128)(2,1)S(1)} %collective-permute-done.2.refs_1_), channel_id=1, source_target_pairs={{0,8},{8,16},{16,24},{24,28},{28,20},{20,12},{12,4},{4,0},{1,9},{9... | collective-permute-start | bytes 3145736 | tf_op jit(solution)/shard_map/ppermute | solution.py:210
  28.4 24.4 %copy-start.10 = (s32[8]{0:T(128)S(1)}, s32[8]{0:T(128)}, u32[]{:S(2)}) copy-start(s32[8]{0:T(128)} %constant.65.clone) | copy-start | bytes 100
  32.0 44.7 %collective-permute-start.1 = (bf16[2,128,4096]{2,1,0:T(8,128)(2,1)}, bf16[2,128,4096]{2,1,0:T(8,128)(2,1)}, u32[]{:S(2)}, u32[]{:S(2)}) collective-permute-start(bf16[2,128,4096]{2,1,0:T(8,128)(2,1)} %maximum_select_fusion.2), channel_id=1, source_target_pairs={{0,1},{1,0},{2,3},{3,2},{4,5},{5,4},{6,7},{7,6},{8,9},{9,8},{10,11... | collective-permute-start | bytes 6291464 | tf_op jit(solution)/shard_map/ppermute | solution.py:219
  50.8 23.6 %collective-permute-start.7 = (bf16[1024,512]{1,0:T(8,128)(2,1)}, bf16[1024,512]{1,0:T(8,128)(2,1)S(1)}, u32[]{:S(2)}, u32[]{:S(2)}) collective-permute-start(bf16[1024,512]{1,0:T(8,128)(2,1)} %collective-permute-done.6.refs_4_.refs_2_.refs_0_), channel_id=1, source_target_pairs={{8,0},{16,8},{24,16},{28,24},{20,28},{12,20},{4,12},{0,4},{9,1},{1... | collective-permute-start | bytes 3145736 | tf_op jit(solution)/shard_map/ppermute | solution.py:213
  52.2 23.5 %collective-permute-start.4 = (bf16[1024,512]{1,0:T(8,128)(2,1)}, bf16[1024,512]{1,0:T(8,128)(2,1)S(1)}, u32[]{:S(2)}, u32[]{:S(2)}) collective-permute-start(bf16[1024,512]{1,0:T(8,128)(2,1)} %collective-permute-done.3.refs_3_.refs_1_), channel_id=1, source_target_pairs={{0,8},{8,16},{16,24},{24,28},{28,20},{20,12},{12,4},{4,0},{1,9},{9... | collective-permute-start | bytes 3145736 | tf_op jit(solution)/shard_map/ppermute | solution.py:210
  74.5 14.2 %copy-start = (bf16[1024,512]{1,0:T(8,128)(2,1)}, bf16[1024,512]{1,0:T(8,128)(2,1)S(1)}, u32[]{:S(2)}) copy-start(bf16[1024,512]{1,0:T(8,128)(2,1)S(1)} %collective-permute-done.7.refs_1_.refs_4_.refs_0_) | copy-start | bytes 3145732
  74.5 14.1 %collective-permute-start.9 = (bf16[512,512]{1,0:T(8,128)(2,1)S(1)}, bf16[512,512]{1,0:T(8,128)(2,1)S(1)}, u32[]{:S(2)}, u32[]{:S(2)}) collective-permute-start(bf16[512,512]{1,0:T(8,128)(2,1)S(1)} %slice.21), channel_id=1, source_target_pairs={{8,0},{16,8},{24,16},{28,24},{20,28},{12,20},{4,12},{0,4},{9,1},{1... | collective-permute-start | bytes 1572872 | tf_op jit(solution)/shard_map/ppermute | solution.py:213
  75.8 12.9 %copy-start.2 = (bf16[1024,512]{1,0:T(8,128)(2,1)}, bf16[1024,512]{1,0:T(8,128)(2,1)S(1)}, u32[]{:S(2)}) copy-start(bf16[1024,512]{1,0:T(8,128)(2,1)S(1)} %collective-permute-done.4.refs_0_.refs_3_.refs_1_) | copy-start | bytes 3145732
  75.8 12.8 %collective-permute-start.8 = (bf16[512,512]{1,0:T(8,128)(2,1)S(1)}, bf16[512,512]{1,0:T(8,128)(2,1)S(1)}, u32[]{:S(2)}, u32[]{:S(2)}) collective-permute-start(bf16[512,512]{1,0:T(8,128)(2,1)S(1)} %slice.20), channel_id=1, source_target_pairs={{0,8},{8,16},{16,24},{24,28},{28,20},{20,12},{12,4},{4,0},{1,9},{9... | collective-permute-start | bytes 1572872 | tf_op jit(solution)/shard_map/ppermute | solution.py:210
  99.8 10.6 %collective-permute-start.10 = (bf16[512,1536]{1,0:T(8,128)(2,1)}, bf16[512,1536]{1,0:T(8,128)(2,1)S(1)}, u32[]{:S(2)}, u32[]{:S(2)}) collective-permute-start(bf16[512,1536]{1,0:T(8,128)(2,1)} %shard_map.40), channel_id=1, source_target_pairs={{0,1},{1,0},{2,3},{3,2},{4,5},{5,4},{6,7},{7,6},{8,9},{9,8},{10,11... | collective-permute-start | bytes 4718600 | tf_op jit(solution)/shard_map/ppermute | solution.py:219
  101.3 7.7 %collective-permute-start.17 = (bf16[512,512]{1,0:T(8,128)(2,1)S(1)}, bf16[512,512]{1,0:T(8,128)(2,1)S(1)}, u32[]{:S(2)}, u32[]{:S(2)}) collective-permute-start(bf16[512,512]{1,0:T(8,128)(2,1)S(1)} %shard_map.42), channel_id=1, source_target_pairs={{0,1},{1,0},{2,3},{3,2},{4,5},{5,4},{6,7},{7,6},{8,9},{9,8},{10,11... | collective-permute-start | bytes 1572872 | tf_op jit(solution)/shard_map/ppermute | solution.py:219
  109.2 14.9 %collective-permute-start.18 = (bf16[512,512]{1,0:T(8,128)(2,1)S(1)}, bf16[512,512]{1,0:T(8,128)(2,1)S(1)}, u32[]{:S(2)}, u32[]{:S(2)}) collective-permute-start(bf16[512,512]{1,0:T(8,128)(2,1)S(1)} %fusion), channel_id=1, source_target_pairs={{0,2},{1,3},{2,0},{3,1},{4,6},{5,7},{6,4},{7,5},{8,10},{9,11},{10,... | collective-permute-start | bytes 1572872 | tf_op jit(solution)/shard_map/ppermute | solution.py:216
  113.0 22.3 %collective-permute-start.15 = (bf16[512,512]{1,0:T(8,128)(2,1)S(1)}, bf16[512,512]{1,0:T(8,128)(2,1)S(1)}, u32[]{:S(2)}, u32[]{:S(2)}) collective-permute-start(bf16[512,512]{1,0:T(8,128)(2,1)S(1)} %get-tuple-element.12), channel_id=1, source_target_pairs={{0,2},{1,3},{2,0},{3,1},{4,6},{5,7},{6,4},{7,5},{8,10},{9,11},{10,... | collective-permute-start | bytes 1572872 | tf_op jit(solution)/shard_map/ppermute | solution.py:216
  114.0 32.5 %collective-permute-start.13 = (bf16[512,512]{1,0:T(8,128)(2,1)S(1)}, bf16[512,512]{1,0:T(8,128)(2,1)S(1)}, u32[]{:S(2)}, u32[]{:S(2)}) collective-permute-start(bf16[512,512]{1,0:T(8,128)(2,1)S(1)} %get-tuple-element.13), channel_id=1, source_target_pairs={{0,2},{1,3},{2,0},{3,1},{4,6},{5,7},{6,4},{7,5},{8,10},{9,11},{10,... | collective-permute-start | bytes 1572872 | tf_op jit(solution)/shard_map/ppermute | solution.py:216
  115.1 41.7 %collective-permute-start.11 = (bf16[512,512]{1,0:T(8,128)(2,1)S(1)}, bf16[512,512]{1,0:T(8,128)(2,1)S(1)}, u32[]{:S(2)}, u32[]{:S(2)}) collective-permute-start(bf16[512,512]{1,0:T(8,128)(2,1)S(1)} %get-tuple-element.14), channel_id=1, source_target_pairs={{0,2},{1,3},{2,0},{3,1},{4,6},{5,7},{6,4},{7,5},{8,10},{9,11},{10,... | collective-permute-start | bytes 1572872 | tf_op jit(solution)/shard_map/ppermute | solution.py:216
  124.3 33.8 %collective-permute-start.19 = (bf16[512,512]{1,0:T(8,128)(2,1)S(1)}, bf16[512,512]{1,0:T(8,128)(2,1)S(1)}, u32[]{:S(2)}, u32[]{:S(2)}) collective-permute-start(bf16[512,512]{1,0:T(8,128)(2,1)S(1)} %add_convert_fusion.mine_ref), channel_id=1, source_target_pairs={{0,1},{1,0},{2,3},{3,2},{4,5},{5,4},{6,7},{7,6},{8,9},{9,8},{10,11... | collective-permute-start | bytes 1572872 | tf_op jit(solution)/shard_map/ppermute | solution.py:219
  157.4 4.4 %collective-permute-start.16 = (bf16[512,512]{1,0:T(8,128)(2,1)S(1)}, bf16[512,512]{1,0:T(8,128)(2,1)S(1)}, u32[]{:S(2)}, u32[]{:S(2)}) collective-permute-start(bf16[512,512]{1,0:T(8,128)(2,1)S(1)} %get-tuple-element.9.mine_ref), channel_id=1, source_target_pairs={{0,1},{1,0},{2,3},{3,2},{4,5},{5,4},{6,7},{7,6},{8,9},{9,8},{10,11... | collective-permute-start | bytes 1572872 | tf_op jit(solution)/shard_map/ppermute | solution.py:219
  157.4 9.7 %collective-permute-start.14 = (bf16[512,512]{1,0:T(8,128)(2,1)S(1)}, bf16[512,512]{1,0:T(8,128)(2,1)S(1)}, u32[]{:S(2)}, u32[]{:S(2)}) collective-permute-start(bf16[512,512]{1,0:T(8,128)(2,1)S(1)} %get-tuple-element.11.mine_ref), channel_id=1, source_target_pairs={{0,1},{1,0},{2,3},{3,2},{4,5},{5,4},{6,7},{7,6},{8,9},{9,8},{10,11... | collective-permute-start | bytes 1572872 | tf_op jit(solution)/shard_map/ppermute | solution.py:219
  157.9 13.2 %collective-permute-start.12 = (bf16[512,512]{1,0:T(8,128)(2,1)S(1)}, bf16[512,512]{1,0:T(8,128)(2,1)S(1)}, u32[]{:S(2)}, u32[]{:S(2)}) collective-permute-start(bf16[512,512]{1,0:T(8,128)(2,1)S(1)} %get-tuple-element.10.mine_ref), channel_id=1, source_target_pairs={{0,1},{1,0},{2,3},{3,2},{4,5},{5,4},{6,7},{7,6},{8,9},{9,8},{10,11... | collective-permute-start | bytes 1572872 | tf_op jit(solution)/shard_map/ppermute | solution.py:219
  (7 other events, 24.9 us)

commit v2 on v0

v2 whole, which is shorter than its diff:
```python
import jax
import jax.numpy as jnp
from jax import lax
from jax.experimental import pallas as pl
from jax.experimental.pallas import tpu as pltpu
from jax.sharding import PartitionSpec as P

BF = jnp.bfloat16
F32 = jnp.float32
ANY = pl.BlockSpec(memory_space=pl.ANY)
HBM = pl.BlockSpec(memory_space=pltpu.HBM)
SMEM = pl.BlockSpec(memory_space=pltpu.SMEM)
VMEM = pl.BlockSpec(memory_space=pltpu.VMEM)
LATE = 256


def contract_last(left, right):
    return lax.dot_general(left, right, (((1,), (1,)), ((), ())), preferred_element_type=F32)


def contract(left, right):
    return lax.dot_general(left, right, (((1,), (0,)), ((), ())), preferred_element_type=F32)


def gathered_form(tokens, weight):
    rows = lax.all_gather(weight, "dp", axis=1, tiled=True)
    toks = lax.all_gather(tokens, "tensor", axis=0, tiled=True)
    first = contract_last(toks, rows)
    part = contract(first.astype(BF), rows).astype(BF)
    second = lax.psum(part, "tensor")
    return (1.5 * first - 0.5 * contract_last(second, rows)).astype(BF)


def tiles(extent, step=256):
    return [slice(at, min(at + step, extent)) for at in range(0, extent, step)]


def call(body, where, ins, outs, flops, after=(), leave=False, scratch=()):
    flat, tree = jax.tree.flatten(ins)
    after = list(after)
    n_in, n_out = len(flat), len(outs)

    scalars = [] if where is None else [where]

    def kernel(*refs):
        where_ref, refs = (refs[0], refs[1:]) if scalars else (None, refs)
        given = jax.tree.unflatten(tree, refs[:n_in])
        rest = refs[n_in + len(after) :]
        body(where_ref, given, rest[:n_out], *rest[n_out:])

    nbytes = sum(v.size * v.dtype.itemsize for v in flat)
    place = pltpu.HBM if leave else pltpu.VMEM
    flat = [pltpu.with_memory_space_constraint(v, place) for v in flat]
    return pl.pallas_call(
        kernel,
        out_shape=[pltpu.VMEM(*o) if isinstance(o, tuple) else o for o in outs],
        in_specs=[SMEM] * len(scalars) + [HBM if leave else VMEM] * n_in + [ANY] * len(after),
        out_specs=[VMEM] * n_out,
        scratch_shapes=[pltpu.SemaphoreType.DMA((n_out,))] if leave else list(scratch),
        compiler_params=pltpu.CompilerParams(vmem_limit_bytes=16 << 20),
        cost_estimate=pl.CostEstimate(flops=flops, bytes_accessed=nbytes, transcendentals=0),
    )(*scalars, *flat, *after)


def bounds(pieces):
    ends = [0]
    for piece in pieces:
        ends.append(ends[-1] + piece.shape[0])
    return ends


def cuts(chunks):
    edges = sorted({e for pieces in chunks for e in bounds(pieces)})
    return [
        slice(a + t.start, a + t.stop) for a, b in zip(edges, edges[1:]) for t in tiles(b - a)
    ]


def at_rows(pieces, rows, cols=slice(None)):
    for ref, start in zip(pieces, bounds(pieces)):
        if start <= rows.start and rows.stop <= start + ref.shape[0]:
            return ref[rows.start - start : rows.stop - start, cols]


def add_dots(pairs, acc=None):
    for left, right in pairs:
        term = contract_last(left, right)
        acc = term if acc is None else acc + term
    return acc


def ring_form(n, tokens, weight):
    rows, width = weight.shape
    own = tokens.shape[0]
    count = 4 * own
    half = width // 2
    early = rows - LATE
    middle = early // 2
    steps = n // 2 - 1
    wide = 4 * LATE
    square = (count, width)
    t = lax.axis_index("tensor")
    i = lax.axis_index("dp")
    offsets = [0] + [o for s in range(1, steps + 1) for o in (-s, s)] + [steps + 1]
    ring = list(range(0, n, 2)) + list(range(n - 1, 0, -2))
    place = jnp.where(i % 2 == 0, i // 2, n - 1 - i // 2)
    spots = (place + jnp.array(offsets, jnp.int32) + n) % n
    source = jnp.where(spots < n // 2, 2 * spots, 2 * (n - 1 - spots) + 1)
    core = t % 2
    x = t // 2
    slots = jnp.stack([t, 2 * (1 - x) + core, 2 * x + 1 - core, 2 * (1 - x) + 1 - core])
    where = jnp.concatenate([source, core[None], slots]).astype(jnp.int32)

    def up(v):
        return lax.ppermute(v, "dp", [(ring[i], ring[(i + 1) % n]) for i in range(n)])

    def down(v):
        return lax.ppermute(v, "dp", [(ring[(i + 1) % n], ring[i]) for i in range(n)])

    def over_x(v):
        return lax.ppermute(v, "tensor", [(t, t ^ 2) for t in range(4)])

    def over_core(v):
        return lax.ppermute(v, "tensor", [(t, t ^ 1) for t in range(4)])

    def copy_from(row):
        def body(where_ref, given, outs, sem):
            src = given[0].at[pl.ds(row, outs[0].shape[0]), :]
            copy = pltpu.make_async_copy(src, outs[0], sem.at[0])
            copy.start()
            copy.wait()

        return body

    def relay(where_ref, given, outs):
        for ref, out in zip(given, outs):
            out[...] = ref[...]

    def relayed(arrays, after):
        return call(relay, None, arrays, [(a.shape, a.dtype) for a in arrays], 0, after)

    def split(where_ref, given, outs):
        cut = outs[0].shape[0]
        outs[0][...] = given[0][:cut, :]
        outs[1][...] = given[1][cut:, :]

    def ends(u, d, after):
        h = u.shape[0] // 2
        return call(split, None, [u, d], [((h, width), BF), ((u.shape[0] - h, width), BF)], 0, after)

    def columns(k):
        return slice(k * width, (k + 1) * width)

    def halves(where_ref, own_half):
        side = where_ref[n]
        return pl.ds(pl.multiple_of((side if own_half else 1 - side) * half, half), half)

    def p_terms(tok, ks, chunks, acc_ref, put):
        for cut in cuts(chunks):
            pairs = [(tok[:, columns(k)], at_rows(c, cut)) for k, c in zip(ks, chunks)]
            put(cut, add_dots(pairs, None if acc_ref is None else acc_ref[:, cut]))

    def project(ks, acc, after=()):
        def body(where_ref, given, outs):
            tok, chunks, acc_ref = given

            def put(cols, value):
                outs[0][:, cols] = value

            p_terms(tok, ks, chunks, acc_ref, put)

        outs = [((count, early), F32)]
        flops = 2 * count * early * width * len(ks)
        return call(body, where, (toks, [w[k] for k in ks], acc), outs, flops, after)[0]

    far = over_x(tokens)
    first = call(copy_from(0), None, [weight], [((early, width), BF)], 0, (), True)[0]
    u1, d1 = up(first), down(first)
    late = call(copy_from(early), None, [weight], [((LATE, width), BF)], 0, [u1, d1], True)[0]
    u2, d2 = up(u1), down(d1)
    u3, d3 = up(u2), down(d2)
    w = [[first], [u1], [d1], [u2], [d2], [u3], [d3]]

    def arrange(where_ref, given, outs):
        for j, ref in enumerate(given):
            row = pl.multiple_of(where_ref[n + 1 + j] * own, own)
            for k in range(n):
                src = pl.multiple_of(where_ref[k] * width, width)
                outs[0][pl.ds(row, own), columns(k)] = ref[:, pl.ds(src, width)]

    toks = call(
        arrange,
        where,
        [tokens, far, over_core(tokens), over_core(far)],
        [((count, n * width), BF)],
        0,
    )[0]
    acc = project(list(range(n - 3)), None)
    late_far = over_x(late)
    a, b = ends(u3, d3, [acc, late_far])
    w.append([up(a), down(b)])
    acc = project([n - 3, n - 2], acc)

    def q_terms(p_ref, chunk, cols):
        total = None
        for ref, start in zip(chunk, bounds(chunk)):
            term = contract(p_ref[:, start : start + ref.shape[0]], ref[:, cols])
            total = term if total is None else total + term
        return total

    groups = [[0, 1], [2, 3], [4, 5], [6, 7]]
    near, more = groups[0] + groups[1], groups[2] + groups[3]
    unit = 2 * count * early * half
    wing = (count, half * len(near))

    def put_q(p_ref, chunks, cols, out):
        for at, chunk in enumerate(chunks):
            q = q_terms(p_ref, chunk, cols)
            out[:, at * half : (at + 1) * half] = q.astype(out.dtype)

    def first_give(where_ref, given, outs):
        tok, last, acc_ref, chunks = given

        def put(cols, value):
            outs[0][:, cols] = value
            outs[1][:, cols] = value.astype(BF)

        p_terms(tok, [n - 1], [last], acc_ref, put)
        put_q(outs[1], chunks, halves(where_ref, False), outs[2])

    p, p_b, give = call(
        first_give,
        where,
        (toks, w[-1], acc, [w[k] for k in near]),
        [((count, early), F32), ((count, early), BF), (wing, BF)],
        6 * unit,
    )

    def q_half(ks, own_half, dtype, after=()):
        def body(where_ref, given, outs):
            put_q(given[0], given[1], halves(where_ref, own_half), outs[0])

        ins = (p_b, [w[k] for k in ks])
        return call(body, where, ins, [(wing, dtype)], unit * len(ks), after)[0]

    def add_two(where_ref, given, outs):
        for g in range(2):
            q = given[0][:, columns(g)] + given[1][:, columns(g)].astype(F32)
            outs[g][...] = q
            outs[2 + g][...] = q.astype(BF)

    def q_pair(keep, got):
        return call(add_two, None, (keep, got), [(square, F32)] * 2 + [(square, BF)] * 2, 0)

    q0, q1, q0_b, q1_b = q_pair(q_half(near, True, F32), over_core(give))
    keep = q_half(more, True, F32, [q0_b])
    give = q_half(more, False, BF, [keep])
    q2, q3, q2_b, q3_b = q_pair(keep, over_core(give))

    def late_part(ks, accs, final, after=()):
        def body(where_ref, given, outs, *scratch):
            tok, lates, earlies, acc_refs = given
            p_out, g_out = scratch if final else outs

            def old(which, rows, cols):
                return None if accs is None else acc_refs[which][rows, cols]

            flat = [[m[0], m[1], o[0], o[1]] if len(m) == 2 else [m[0], o[0]] for m, o in lates]
            sets = [slice(j * LATE, (j + 1) * LATE) for j in range(4)]
            for cols in sets:
                pairs = [(tok[:, columns(k)], at_rows(f, cols)) for k, f in zip(ks, flat)]
                value = add_dots(pairs, old(0, slice(None), cols))
                p_out[:, cols] = value.astype(p_out.dtype)
                if final and cols.start == 0:
                    outs[0][...] = value
            for here in sets:
                for cols in cuts(earlies):
                    pairs = [(at_rows(f, here), at_rows(e, cols)) for f, e in zip(flat, earlies)]
                    g_out[here, cols] = add_dots(pairs, old(1, here, cols)).astype(g_out.dtype)
                cols = slice(early, rows)
                pairs = [(at_rows(f, here), at_rows(f, sets[0])) for f in flat]
                g_out[here, cols] = add_dots(pairs, old(1, here, cols)).astype(g_out.dtype)
            if final:
                for cols in tiles(rows):
                    outs[1][:, cols] = contract(p_out[...], g_out[:, cols])

        if final:
            outs = [((count, LATE), F32), ((count, rows), F32)]
            scratch = [pltpu.VMEM((count, wide), BF), pltpu.VMEM((wide, rows), BF)]
        else:
            outs = [((count, wide), F32), ((wide, rows), F32)]
            scratch = []
        flops = 2 * wide * (count + rows) * width * len(ks)
        ins = (toks, [v[k] for k in ks], [w[k] for k in ks], accs)
        return call(body, where, ins, outs, flops, after, False, scratch)

    def collect(ks, sides, out, final, after=()):
        def body(where_ref, given, outs):
            side_refs, chunks, out_ref, more = given
            for cols in cuts([e for e, _ in chunks]) + [slice(early, rows)]:
                term = None if out is None else out_ref[:, cols]
                for k, (early_rows, late_rows) in enumerate(chunks):
                    for ref, mine in zip(side_refs, (True, False)):
                        left = ref[:, k * half : (k + 1) * half]
                        if cols.start < early:
                            right = at_rows(early_rows, cols, halves(where_ref, mine))
                        else:
                            right = late_rows[0][0][:LATE, halves(where_ref, mine)]
                        term = add_dots([(left, right)], term)
                if final:
                    p_ref, late_ref, add_ref = more
                    p_val = p_ref[:, cols] if cols.start < early else late_ref[...]
                    term = 1.5 * p_val - 0.5 * (term + add_ref[:, cols])
                outs[0][:, cols] = term.astype(outs[0].dtype)

        outs = [jax.ShapeDtypeStruct((count, rows), BF) if final else ((count, rows), F32)]
        ins = (sides, [(w[k], v[k]) for k in ks], out, [p, p_late, out_late] if final else None)
        return call(body, where, ins, outs, 4 * count * rows * width, after)[0]

    def join(where_ref, given, outs):
        outs[0][:LATE, :] = given[0][...]
        outs[0][LATE:, :] = given[1][...]

    def turn(where_ref, given, outs):
        q_ref, far_ref, ring_refs, next_ref = given
        outs[0][...] = (q_ref[...] + far_ref[...].astype(F32)).astype(BF)
        if next_ref is not None:
            outs[1][...] = next_ref[...]
            relay(None, ring_refs, outs[2:4])
            if len(outs) > 4:
                split(None, ring_refs, outs[4:])

    def turned(q, far, ring_pair, next_q, last, after):
        outs = [(square, BF)]
        if next_q is not None:
            outs += [(square, BF)] + [((tall, width), BF)] * 2
            if last:
                outs += [((LATE, width), BF)] * 2
        return call(turn, None, (q, far, ring_pair, next_q), outs, 0, after)

    def both(pieces):
        return (pieces, [over_core(c) for c in pieces])

    tall = 2 * LATE
    block = call(join, None, [late, late_far], [((tall, width), BF)], 0, [p_b])[0]
    v = [both([block])]
    far, u, d = over_x(q0_b), up(block), down(block)
    sums = late_part([0], None, False, [q0_b])
    s0, nq, ru, rd = turned(q0, far, [u, d], q1_b, False, [sums[0], give])
    v += [both([ru]), both([rd])]
    far, u, d = over_x(nq), up(ru), down(rd)
    sums = late_part([1, 2], sums, False, [s0])
    s1, nq, ru, rd = turned(q1, far, [u, d], q2_b, False, [sums[0]])
    v += [both([ru]), both([rd])]
    far, u, d = over_x(nq), up(ru), down(rd)
    sums = late_part([3, 4], sums, False, [s1])
    out = collect(groups[0], [s0, over_core(s0)], None, False, [sums[0]])
    s2, nq, ru, rd, ra, rb = turned(q2, far, [u, d], q3_b, True, [out])
    v += [both([ru]), both([rd])]
    far, a, b = over_x(nq), up(ra), down(rb)
    sums = late_part([5, 6], sums, False, [s2])
    v += [both([a, b])]
    out = collect(groups[1], [s1, over_core(s1)], out, False, [sums[0]])
    out = collect(groups[2], [s2, over_core(s2)], out, False)
    s3 = turned(q3, far, None, None, False, [out])[0]
    p_late, out_late = late_part([n - 1], sums, True, [s3])
    return collect(groups[3], [s3, over_core(s3)], out, True)


def solution(mesh):
    n = mesh.shape["dp"]

    def on_device(tokens, weight):
        if mesh.shape["tensor"] == 4 and n == 8:
            return ring_form(n, tokens, weight)
        return gathered_form(tokens, weight)

    placed = (P(("dp", "tensor"), None), P("tensor", "dp"))
    return jax.shard_map(
        on_device, mesh=mesh, in_specs=placed, out_specs=P("dp", "tensor"), check_vma=False
    )
```

time: 855 us -> 151 us (0.18)
  blocking collectives: 645 us -> 0 us
  waiting for transfers between devices: 163 us -> 67.8 us
  Pallas kernels: 0 us -> 50.3 us
  matrix products: 33 us -> 0 us
  starting transfers between devices: 0.08 us -> 29.4 us
  between operations: 13.1 us -> 0.35 us
    psum x1 -> x0, blocking collectives: 645 us -> none  [on_device(): gram_cols = lax.psum(term, 'dp').astype(jnp.bfloat16)]
    all_gather x3 -> x0, waiting for transfers between devices: 161 us -> none  [the longest x1 123 us: on_device(): full_rows = lax.all_gather(ortho, 'dp', axis=1, tiled=True)]
    ppermute x0 -> x39, waiting for transfers between devices: none -> 67.8 us  [the longest x8 37 us: up(): lax.ppermute(v, 'dp', [(ring[i], ring[(i + 1) % n]) for i in range(n)])]
    pallas_call x0 -> x26, Pallas kernels: none -> 50.3 us  [call(): pl.pallas_call(kernel, out_shape=[pltpu.VMEM(*o) if isinstance(o, tuple)...]
    dot_general x3 -> x0, matrix products: 33 us -> none  [the longest x2 22.9 us: contract_last(): lax.dot_general(left, right, (((1,), (1,)), ((), ())), preferred_element_...]
    ppermute x0 -> x39, starting transfers between devices: none -> 29.4 us  [the longest x8 13.5 us: up(): lax.ppermute(v, 'dp', [(ring[i], ring[(i + 1) % n]) for i in range(n)])]
  transfers between devices with their start and end apart: 3 -> 39, of which waited for: 2 -> 17; matrix products, arithmetic and copies ran while one was open for 3% -> 0% of each run, Pallas kernels for 0% -> 29%
where the time goes in v2:
time: 151 us; the launch traced here: 150 us
  waiting for transfers between devices  67.8 us (45%)
  Pallas kernels  50.3 us (33%)
  starting transfers between devices  29.4 us (19%)
  local copies, waits for them, and re-layouts  2.26 us (1%)
    pallas_call x26, Pallas kernels, call(): pl.pallas_call(kernel, out_shape=[pltpu.VMEM(*o) if isinstance(o, tuple)...  50.3 us
    ppermute x8, waiting for transfers between devices, up(): lax.ppermute(v, 'dp', [(ring[i], ring[(i + 1) % n]) for i in range(n)])  37 us
    ppermute x6, waiting for transfers between devices, over_x(): return lax.ppermute(v, 'tensor', [(t, t ^ 2) for t in range(4)])  23.7 us
    ppermute x8, starting transfers between devices, up(): lax.ppermute(v, 'dp', [(ring[i], ring[(i + 1) % n]) for i in range(n)])  13.5 us
    ppermute x6, starting transfers between devices, over_x(): return lax.ppermute(v, 'tensor', [(t, t ^ 2) for t in range(4)])  8.46 us
    ppermute x8, waiting for transfers between devices, down(): lax.ppermute(v, 'dp', [(ring[(i + 1) % n], ring[i]) for i in range(n)])  5.05 us
    ppermute x8, starting transfers between devices, down(): lax.ppermute(v, 'dp', [(ring[(i + 1) % n], ring[i]) for i in range(n)])  3.78 us
    ppermute x17, starting transfers between devices, over_core(): return lax.ppermute(v, 'tensor', [(t, t ^ 1) for t in range(4)])  3.65 us
  transfers between devices with their start and end apart: 39, of which 17 were waited for; matrix products, arithmetic and copies ran while one was open for 0% of the time, Pallas kernels for 29%

profile of v2, /device:TPU:0, one launch (start us, length us, event | category | flops | bytes accessed | tf_op | source)
XLA Modules:
  0.0 150.2 jit_solution(16776054878016400884)
XLA Ops:
  1.2 3.1 %collective-permute-start.3 = (bf16[768,512]{1,0:T(8,128)(2,1)S(1)}, bf16[768,512]{1,0:T(8,128)(2,1)S(1)}, u32[]{:S(2)}, u32[]{:S(2)}) collective-permute-start(bf16[768,512]{1,0:T(8,128)(2,1)S(1)} %shard_map.38.refs_2_.refs_5_.refs_4_.refs_3_), channel_id=1, source_target_pairs={{0,8},{8,16},{16,24},{24,28},{28,20},{20,12},{12,4},{4,0},{1,9},{9... | collective-permute-start | bytes 2359304 | tf_op jit(solution)/shard_map/ppermute | solution.py:115
  5.1 1.9 %collective-permute-start = (bf16[128,4096]{1,0:T(8,128)(2,1)}, bf16[128,4096]{1,0:T(8,128)(2,1)}, u32[]{:S(2)}, u32[]{:S(2)}) collective-permute-start(bf16[128,4096]{1,0:T(8,128)(2,1)} %refs_1_.1), channel_id=1, source_target_pairs={{0,2},{1,3},{2,0},{3,1},{4,6},{5,7},{6,4},{7,5},{8,10},{9,11},{10,... | collective-permute-start | bytes 3145736 | tf_op jit(solution)/shard_map/ppermute | solution.py:121
  7.1 14.7 %collective-permute-done.3.refs_3_.refs_1_.refs_6_ = bf16[768,512]{1,0:T(8,128)(2,1)S(1)} collective-permute-done((bf16[768,512]{1,0:T(8,128)(2,1)S(1)}, bf16[768,512]{1,0:T(8,128)(2,1)S(1)}, u32[]{:S(2)}, u32[]{:S(2)}) %collective-permute-start.3) | collective-permute-done | bytes 786464 | tf_op jit(solution)/shard_map/ppermute | solution.py:115
  23.8 6.3 %collective-permute-done.refs_2_ = bf16[128,4096]{1,0:T(8,128)(2,1)} collective-permute-done((bf16[128,4096]{1,0:T(8,128)(2,1)}, bf16[128,4096]{1,0:T(8,128)(2,1)}, u32[]{:S(2)}, u32[]{:S(2)}) %collective-permute-start) | collective-permute-done | bytes 1048608 | tf_op jit(solution)/shard_map/ppermute | solution.py:121
  30.1 10.6 %collective-permute-done.4.refs_5_.refs_8_.refs_6_ = bf16[768,512]{1,0:T(8,128)(2,1)} collective-permute-done((bf16[768,512]{1,0:T(8,128)(2,1)S(1)}, bf16[768,512]{1,0:T(8,128)(2,1)}, u32[]{:S(2)}, u32[]{:S(2)}) %collective-permute-start.4) | collective-permute-done | bytes 786464 | tf_op jit(solution)/shard_map/ppermute | solution.py:115
  46.6 2.2 %shard_map.37.refs_1_ = bf16[512,4096]{1,0:T(8,128)(2,1)S(1)} custom-call(s32[13]{0:T(128)S(1)} %concatenate.3.refs_0_, bf16[128,4096]{1,0:T(8,128)(2,1)S(1)} %copy-done.2, bf16[128,4096]{1,0:T(8,128)(2,1)} %collective-permute-done.refs_2_, bf16[128,4096]{1,0:T(8,128)(2,1)} %collective-permute-done.1.refs_3_, bf16[128,4096]{1,0:T(8,128)(2,1)} %collective-permute-done.2.refs_4_), custom_call_target="tpu_custom_call" | custom-call | bytes 4194304 | tf_op jit(solution)/shard_map/pallas_call | solution.py:54
  48.8 3.6 %shard_map.39.refs_2_.refs_4_ = f32[512,768]{1,0:T(8,128)S(1)} custom-call(s32[13]{0:T(128)S(1)} %concatenate.3.refs_0_, bf16[512,4096]{1,0:T(8,128)(2,1)S(1)} %shard_map.37.refs_1_, bf16[768,512]{1,0:T(8,128)(2,1)S(1)} %copy-done.1, bf16[768,512]{1,0:T(8,128)(2,1)S(1)} %collective-permute-done.3.refs_3_.refs_1_.refs_6_, ...), custom_call_target="tpu_custom_call" | custom-call | flops 2013265920 | bytes 8126464 | tf_op jit(solution)/shard_map/pallas_call | solution.py:54
  52.4 6.3 %collective-permute-done.5.refs_0_.refs_2_.refs_3_.refs_6_ = bf16[768,512]{1,0:T(8,128)(2,1)S(1)} collective-permute-done((bf16[768,512]{1,0:T(8,128)(2,1)}, bf16[768,512]{1,0:T(8,128)(2,1)S(1)}, u32[]{:S(2)}, u32[]{:S(2)}) %collective-permute-start.5) | collective-permute-done | bytes 786464 | tf_op jit(solution)/shard_map/ppermute | solution.py:115
  63.4 4.4 %collective-permute-done.10.refs_2_.refs_5_.refs_6_ = bf16[384,512]{1,0:T(8,128)(2,1)S(1)} collective-permute-done((bf16[384,512]{1,0:T(8,128)(2,1)S(1)}, bf16[384,512]{1,0:T(8,128)(2,1)S(1)}, u32[]{:S(2)}, u32[]{:S(2)}) %collective-permute-start.10) | collective-permute-done | bytes 393248 | tf_op jit(solution)/shard_map/ppermute | solution.py:115
  69.1 2.7 %shard_map.43 = (f32[512,768]{1,0:T(8,128)S(1)}, bf16[512,768]{1,0:T(8,128)(2,1)S(1)}, bf16[512,1024]{1,0:T(8,128)(2,1)S(1)}) custom-call(s32[13]{0:T(128)S(1)} %concatenate.3.refs_0_, bf16[512,4096]{1,0:T(8,128)(2,1)S(1)} %shard_map.37.refs_1_, bf16[384,512]{1,0:T(8,128)(2,1)S(1)} %collective-permute-done.10.refs_2_.refs_5_.refs_6_, ...), custom_call_target="tpu_custom_call" | custom-call | flops 1207959552 | bytes 9699328 | tf_op jit(solution)/shard_map/pallas_call | solution.py:54
  75.5 2.1 %shard_map.44.refs_0_ = f32[512,1024]{1,0:T(8,128)S(1)} custom-call(s32[13]{0:T(128)S(1)} %concatenate.3.refs_0_, bf16[512,768]{1,0:T(8,128)(2,1)S(1)} %get-tuple-element.44.refs_1_.refs_2_, bf16[768,512]{1,0:T(8,128)(2,1)S(1)} %copy-done.1, bf16[768,512]{1,0:T(8,128)(2,1)S(1)} %collective-permute-done.3.refs_3_.refs_1_.refs_6_, ...), custom_call_target="tpu_custom_call" | custom-call | flops 805306368 | bytes 3932160 | tf_op jit(solution)/shard_map/pallas_call | solution.py:54
  79.5 2.2 %shard_map.46.refs_7_.refs_0_ = f32[512,1024]{1,0:T(8,128)S(1)} custom-call(s32[13]{0:T(128)S(1)} %concatenate.3.refs_0_, bf16[512,768]{1,0:T(8,128)(2,1)S(1)} %get-tuple-element.44.refs_1_.refs_2_, bf16[768,512]{1,0:T(8,128)(2,1)} %collective-permute-done.7.refs_6_.refs_2_.refs_7_.refs_3_, ...), custom_call_target="tpu_custom_call" | custom-call | flops 805306368 | bytes 3932160 | tf_op jit(solution)/shard_map/pallas_call | solution.py:54
  81.7 2.2 %shard_map.47.refs_6_ = bf16[512,1024]{1,0:T(8,128)(2,1)S(1)} custom-call(s32[13]{0:T(128)S(1)} %concatenate.3.refs_0_, bf16[512,768]{1,0:T(8,128)(2,1)S(1)} %get-tuple-element.44.refs_1_.refs_2_, bf16[768,512]{1,0:T(8,128)(2,1)} %collective-permute-done.7.refs_6_.refs_2_.refs_7_.refs_3_, ...), custom_call_target="tpu_custom_call" | custom-call | flops 805306368 | bytes 3932160 | tf_op jit(solution)/shard_map/pallas_call | solution.py:54
  84.0 2.4 %shard_map.50 = (f32[512,1024]{1,0:T(8,128)S(1)}, f32[1024,1024]{1,0:T(8,128)S(1)}) custom-call(s32[13]{0:T(128)S(1)} %concatenate.3.refs_0_, bf16[512,4096]{1,0:T(8,128)(2,1)S(1)} %shard_map.37.refs_1_, bf16[512,512]{1,0:T(8,128)(2,1)S(1)} %shard_map.49.refs_2_.refs_4_, bf16[512,512]{1,0:T(8,128)(2,1)S(1)} %collective-permute-done.17.refs_3_.refs_5_, ...), custom_call_target="tpu_custom_call" | custom-call | flops 1610612736 | bytes 6029312 | tf_op jit(solution)/shard_map/pallas_call | solution.py:54
  88.6 2.7 %collective-permute-done.14.refs_1_ = bf16[512,512]{1,0:T(8,128)(2,1)S(1)} collective-permute-done((bf16[512,512]{1,0:T(8,128)(2,1)S(1)}, bf16[512,512]{1,0:T(8,128)(2,1)S(1)}, u32[]{:S(2)}, u32[]{:S(2)}) %collective-permute-start.14) | collective-permute-done | bytes 524320 | tf_op jit(solution)/shard_map/ppermute | solution.py:121
  95.6 4.1 %shard_map.52 = (f32[512,1024]{1,0:T(8,128)S(1)}, f32[1024,1024]{1,0:T(8,128)S(1)}) custom-call(s32[13]{0:T(128)S(1)} %concatenate.3.refs_0_, bf16[512,4096]{1,0:T(8,128)(2,1)S(1)} %shard_map.37.refs_1_, bf16[512,512]{1,0:T(8,128)(2,1)S(1)} %get-tuple-element.54.refs_2_.refs_7_, bf16[512,512]{1,0:T(8,128)(2,1)S(1)} %collective-permute-done.21.refs_3_.refs_8_, ...), custom_call_target="tpu_custom_call" | custom-call | flops 3221225472 | bytes 14155776 | tf_op jit(solution)/shard_map/pallas_call | solution.py:54
  100.1 7.2 %collective-permute-done.18.refs_1_ = bf16[512,512]{1,0:T(8,128)(2,1)S(1)} collective-permute-done((bf16[512,512]{1,0:T(8,128)(2,1)S(1)}, bf16[512,512]{1,0:T(8,128)(2,1)S(1)}, u32[]{:S(2)}, u32[]{:S(2)}) %collective-permute-start.18) | collective-permute-done | bytes 524320 | tf_op jit(solution)/shard_map/ppermute | solution.py:121
  111.9 5.0 %shard_map.54 = (f32[512,1024]{1,0:T(8,128)S(1)}, f32[1024,1024]{1,0:T(8,128)S(1)}) custom-call(s32[13]{0:T(128)S(1)} %concatenate.3.refs_0_, bf16[512,4096]{1,0:T(8,128)(2,1)S(1)} %shard_map.37.refs_1_, bf16[512,512]{1,0:T(8,128)(2,1)S(1)} %get-tuple-element.61.refs_2_.refs_7_, bf16[512,512]{1,0:T(8,128)(2,1)S(1)} %collective-permute-done.27.refs_3_.refs_8_, ...), custom_call_target="tpu_custom_call" | custom-call | flops 3221225472 | bytes 14155776 | tf_op jit(solution)/shard_map/pallas_call | solution.py:54
  118.8 6.1 %collective-permute-done.23.refs_1_ = bf16[512,512]{1,0:T(8,128)(2,1)S(1)} collective-permute-done((bf16[512,512]{1,0:T(8,128)(2,1)S(1)}, bf16[512,512]{1,0:T(8,128)(2,1)S(1)}, u32[]{:S(2)}, u32[]{:S(2)}) %collective-permute-start.23) | collective-permute-done | bytes 524320 | tf_op jit(solution)/shard_map/ppermute | solution.py:121
  130.0 4.1 %shard_map.57 = (f32[512,1024]{1,0:T(8,128)S(1)}, f32[1024,1024]{1,0:T(8,128)S(1)}) custom-call(s32[13]{0:T(128)S(1)} %concatenate.3.refs_0_, bf16[512,4096]{1,0:T(8,128)(2,1)S(1)} %shard_map.37.refs_1_, bf16[512,512]{1,0:T(8,128)(2,1)S(1)} %get-tuple-element.69.refs_2_.refs_7_, bf16[512,512]{1,0:T(8,128)(2,1)S(1)} %collective-permute-done.31.refs_3_.refs_8_, ...), custom_call_target="tpu_custom_call" | custom-call | flops 3221225472 | bytes 14155776 | tf_op jit(solution)/shard_map/pallas_call | solution.py:54
  134.1 2.4 %shard_map.58.refs_9_ = f32[512,1024]{1,0:T(8,128)S(1)} custom-call(s32[13]{0:T(128)S(1)} %concatenate.3.refs_0_, bf16[512,512]{1,0:T(8,128)(2,1)S(1)} %get-tuple-element.65.refs_10_.refs_1_, bf16[512,512]{1,0:T(8,128)(2,1)S(1)} %collective-permute-done.32.refs_2_, bf16[768,512]{1,0:T(8,128)(2,1)S(1)} %collective-permute-done.6.refs_4_.refs_2_.refs_7_.refs_3_, ...), custom_call_target="tpu_custom_call" | custom-call | flops 1073741824 | bytes 6815744 | tf_op jit(solution)/shard_map/pallas_call | solution.py:54
  136.6 2.4 %shard_map.59.refs_2_.refs_12_ = f32[512,1024]{1,0:T(8,128)S(1)} custom-call(s32[13]{0:T(128)S(1)} %concatenate.3.refs_0_, bf16[512,512]{1,0:T(8,128)(2,1)S(1)} %get-tuple-element.68.refs_10_.refs_1_, bf16[512,512]{1,0:T(8,128)(2,1)S(1)} %collective-permute-done.30.refs_2_, bf16[768,512]{1,0:T(8,128)(2,1)} %collective-permute-done.7.refs_6_.refs_2_.refs_7_.refs_3_, ...), custom_call_target="tpu_custom_call" | custom-call | flops 1073741824 | bytes 6815744 | tf_op jit(solution)/shard_map/pallas_call | solution.py:54
  143.2 3.8 %shard_map.61 = (f32[512,256]{1,0:T(8,128)S(1)}, f32[512,1024]{1,0:T(8,128)S(1)}) custom-call(s32[13]{0:T(128)S(1)} %concatenate.3.refs_0_, bf16[512,4096]{1,0:T(8,128)(2,1)S(1)} %shard_map.37.refs_1_, bf16[256,512]{1,0:T(8,128)(2,1)S(1)} %collective-permute-done.35.refs_2_.refs_8_, bf16[256,512]{1,0:T(8,128)(2,1)S(1)} %collective-permute-done.36.refs_3_.refs_9_, ...), custom_call_target="tpu_custom_call" | custom-call | flops 1610612736 | bytes 12320768 | tf_op jit(solution)/shard_map/pallas_call | solution.py:54
  147.0 3.2 %shard_map.62 = bf16[512,1024]{1,0:T(8,128)(2,1)} custom-call(s32[13]{0:T(128)S(1)} %concatenate.3.refs_0_, bf16[512,512]{1,0:T(8,128)(2,1)S(1)} %shard_map.60.refs_10_.refs_1_, bf16[512,512]{1,0:T(8,128)(2,1)S(1)} %collective-permute-done.34.refs_2_, bf16[768,512]{1,0:T(8,128)(2,1)S(1)} %collective-permute-done.8.refs_1_.refs_3_.refs_4_.refs_7_, ...), custom_call_target="tpu_custom_call" | custom-call | flops 1073741824 | bytes 11010048 | tf_op jit(solution)/shard_map/pallas_call | solution.py:54
  (90 shorter events, 44.0 us)
Async XLA Ops:
  1.2 20.6 %collective-permute-start.3 = (bf16[768,512]{1,0:T(8,128)(2,1)S(1)}, bf16[768,512]{1,0:T(8,128)(2,1)S(1)}, u32[]{:S(2)}, u32[]{:S(2)}) collective-permute-start(bf16[768,512]{1,0:T(8,128)(2,1)S(1)} %shard_map.38.refs_2_.refs_5_.refs_4_.refs_3_), channel_id=1, source_target_pairs={{0,8},{8,16},{16,24},{24,28},{28,20},{20,12},{12,4},{4,0},{1,9},{9... | collective-permute-start | bytes 2359304 | tf_op jit(solution)/shard_map/ppermute | solution.py:115
  4.2 19.3 %collective-permute-start.6 = (bf16[768,512]{1,0:T(8,128)(2,1)S(1)}, bf16[768,512]{1,0:T(8,128)(2,1)S(1)}, u32[]{:S(2)}, u32[]{:S(2)}) collective-permute-start(bf16[768,512]{1,0:T(8,128)(2,1)S(1)} %shard_map.38.refs_2_.refs_5_.refs_4_.refs_3_), channel_id=1, source_target_pairs={{8,0},{16,8},{24,16},{28,24},{20,28},{12,20},{4,12},{0,4},{9,1},{1... | collective-permute-start | bytes 2359304 | tf_op jit(solution)/shard_map/ppermute | solution.py:118
  5.1 24.9 %collective-permute-start = (bf16[128,4096]{1,0:T(8,128)(2,1)}, bf16[128,4096]{1,0:T(8,128)(2,1)}, u32[]{:S(2)}, u32[]{:S(2)}) collective-permute-start(bf16[128,4096]{1,0:T(8,128)(2,1)} %refs_1_.1), channel_id=1, source_target_pairs={{0,2},{1,3},{2,0},{3,1},{4,6},{5,7},{6,4},{7,5},{8,10},{9,11},{10,... | collective-permute-start | bytes 3145736 | tf_op jit(solution)/shard_map/ppermute | solution.py:121
  21.7 18.9 %collective-permute-start.4 = (bf16[768,512]{1,0:T(8,128)(2,1)S(1)}, bf16[768,512]{1,0:T(8,128)(2,1)}, u32[]{:S(2)}, u32[]{:S(2)}) collective-permute-start(bf16[768,512]{1,0:T(8,128)(2,1)S(1)} %collective-permute-done.3.refs_3_.refs_1_.refs_6_), channel_id=1, source_target_pairs={{0,8},{8,16},{16,24},{24,28},{28,20},{20,12},{12,4},{4,0},{1,9},{9... | collective-permute-start | bytes 2359304 | tf_op jit(solution)/shard_map/ppermute | solution.py:115
  23.5 18.6 %collective-permute-start.7 = (bf16[768,512]{1,0:T(8,128)(2,1)S(1)}, bf16[768,512]{1,0:T(8,128)(2,1)}, u32[]{:S(2)}, u32[]{:S(2)}) collective-permute-start(bf16[768,512]{1,0:T(8,128)(2,1)S(1)} %collective-permute-done.6.refs_4_.refs_2_.refs_7_.refs_3_), channel_id=1, source_target_pairs={{8,0},{16,8},{24,16},{28,24},{20,28},{12,20},{4,12},{0,4},{9,1},{1... | collective-permute-start | bytes 2359304 | tf_op jit(solution)/shard_map/ppermute | solution.py:118
  23.8 21.5 %collective-permute-start.1 = (bf16[128,4096]{1,0:T(8,128)(2,1)}, bf16[128,4096]{1,0:T(8,128)(2,1)}, u32[]{:S(2)}, u32[]{:S(2)}) collective-permute-start(bf16[128,4096]{1,0:T(8,128)(2,1)} %refs_1_.1), channel_id=1, source_target_pairs={{0,1},{1,0},{2,3},{3,2},{4,5},{5,4},{6,7},{7,6},{8,9},{9,8},{10,11... | collective-permute-start | bytes 3145736 | tf_op jit(solution)/shard_map/ppermute | solution.py:124
  30.1 15.2 %collective-permute-start.2 = (bf16[128,4096]{1,0:T(8,128)(2,1)}, bf16[128,4096]{1,0:T(8,128)(2,1)}, u32[]{:S(2)}, u32[]{:S(2)}) collective-permute-start(bf16[128,4096]{1,0:T(8,128)(2,1)} %collective-permute-done.refs_2_), channel_id=1, source_target_pairs={{0,1},{1,0},{2,3},{3,2},{4,5},{5,4},{6,7},{7,6},{8,9},{9,8},{10,11... | collective-permute-start | bytes 3145736 | tf_op jit(solution)/shard_map/ppermute | solution.py:124
  40.7 18.1 %collective-permute-start.5 = (bf16[768,512]{1,0:T(8,128)(2,1)}, bf16[768,512]{1,0:T(8,128)(2,1)S(1)}, u32[]{:S(2)}, u32[]{:S(2)}) collective-permute-start(bf16[768,512]{1,0:T(8,128)(2,1)} %collective-permute-done.4.refs_5_.refs_8_.refs_6_), channel_id=1, source_target_pairs={{0,8},{8,16},{16,24},{24,28},{28,20},{20,12},{12,4},{4,0},{1,9},{9... | collective-permute-start | bytes 2359304 | tf_op jit(solution)/shard_map/ppermute | solution.py:115
  42.1 17.5 %collective-permute-start.8 = (bf16[768,512]{1,0:T(8,128)(2,1)}, bf16[768,512]{1,0:T(8,128)(2,1)S(1)}, u32[]{:S(2)}, u32[]{:S(2)}) collective-permute-start(bf16[768,512]{1,0:T(8,128)(2,1)} %collective-permute-done.7.refs_6_.refs_2_.refs_7_.refs_3_), channel_id=1, source_target_pairs={{8,0},{16,8},{24,16},{28,24},{20,28},{12,20},{4,12},{0,4},{9,1},{1... | collective-permute-start | bytes 2359304 | tf_op jit(solution)/shard_map/ppermute | solution.py:118
  72.9 11.1 %collective-permute-start.17 = (bf16[512,512]{1,0:T(8,128)(2,1)S(1)}, bf16[512,512]{1,0:T(8,128)(2,1)S(1)}, u32[]{:S(2)}, u32[]{:S(2)}) collective-permute-start(bf16[512,512]{1,0:T(8,128)(2,1)S(1)} %shard_map.49.refs_2_.refs_4_), channel_id=1, source_target_pairs={{0,1},{1,0},{2,3},{3,2},{4,5},{5,4},{6,7},{7,6},{8,9},{9,8},{10,11... | collective-permute-start | bytes 1572872 | tf_op jit(solution)/shard_map/ppermute | solution.py:124
  73.5 13.9 %collective-permute-start.15 = (bf16[512,512]{1,0:T(8,128)(2,1)S(1)}, bf16[512,512]{1,0:T(8,128)(2,1)S(1)}, u32[]{:S(2)}, u32[]{:S(2)}) collective-permute-start(bf16[512,512]{1,0:T(8,128)(2,1)S(1)} %shard_map.49.refs_2_.refs_4_), channel_id=1, source_target_pairs={{0,8},{8,16},{16,24},{24,28},{28,20},{20,12},{12,4},{4,0},{1,9},{9... | collective-permute-start | bytes 1572872 | tf_op jit(solution)/shard_map/ppermute | solution.py:115
  75.0 13.6 %collective-permute-start.16 = (bf16[512,512]{1,0:T(8,128)(2,1)S(1)}, bf16[512,512]{1,0:T(8,128)(2,1)S(1)}, u32[]{:S(2)}, u32[]{:S(2)}) collective-permute-start(bf16[512,512]{1,0:T(8,128)(2,1)S(1)} %shard_map.49.refs_2_.refs_4_), channel_id=1, source_target_pairs={{8,0},{16,8},{24,16},{28,24},{20,28},{12,20},{4,12},{0,4},{9,1},{1... | collective-permute-start | bytes 1572872 | tf_op jit(solution)/shard_map/ppermute | solution.py:118
  77.9 13.4 %collective-permute-start.14 = (bf16[512,512]{1,0:T(8,128)(2,1)S(1)}, bf16[512,512]{1,0:T(8,128)(2,1)S(1)}, u32[]{:S(2)}, u32[]{:S(2)}) collective-permute-start(bf16[512,512]{1,0:T(8,128)(2,1)S(1)} %get-tuple-element.46.refs_7_.refs_5_), channel_id=1, source_target_pairs={{0,2},{1,3},{2,0},{3,1},{4,6},{5,7},{6,4},{7,5},{8,10},{9,11},{10,... | collective-permute-start | bytes 1572872 | tf_op jit(solution)/shard_map/ppermute | solution.py:121
  83.9 15.9 %collective-permute-start.13 = (bf16[512,1024]{1,0:T(8,128)(2,1)S(1)}, bf16[512,1024]{1,0:T(8,128)(2,1)S(1)}, u32[]{:S(2)}, u32[]{:S(2)}) collective-permute-start(bf16[512,1024]{1,0:T(8,128)(2,1)S(1)} %shard_map.47.refs_6_), channel_id=1, source_target_pairs={{0,1},{1,0},{2,3},{3,2},{4,5},{5,4},{6,7},{7,6},{8,9},{9,8},{10,11... | collective-permute-start | bytes 3145736 | tf_op jit(solution)/shard_map/ppermute | solution.py:124
  92.1 15.2 %collective-permute-start.19 = (bf16[512,512]{1,0:T(8,128)(2,1)S(1)}, bf16[512,512]{1,0:T(8,128)(2,1)S(1)}, u32[]{:S(2)}, u32[]{:S(2)}) collective-permute-start(bf16[512,512]{1,0:T(8,128)(2,1)S(1)} %get-tuple-element.54.refs_2_.refs_7_), channel_id=1, source_target_pairs={{0,8},{8,16},{16,24},{24,28},{28,20},{20,12},{12,4},{4,0},{1,9},{9... | collective-permute-start | bytes 1572872 | tf_op jit(solution)/shard_map/ppermute | solution.py:115
  93.7 13.6 %collective-permute-start.18 = (bf16[512,512]{1,0:T(8,128)(2,1)S(1)}, bf16[512,512]{1,0:T(8,128)(2,1)S(1)}, u32[]{:S(2)}, u32[]{:S(2)}) collective-permute-start(bf16[512,512]{1,0:T(8,128)(2,1)S(1)} %get-tuple-element.53), channel_id=1, source_target_pairs={{0,2},{1,3},{2,0},{3,1},{4,6},{5,7},{6,4},{7,5},{8,10},{9,11},{10,... | collective-permute-start | bytes 1572872 | tf_op jit(solution)/shard_map/ppermute | solution.py:121
  95.2 13.3 %collective-permute-start.20 = (bf16[512,512]{1,0:T(8,128)(2,1)S(1)}, bf16[512,512]{1,0:T(8,128)(2,1)S(1)}, u32[]{:S(2)}, u32[]{:S(2)}) collective-permute-start(bf16[512,512]{1,0:T(8,128)(2,1)S(1)} %get-tuple-element.55.refs_4_), channel_id=1, source_target_pairs={{8,0},{16,8},{24,16},{28,24},{20,28},{12,20},{4,12},{0,4},{9,1},{1... | collective-permute-start | bytes 1572872 | tf_op jit(solution)/shard_map/ppermute | solution.py:118
  109.4 15.5 %collective-permute-start.24 = (bf16[512,512]{1,0:T(8,128)(2,1)S(1)}, bf16[512,512]{1,0:T(8,128)(2,1)S(1)}, u32[]{:S(2)}, u32[]{:S(2)}) collective-permute-start(bf16[512,512]{1,0:T(8,128)(2,1)S(1)} %get-tuple-element.61.refs_2_.refs_7_), channel_id=1, source_target_pairs={{0,8},{8,16},{16,24},{24,28},{28,20},{20,12},{12,4},{4,0},{1,9},{9... | collective-permute-start | bytes 1572872 | tf_op jit(solution)/shard_map/ppermute | solution.py:115
  110.9 14.0 %collective-permute-start.23 = (bf16[512,512]{1,0:T(8,128)(2,1)S(1)}, bf16[512,512]{1,0:T(8,128)(2,1)S(1)}, u32[]{:S(2)}, u32[]{:S(2)}) collective-permute-start(bf16[512,512]{1,0:T(8,128)(2,1)S(1)} %get-tuple-element.60), channel_id=1, source_target_pairs={{0,2},{1,3},{2,0},{3,1},{4,6},{5,7},{6,4},{7,5},{8,10},{9,11},{10,... | collective-permute-start | bytes 1572872 | tf_op jit(solution)/shard_map/ppermute | solution.py:121
  111.4 13.7 %collective-permute-start.25 = (bf16[512,512]{1,0:T(8,128)(2,1)S(1)}, bf16[512,512]{1,0:T(8,128)(2,1)S(1)}, u32[]{:S(2)}, u32[]{:S(2)}) collective-permute-start(bf16[512,512]{1,0:T(8,128)(2,1)S(1)} %get-tuple-element.62.refs_4_), channel_id=1, source_target_pairs={{8,0},{16,8},{24,16},{28,24},{20,28},{12,20},{4,12},{0,4},{9,1},{1... | collective-permute-start | bytes 1572872 | tf_op jit(solution)/shard_map/ppermute | solution.py:118
  126.0 10.5 %collective-permute-start.30 = (bf16[512,512]{1,0:T(8,128)(2,1)S(1)}, bf16[512,512]{1,0:T(8,128)(2,1)S(1)}, u32[]{:S(2)}, u32[]{:S(2)}) collective-permute-start(bf16[512,512]{1,0:T(8,128)(2,1)S(1)} %get-tuple-element.68.refs_10_.refs_1_), channel_id=1, source_target_pairs={{0,1},{1,0},{2,3},{3,2},{4,5},{5,4},{6,7},{7,6},{8,9},{9,8},{10,11... | collective-permute-start | bytes 1572872 | tf_op jit(solution)/shard_map/ppermute | solution.py:124
  126.5 13.9 %collective-permute-start.29 = (bf16[512,512]{1,0:T(8,128)(2,1)S(1)}, bf16[512,512]{1,0:T(8,128)(2,1)S(1)}, u32[]{:S(2)}, u32[]{:S(2)}) collective-permute-start(bf16[512,512]{1,0:T(8,128)(2,1)S(1)} %get-tuple-element.67), channel_id=1, source_target_pairs={{0,2},{1,3},{2,0},{3,1},{4,6},{5,7},{6,4},{7,5},{8,10},{9,11},{10,... | collective-permute-start | bytes 1572872 | tf_op jit(solution)/shard_map/ppermute | solution.py:121
  128.0 12.6 %collective-permute-start.35 = (bf16[256,512]{1,0:T(8,128)(2,1)S(1)}, bf16[256,512]{1,0:T(8,128)(2,1)S(1)}, u32[]{:S(2)}, u32[]{:S(2)}) collective-permute-start(bf16[256,512]{1,0:T(8,128)(2,1)S(1)} %get-tuple-element.73), channel_id=1, source_target_pairs={{0,8},{8,16},{16,24},{24,28},{28,20},{20,12},{12,4},{4,0},{1,9},{9... | collective-permute-start | bytes 786440 | tf_op jit(solution)/shard_map/ppermute | solution.py:115
  128.8 12.2 %collective-permute-start.36 = (bf16[256,512]{1,0:T(8,128)(2,1)S(1)}, bf16[256,512]{1,0:T(8,128)(2,1)S(1)}, u32[]{:S(2)}, u32[]{:S(2)}) collective-permute-start(bf16[256,512]{1,0:T(8,128)(2,1)S(1)} %get-tuple-element.74), channel_id=1, source_target_pairs={{8,0},{16,8},{24,16},{28,24},{20,28},{12,20},{4,12},{0,4},{9,1},{1... | collective-permute-start | bytes 786440 | tf_op jit(solution)/shard_map/ppermute | solution.py:118
  (19 other events, 127.4 us)

commit v3 on v2

v3 whole, which is shorter than its diff:
```python
import jax
import jax.numpy as jnp
from jax import lax
from jax.experimental import pallas as pl
from jax.experimental.pallas import tpu as pltpu
from jax.sharding import PartitionSpec as P

BF = jnp.bfloat16
F32 = jnp.float32
ANY = pl.BlockSpec(memory_space=pl.ANY)
HBM = pl.BlockSpec(memory_space=pltpu.HBM)
VMEM = pl.BlockSpec(memory_space=pltpu.VMEM)
LATE = 256


def contract_last(left, right):
    return lax.dot_general(left, right, (((1,), (1,)), ((), ())), preferred_element_type=F32)


def contract(left, right):
    return lax.dot_general(left, right, (((1,), (0,)), ((), ())), preferred_element_type=F32)


def gathered_form(tokens, weight):
    rows = lax.all_gather(weight, "dp", axis=1, tiled=True)
    toks = lax.all_gather(tokens, "tensor", axis=0, tiled=True)
    first = contract_last(toks, rows)
    part = contract(first.astype(BF), rows).astype(BF)
    second = lax.psum(part, "tensor")
    return (1.5 * first - 0.5 * contract_last(second, rows)).astype(BF)


def tiles(extent, step=256):
    return [slice(at, min(at + step, extent)) for at in range(0, extent, step)]


def call(body, ins, outs, flops, after=(), leave=False, scratch=()):
    flat, tree = jax.tree.flatten(ins)
    after = list(after)
    n_in, n_out = len(flat), len(outs)

    def kernel(*refs):
        given = jax.tree.unflatten(tree, refs[:n_in])
        rest = refs[n_in + len(after) :]
        body(given, rest[:n_out], *rest[n_out:])

    nbytes = sum(v.size * v.dtype.itemsize for v in flat)
    place = pltpu.HBM if leave else pltpu.VMEM
    flat = [pltpu.with_memory_space_constraint(v, place) for v in flat]
    return pl.pallas_call(
        kernel,
        out_shape=[pltpu.VMEM(*o) if isinstance(o, tuple) else o for o in outs],
        in_specs=[HBM if leave else VMEM] * n_in + [ANY] * len(after),
        out_specs=[VMEM] * n_out,
        scratch_shapes=[pltpu.SemaphoreType.DMA((n_out,))] if leave else list(scratch),
        compiler_params=pltpu.CompilerParams(vmem_limit_bytes=16 << 20),
        cost_estimate=pl.CostEstimate(flops=flops // 20, bytes_accessed=nbytes // 20, transcendentals=0),
    )(*flat, *after)


def bounds(pieces):
    ends = [0]
    for piece in pieces:
        ends.append(ends[-1] + piece.shape[0])
    return ends


def cuts(chunks):
    edges = sorted({e for pieces in chunks for e in bounds(pieces)})
    return [
        slice(a + t.start, a + t.stop) for a, b in zip(edges, edges[1:]) for t in tiles(b - a)
    ]


def at_rows(pieces, rows, cols=slice(None)):
    for ref, start in zip(pieces, bounds(pieces)):
        if start <= rows.start and rows.stop <= start + ref.shape[0]:
            return ref[rows.start - start : rows.stop - start, cols]


def add_dots(pairs, acc=None):
    for left, right in pairs:
        term = contract_last(left, right)
        acc = term if acc is None else acc + term
    return acc


def ring_form(n, tokens, weight):
    rows, width = weight.shape
    own = tokens.shape[0]
    count = 4 * own
    half = width // 2
    early = rows - LATE
    middle = early // 2
    steps = n // 2 - 1
    wide = 4 * LATE
    square = (count, width)
    offsets = [0] + [o for s in range(1, steps + 1) for o in (-s, s)] + [steps + 1]
    ring = list(range(0, n, 2)) + list(range(n - 1, 0, -2))

    def source(k):
        i = lax.axis_index("dp")
        place = jnp.where(lax.rem(i, 2) == 0, i // 2, n - 1 - i // 2)
        spot = lax.rem(place + offsets[k] + n, n)
        return jnp.where(spot < n // 2, 2 * spot, 2 * (n - 1 - spot) + 1)

    def side(mine):
        core = lax.rem(lax.axis_index("tensor"), 2)
        return core if mine else 1 - core

    def up(v):
        return lax.ppermute(v, "dp", [(ring[i], ring[(i + 1) % n]) for i in range(n)])

    def down(v):
        return lax.ppermute(v, "dp", [(ring[(i + 1) % n], ring[i]) for i in range(n)])

    def over_x(v):
        return lax.ppermute(v, "tensor", [(t, t ^ 2) for t in range(4)])

    def over_core(v):
        return lax.ppermute(v, "tensor", [(t, t ^ 1) for t in range(4)])

    def copy_from(row):
        def body(given, outs, sem):
            src = given[0].at[pl.ds(row, outs[0].shape[0]), :]
            copy = pltpu.make_async_copy(src, outs[0], sem.at[0])
            copy.start()
            copy.wait()

        return body

    def relay(given, outs):
        for ref, out in zip(given, outs):
            out[...] = ref[...]

    def relayed(arrays, after):
        return call(relay, arrays, [(a.shape, a.dtype) for a in arrays], 0, after)

    def split(given, outs):
        cut = outs[0].shape[0]
        outs[0][...] = given[0][:cut, :]
        outs[1][...] = given[1][cut:, :]

    def ends(u, d, after):
        h = u.shape[0] // 2
        return call(split, [u, d], [((h, width), BF), ((u.shape[0] - h, width), BF)], 0, after)

    def columns(k):
        return slice(k * width, (k + 1) * width)

    def halves(mine):
        return pl.ds(pl.multiple_of(side(mine) * half, half), half)

    def p_terms(tok, ks, chunks, acc_ref, put):
        for cut in cuts(chunks):
            pairs = [(tok[:, columns(k)], at_rows(c, cut)) for k, c in zip(ks, chunks)]
            put(cut, add_dots(pairs, None if acc_ref is None else acc_ref[:, cut]))

    def project(ks, acc, after=()):
        def body(given, outs):
            tok, chunks, acc_ref = given

            def put(cols, value):
                outs[0][:, cols] = value

            p_terms(tok, ks, chunks, acc_ref, put)

        outs = [((count, early), F32)]
        flops = 2 * count * early * width * len(ks)
        return call(body, (toks, [w[k] for k in ks], acc), outs, flops, after)[0]

    far = over_x(tokens)
    first = call(copy_from(0), [weight], [((early, width), BF)], 0, (), True)[0]
    u1, d1 = up(first), down(first)
    late = call(copy_from(early), [weight], [((LATE, width), BF)], 0, [u1, d1], True)[0]
    u2, d2 = up(u1), down(d1)
    u3, d3 = up(u2), down(d2)
    w = [[first], [u1], [d1], [u2], [d2], [u3], [d3]]

    def arrange(given, outs):
        core, x = side(True), lax.axis_index("tensor") // 2
        slots = [2 * x + core, 2 * (1 - x) + core, 2 * x + 1 - core, 2 * (1 - x) + 1 - core]
        for ref, slot in zip(given, slots):
            row = pl.multiple_of(slot * own, own)
            for k in range(n):
                src = pl.multiple_of(source(k) * width, width)
                outs[0][pl.ds(row, own), columns(k)] = ref[:, pl.ds(src, width)]

    toks = call(
        arrange,
        [tokens, far, over_core(tokens), over_core(far)],
        [((count, n * width), BF)],
        0,
    )[0]
    acc = project(list(range(n - 3)), None)
    late_far = over_x(late)
    a, b = ends(u3, d3, [acc, late_far])
    w.append([up(a), down(b)])
    acc = project([n - 3, n - 2], acc)

    def q_terms(p_ref, chunk, cols):
        total = None
        for ref, start in zip(chunk, bounds(chunk)):
            term = contract(p_ref[:, start : start + ref.shape[0]], ref[:, cols])
            total = term if total is None else total + term
        return total

    sizes = [5 * half // 2, 5 * half // 2, 2 * half, half]
    starts = [sum(sizes[:g]) for g in range(len(sizes))]

    def spots(g):
        found = []
        for k in range(n):
            lo = max(starts[g], k * half)
            hi = min(starts[g] + sizes[g], (k + 1) * half)
            if lo < hi:
                found.append((k, slice(lo - starts[g], hi - starts[g]), lo - k * half, hi - lo))
        return found

    def block_columns(mine, offset, size):
        return pl.ds(pl.multiple_of(side(mine) * half + offset, 128), size)

    def put_q(p_ref, g, chunks, mine, out):
        for (_, here, offset, size), chunk in zip(spots(g), chunks):
            q = q_terms(p_ref, chunk, block_columns(mine, offset, size))
            out[:, here] = q.astype(out.dtype)

    def part_of_w(g):
        return [w[k] for k, *_ in spots(g)]

    def first_give(given, outs):
        tok, last, acc_ref, chunks = given

        def put(cols, value):
            outs[0][:, cols] = value
            outs[1][:, cols] = value.astype(BF)

        p_terms(tok, [n - 1], [last], acc_ref, put)
        put_q(outs[1], 0, chunks, False, outs[2])

    def q_flops(g):
        return 2 * count * early * sizes[g]

    p, p_b, give = call(
        first_give,
        (toks, w[-1], acc, part_of_w(0)),
        [((count, early), F32), ((count, early), BF), ((count, sizes[0]), BF)],
        2 * q_flops(0),
    )

    def q_part(gs, mine, dtype, after=()):
        def body(given, outs):
            start = 0
            for at, (g, chunks) in enumerate(zip(gs, given[1])):
                out = outs[at] if mine else outs[0].at[:, start : start + sizes[g]]
                put_q(given[0], g, chunks, mine, out)
                start += sizes[g]

        outs = [((count, sizes[g]), dtype) for g in gs]
        if not mine:
            outs = [((count, sum(sizes[g] for g in gs)), dtype)]
        ins = (p_b, [part_of_w(g) for g in gs])
        return call(body, ins, outs, sum(q_flops(g) for g in gs), after)

    def add_two(given, outs):
        keep, got = given
        start = 0
        for at, a in enumerate(keep):
            q = a[...] + got[:, start : start + a.shape[1]].astype(F32)
            outs[2 * at][...] = q
            outs[2 * at + 1][...] = q.astype(BF)
            start += a.shape[1]

    def q_sum(keep, give):
        outs = [((count, k.shape[1]), dtype) for k in keep for dtype in (F32, BF)]
        return call(add_two, (keep, over_core(give)), outs, 0)

    keep = q_part([0], True, F32)
    give1 = q_part([1], False, BF, keep)[0]
    q0, q0_b = q_sum(keep, give)
    keep = q_part([1], True, F32, [q0_b])
    q1, q1_b = q_sum(keep, give1)
    keep = q_part([2, 3], True, F32, [q0_b])
    give = q_part([2, 3], False, BF, keep)[0]
    q2, q2_b, q3, q3_b = q_sum(keep, give)

    def late_part(ks, accs, final, after=(), more=None):
        def body(given, outs, *scratch):
            tok, lates, earlies, acc_refs, more = given
            p_out, g_out = scratch if final else outs

            def old(which, rows, cols):
                return None if accs is None else acc_refs[which][rows, cols]

            flat = [[m[0], m[1], o[0], o[1]] if len(m) == 2 else [m[0], o[0]] for m, o in lates]
            sets = [slice(j * LATE, (j + 1) * LATE) for j in range(4)]
            for cols in sets:
                pairs = [(tok[:, columns(k)], at_rows(f, cols)) for k, f in zip(ks, flat)]
                value = add_dots(pairs, old(0, slice(None), cols))
                p_out[:, cols] = value.astype(p_out.dtype)
                if final and cols.start == 0:
                    p_own = value
            for here in sets:
                for cols in cuts(earlies):
                    pairs = [(at_rows(f, here), at_rows(e, cols)) for f, e in zip(flat, earlies)]
                    g_out[here, cols] = add_dots(pairs, old(1, here, cols)).astype(g_out.dtype)
                cols = slice(early, rows)
                pairs = [(at_rows(f, here), at_rows(f, sets[0])) for f in flat]
                g_out[here, cols] = add_dots(pairs, old(1, here, cols)).astype(g_out.dtype)
            if final:
                p_ref, q_ref = more
                for cols in tiles(early) + [slice(early, rows)]:
                    p_val = p_ref[:, cols] if cols.start < early else p_own
                    term = q_ref[:, cols] + contract(p_out[...], g_out[:, cols])
                    outs[0][:, cols] = 1.5 * p_val - 0.5 * term

        if final:
            outs = [((count, rows), F32)]
            scratch = [pltpu.VMEM((count, wide), BF), pltpu.VMEM((wide, rows), BF)]
        else:
            outs = [((count, wide), F32), ((wide, rows), F32)]
            scratch = []
        flops = 2 * wide * (count + rows) * width * len(ks)
        ins = (toks, [v[k] for k in ks], [w[k] for k in ks], accs, more)
        return call(body, ins, outs, flops, after, False, scratch)

    def collect(g, sides, out, final, after=()):
        def body(given, outs):
            side_refs, chunks, base_ref = given
            for cols in cuts([e for e, _ in chunks]) + [slice(early, rows)]:
                term = None if out is None or final else base_ref[:, cols]
                for (_, here, offset, size), (early_rows, late_rows) in zip(spots(g), chunks):
                    for ref, mine in zip(side_refs, (True, False)):
                        left = ref[:, here]
                        block_cols = block_columns(mine, offset, size)
                        if cols.start < early:
                            right = at_rows(early_rows, cols, block_cols)
                        else:
                            right = late_rows[0][0][:LATE, block_cols]
                        term = add_dots([(left, right)], term)
                if final:
                    term = base_ref[:, cols] - 0.5 * term
                outs[0][:, cols] = term.astype(outs[0].dtype)

        outs = [jax.ShapeDtypeStruct((count, rows), BF) if final else ((count, rows), F32)]
        ins = (sides, [(w[k], v[k]) for k, *_ in spots(g)], out)
        return call(body, ins, outs, 4 * count * rows * sizes[g], after)[0]

    def join(given, outs):
        outs[0][:LATE, :] = given[0][...]
        outs[0][LATE:, :] = given[1][...]

    def turn(given, outs):
        q_ref, far_ref, next_ref = given
        outs[0][...] = (q_ref[...] + far_ref[...].astype(F32)).astype(BF)
        if next_ref is not None:
            outs[1][...] = next_ref[...]

    def turned(q, far, next_q, after):
        outs = [(q.shape, BF)] + ([] if next_q is None else [(next_q.shape, BF)])
        return call(turn, (q, far, next_q), outs, 0, after)

    def step(given, outs):
        relay(given, outs[:2])
        if len(outs) > 2:
            split(given, outs[2:])

    def stepped(u, d, last, after):
        outs = [(u.shape, BF), (d.shape, BF)] + ([((LATE, width), BF)] * 2 if last else [])
        return call(step, [u, d], outs, 0, after)

    def both(pieces):
        return (pieces, [over_core(c) for c in pieces])

    tall = 2 * LATE
    block = call(join, [late, late_far], [((tall, width), BF)], 0, [p_b])[0]
    v = [both([block])]
    u, d = up(block), down(block)
    far = over_x(q0_b)
    sums = late_part([0], None, False, [q0_b])
    ru, rd = stepped(u, d, False, [sums[0]])
    v += [both([ru]), both([rd])]
    u, d = up(ru), down(rd)
    s0, nq = turned(q0, far, q1_b, [ru, q2_b])
    far = over_x(nq)
    sums = late_part([1, 2], sums, False, [s0])
    ru, rd = stepped(u, d, False, [sums[0]])
    v += [both([ru]), both([rd])]
    u, d = up(ru), down(rd)
    out = collect(0, [s0, over_core(s0)], None, False, [ru])
    s1, nq = turned(q1, far, q2_b, [out])
    far = over_x(nq)
    sums = late_part([3, 4], sums, False, [s1])
    ru, rd, a, b = stepped(u, d, True, [sums[0]])
    v += [both([ru]), both([rd])]
    a, b = up(a), down(b)
    out = collect(1, [s1, over_core(s1)], out, False, [ru])
    a, b = stepped(a, b, False, [out])
    v += [both([a, b])]
    s2, nq = turned(q2, far, q3_b, [a])
    far = over_x(nq)
    sums = late_part([5, 6], sums, False, [s2])
    out = collect(2, [s2, over_core(s2)], out, False, sums[:1])
    out = late_part([n - 1], sums, True, [], [p, out])[0]
    s3 = turned(q3, far, None, [out])[0]
    return collect(3, [s3, over_core(s3)], out, True)


def solution(mesh):
    n = mesh.shape["dp"]

    def on_device(tokens, weight):
        if mesh.shape["tensor"] == 4 and n == 8:
            return ring_form(n, tokens, weight)
        return gathered_form(tokens, weight)

    placed = (P(("dp", "tensor"), None), P("tensor", "dp"))
    return jax.shard_map(
        on_device, mesh=mesh, in_specs=placed, out_specs=P("dp", "tensor"), check_vma=False
    )
```

time: 151 us -> 140 us (0.927)
  Pallas kernels: 50.3 us -> 34.8 us
  waiting for transfers between devices: 67.8 us -> 74.4 us
  local copies, waits for them, and re-layouts: 2.26 us -> 0.01 us
    ppermute x8, waiting for transfers between devices: 5.05 us -> 40.8 us  [down(): lax.ppermute(v, 'dp', [(ring[(i + 1) % n], ring[i]) for i in range(n)])]
    ppermute x8, waiting for transfers between devices: 37 us -> 15.2 us  [up(): lax.ppermute(v, 'dp', [(ring[i], ring[(i + 1) % n]) for i in range(n)])]
    pallas_call x26 -> x33, Pallas kernels: 50.3 us -> 34.8 us  [call(): pl.pallas_call(kernel, out_shape=[pltpu.VMEM(*o) if isinstance(o, tuple)...]
    ppermute x6, waiting for transfers between devices: 23.7 us -> 17 us  [over_x(): return lax.ppermute(v, 'tensor', [(t, t ^ 2) for t in range(4)])]
    ppermute x8, starting transfers between devices: 3.78 us -> 9.5 us  [down(): lax.ppermute(v, 'dp', [(ring[(i + 1) % n], ring[i]) for i in range(n)])]
    ppermute x8, starting transfers between devices: 13.5 us -> 7.93 us  [up(): lax.ppermute(v, 'dp', [(ring[i], ring[(i + 1) % n]) for i in range(n)])]
    unnamed x8 -> x2, local copies, waits for them, and re-layouts: 2.18 us -> 0.01 us
    ppermute x17 -> x18, starting transfers between devices: 3.65 us -> 3.93 us  [over_core(): return lax.ppermute(v, 'tensor', [(t, t ^ 1) for t in range(4)])]
  transfers between devices with their start and end apart: 39 -> 40, of which waited for: 17 -> 19; matrix products, arithmetic and copies ran while one was open for 0% -> 0% of each run, Pallas kernels for 29% -> 22%
where the time goes in v3:
time: 140 us; the launch traced here: 139 us
  waiting for transfers between devices  74.4 us (53%)
  Pallas kernels  34.8 us (25%)
  starting transfers between devices  29.8 us (21%)
    ppermute x8, waiting for transfers between devices, down(): lax.ppermute(v, 'dp', [(ring[(i + 1) % n], ring[i]) for i in range(n)])  40.8 us
    pallas_call x33, Pallas kernels, call(): pl.pallas_call(kernel, out_shape=[pltpu.VMEM(*o) if isinstance(o, tuple)...  34.8 us
    ppermute x6, waiting for transfers between devices, over_x(): return lax.ppermute(v, 'tensor', [(t, t ^ 2) for t in range(4)])  17 us
    ppermute x8, waiting for transfers between devices, up(): lax.ppermute(v, 'dp', [(ring[i], ring[(i + 1) % n]) for i in range(n)])  15.2 us
    ppermute x8, starting transfers between devices, down(): lax.ppermute(v, 'dp', [(ring[(i + 1) % n], ring[i]) for i in range(n)])  9.5 us
    ppermute x6, starting transfers between devices, over_x(): return lax.ppermute(v, 'tensor', [(t, t ^ 2) for t in range(4)])  8.43 us
    ppermute x8, starting transfers between devices, up(): lax.ppermute(v, 'dp', [(ring[i], ring[(i + 1) % n]) for i in range(n)])  7.93 us
    ppermute x18, starting transfers between devices, over_core(): return lax.ppermute(v, 'tensor', [(t, t ^ 1) for t in range(4)])  3.93 us
  transfers between devices with their start and end apart: 40, of which 19 were waited for; matrix products, arithmetic and copies ran while one was open for 0% of the time, Pallas kernels for 22%

profile of v3, /device:TPU:0, one launch (start us, length us, event | category | flops | bytes accessed | tf_op | source)
XLA Modules:
  0.0 139.4 jit_solution(9559076502530663281)
XLA Ops:
  1.2 3.0 %collective-permute-start.6 = (bf16[768,512]{1,0:T(8,128)(2,1)S(1)}, bf16[768,512]{1,0:T(8,128)(2,1)S(1)}, u32[]{:S(2)}, u32[]{:S(2)}) collective-permute-start(bf16[768,512]{1,0:T(8,128)(2,1)S(1)} %shard_map.29.refs_1_.refs_4_.refs_3_.refs_2_), channel_id=1, source_target_pairs={{8,0},{16,8},{24,16},{28,24},{20,28},{12,20},{4,12},{0,4},{9,1},{1... | collective-permute-start | bytes 2359304 | tf_op jit(solution)/shard_map/ppermute | solution.py:115
  4.4 1.9 %collective-permute-start = (bf16[128,4096]{1,0:T(8,128)(2,1)}, bf16[128,4096]{1,0:T(8,128)(2,1)S(1)}, u32[]{:S(2)}, u32[]{:S(2)}) collective-permute-start(bf16[128,4096]{1,0:T(8,128)(2,1)} %refs_0_.3), channel_id=1, source_target_pairs={{0,2},{1,3},{2,0},{3,1},{4,6},{5,7},{6,4},{7,5},{8,10},{9,11},{10,... | collective-permute-start | bytes 3145736 | tf_op jit(solution)/shard_map/ppermute | solution.py:118
  6.3 15.6 %collective-permute-done.6.refs_3_.refs_2_.refs_6_.refs_1_.refs_8_ = bf16[768,512]{1,0:T(8,128)(2,1)S(1)} collective-permute-done((bf16[768,512]{1,0:T(8,128)(2,1)S(1)}, bf16[768,512]{1,0:T(8,128)(2,1)S(1)}, u32[]{:S(2)}, u32[]{:S(2)}) %collective-permute-start.6) | collective-permute-done | bytes 786464 | tf_op jit(solution)/shard_map/ppermute | solution.py:115
  21.9 1.7 %collective-permute-start.7 = (bf16[768,512]{1,0:T(8,128)(2,1)S(1)}, bf16[768,512]{1,0:T(8,128)(2,1)S(1)}, u32[]{:S(2)}, u32[]{:S(2)}) collective-permute-start(bf16[768,512]{1,0:T(8,128)(2,1)S(1)} %collective-permute-done.6.refs_3_.refs_2_.refs_6_.refs_1_.refs_8_), channel_id=1, source_target_pairs={{8,0},{16,8},{24,16},{28,24},{20,28},{12,20},{4,12},{0,4},{9,1},{1... | collective-permute-start | bytes 2359304 | tf_op jit(solution)/shard_map/ppermute | solution.py:115
  23.9 5.3 %collective-permute-done.refs_1_ = bf16[128,4096]{1,0:T(8,128)(2,1)S(1)} collective-permute-done((bf16[128,4096]{1,0:T(8,128)(2,1)}, bf16[128,4096]{1,0:T(8,128)(2,1)S(1)}, u32[]{:S(2)}, u32[]{:S(2)}) %collective-permute-start) | collective-permute-done | bytes 1048608 | tf_op jit(solution)/shard_map/ppermute | solution.py:118
  29.2 11.4 %collective-permute-done.7.refs_5_.refs_3_.refs_6_.refs_8_ = bf16[768,512]{1,0:T(8,128)(2,1)S(1)} collective-permute-done((bf16[768,512]{1,0:T(8,128)(2,1)S(1)}, bf16[768,512]{1,0:T(8,128)(2,1)S(1)}, u32[]{:S(2)}, u32[]{:S(2)}) %collective-permute-start.7) | collective-permute-done | bytes 786464 | tf_op jit(solution)/shard_map/ppermute | solution.py:115
  45.3 2.2 %shard_map.30.refs_2_.refs_3_ = f32[512,768]{1,0:T(8,128)S(1)} custom-call(bf16[512,4096]{1,0:T(8,128)(2,1)S(1)} %shard_map.28.refs_0_, bf16[768,512]{1,0:T(8,128)(2,1)S(1)} %shard_map.29.refs_1_.refs_4_.refs_3_.refs_2_, bf16[768,512]{1,0:T(8,128)(2,1)S(1)} %collective-permute-done.3.refs_2_.refs_1_.refs_5_, ...), custom_call_target="tpu_custom_call" | custom-call | flops 100663296 | bytes 406323 | tf_op jit(solution)/shard_map/pallas_call | solution.py:50
  47.6 2.5 %collective-permute-done.9.refs_3_.refs_1_ = bf16[256,512]{1,0:T(8,128)(2,1)S(1)} collective-permute-done((bf16[256,512]{1,0:T(8,128)(2,1)S(1)}, bf16[256,512]{1,0:T(8,128)(2,1)S(1)}, u32[]{:S(2)}, u32[]{:S(2)}) %collective-permute-start.9) | collective-permute-done | bytes 262176 | tf_op jit(solution)/shard_map/ppermute | solution.py:118
  50.0 8.4 %collective-permute-done.8.refs_1_.refs_2_.refs_6_.refs_5_ = bf16[768,512]{1,0:T(8,128)(2,1)S(1)} collective-permute-done((bf16[768,512]{1,0:T(8,128)(2,1)S(1)}, bf16[768,512]{1,0:T(8,128)(2,1)S(1)}, u32[]{:S(2)}, u32[]{:S(2)}) %collective-permute-start.8) | collective-permute-done | bytes 786464 | tf_op jit(solution)/shard_map/ppermute | solution.py:115
  62.7 4.9 %collective-permute-done.10.refs_1_.refs_3_.refs_5_.refs_2_ = bf16[384,512]{1,0:T(8,128)(2,1)S(1)} collective-permute-done((bf16[384,512]{1,0:T(8,128)(2,1)S(1)}, bf16[384,512]{1,0:T(8,128)(2,1)S(1)}, u32[]{:S(2)}, u32[]{:S(2)}) %collective-permute-start.10) | collective-permute-done | bytes 393248 | tf_op jit(solution)/shard_map/ppermute | solution.py:112
  77.7 1.8 %shard_map.44 = (f32[512,1024]{1,0:T(8,128)S(1)}, f32[1024,1024]{1,0:T(8,128)S(1)}) custom-call(bf16[512,4096]{1,0:T(8,128)(2,1)S(1)} %shard_map.28.refs_0_, bf16[512,512]{1,0:T(8,128)(2,1)S(1)} %shard_map.43.refs_1_.refs_3_, bf16[512,512]{1,0:T(8,128)(2,1)S(1)} %collective-permute-done.18.refs_2_.refs_4_, ...), custom_call_target="tpu_custom_call" | custom-call | flops 80530640 | bytes 301465 | tf_op jit(solution)/shard_map/pallas_call | solution.py:50
  79.5 4.7 %collective-permute-done.16.refs_0_ = bf16[512,512]{1,0:T(8,128)(2,1)S(1)} collective-permute-done((bf16[512,512]{1,0:T(8,128)(2,1)S(1)}, bf16[512,512]{1,0:T(8,128)(2,1)S(1)}, u32[]{:S(2)}, u32[]{:S(2)}) %collective-permute-start.16) | collective-permute-done | bytes 524320 | tf_op jit(solution)/shard_map/ppermute | solution.py:112
  89.1 4.1 %collective-permute-done.15.refs_1_ = bf16[512,640]{1,0:T(8,128)(2,1)S(1)} collective-permute-done((bf16[512,640]{1,0:T(8,128)(2,1)S(1)}, bf16[512,640]{1,0:T(8,128)(2,1)S(1)}, u32[]{:S(2)}, u32[]{:S(2)}) %collective-permute-start.15) | collective-permute-done | bytes 655392 | tf_op jit(solution)/shard_map/ppermute | solution.py:118
  94.7 3.4 %shard_map.47 = (f32[512,1024]{1,0:T(8,128)S(1)}, f32[1024,1024]{1,0:T(8,128)S(1)}) custom-call(bf16[512,4096]{1,0:T(8,128)(2,1)S(1)} %shard_map.28.refs_0_, bf16[512,512]{1,0:T(8,128)(2,1)S(1)} %get-tuple-element.57.refs_3_.refs_1_.refs_6_, bf16[512,512]{1,0:T(8,128)(2,1)S(1)} %collective-permute-done.21.refs_2_.refs_7_, ...), custom_call_target="tpu_custom_call" | custom-call | flops 161061280 | bytes 707788 | tf_op jit(solution)/shard_map/pallas_call | solution.py:50
  101.7 1.6 %collective-permute-start.26 = (bf16[512,512]{1,0:T(8,128)(2,1)S(1)}, bf16[512,512]{1,0:T(8,128)(2,1)S(1)}, u32[]{:S(2)}, u32[]{:S(2)}) collective-permute-start(bf16[512,512]{1,0:T(8,128)(2,1)S(1)} %get-tuple-element.64.refs_11_.refs_1_.refs_6_), channel_id=1, source_target_pairs={{0,8},{8,16},{16,24},{24,28},{28,20},{20,12},{12,4},{4,0},{1,9},{9... | collective-permute-start | bytes 1572872 | tf_op jit(solution)/shard_map/ppermute | solution.py:112
  103.8 1.8 %shard_map.49.refs_3_.refs_11_ = f32[512,1024]{1,0:T(8,128)S(1)} custom-call(bf16[512,640]{1,0:T(8,128)(2,1)S(1)} %get-tuple-element.60.refs_9_.refs_0_, bf16[512,640]{1,0:T(8,128)(2,1)S(1)} %collective-permute-done.20.refs_1_, bf16[768,512]{1,0:T(8,128)(2,1)S(1)} %shard_map.29.refs_1_.refs_4_.refs_3_.refs_2_, ...), custom_call_target="tpu_custom_call" | custom-call | flops 67108864 | bytes 340787 | tf_op jit(solution)/shard_map/pallas_call | solution.py:50
  105.6 5.0 %collective-permute-done.19.refs_1_ = bf16[512,640]{1,0:T(8,128)(2,1)S(1)} collective-permute-done((bf16[512,640]{1,0:T(8,128)(2,1)S(1)}, bf16[512,640]{1,0:T(8,128)(2,1)S(1)}, u32[]{:S(2)}, u32[]{:S(2)}) %collective-permute-start.19) | collective-permute-done | bytes 655392 | tf_op jit(solution)/shard_map/ppermute | solution.py:118
  112.1 3.5 %shard_map.51 = (f32[512,1024]{1,0:T(8,128)S(1)}, f32[1024,1024]{1,0:T(8,128)S(1)}) custom-call(bf16[512,4096]{1,0:T(8,128)(2,1)S(1)} %shard_map.28.refs_0_, bf16[512,512]{1,0:T(8,128)(2,1)S(1)} %get-tuple-element.64.refs_11_.refs_1_.refs_6_, bf16[512,512]{1,0:T(8,128)(2,1)S(1)} %collective-permute-done.28.refs_2_.refs_7_, ...), custom_call_target="tpu_custom_call" | custom-call | flops 161061280 | bytes 707788 | tf_op jit(solution)/shard_map/pallas_call | solution.py:50
  117.1 1.6 %collective-permute-start.30 = (bf16[256,512]{1,0:T(8,128)(2,1)S(1)}, bf16[256,512]{1,0:T(8,128)(2,1)S(1)}, u32[]{:S(2)}, u32[]{:S(2)}) collective-permute-start(bf16[256,512]{1,0:T(8,128)(2,1)S(1)} %get-tuple-element.71), channel_id=1, source_target_pairs={{0,8},{8,16},{16,24},{24,28},{28,20},{20,12},{12,4},{4,0},{1,9},{9... | collective-permute-start | bytes 786440 | tf_op jit(solution)/shard_map/ppermute | solution.py:112
  119.7 1.8 %shard_map.53.refs_2_.refs_8_ = f32[512,1024]{1,0:T(8,128)S(1)} custom-call(bf16[512,640]{1,0:T(8,128)(2,1)S(1)} %get-tuple-element.69.refs_9_.refs_0_, bf16[512,640]{1,0:T(8,128)(2,1)S(1)} %collective-permute-done.32.refs_1_, bf16[768,512]{1,0:T(8,128)(2,1)S(1)} %collective-permute-done.6.refs_3_.refs_2_.refs_6_.refs_1_.refs_8_, ...), custom_call_target="tpu_custom_call" | custom-call | flops 67108864 | bytes 445644 | tf_op jit(solution)/shard_map/pallas_call | solution.py:50
  121.5 2.8 %collective-permute-done.30.refs_0_ = bf16[256,512]{1,0:T(8,128)(2,1)S(1)} collective-permute-done((bf16[256,512]{1,0:T(8,128)(2,1)S(1)}, bf16[256,512]{1,0:T(8,128)(2,1)S(1)}, u32[]{:S(2)}, u32[]{:S(2)}) %collective-permute-start.30) | collective-permute-done | bytes 262176 | tf_op jit(solution)/shard_map/ppermute | solution.py:112
  127.9 3.4 %shard_map.56 = (f32[512,1024]{1,0:T(8,128)S(1)}, f32[1024,1024]{1,0:T(8,128)S(1)}) custom-call(bf16[512,4096]{1,0:T(8,128)(2,1)S(1)} %shard_map.28.refs_0_, bf16[512,512]{1,0:T(8,128)(2,1)S(1)} %get-tuple-element.73.refs_12_.refs_1_.refs_3_, bf16[512,512]{1,0:T(8,128)(2,1)S(1)} %collective-permute-done.36.refs_2_.refs_4_, ...), custom_call_target="tpu_custom_call" | custom-call | flops 161061280 | bytes 707788 | tf_op jit(solution)/shard_map/pallas_call | solution.py:50
  132.7 3.2 %shard_map.58.refs_2_.refs_8_ = f32[512,1024]{1,0:T(8,128)S(1)} custom-call(bf16[512,4096]{1,0:T(8,128)(2,1)S(1)} %shard_map.28.refs_0_, bf16[256,512]{1,0:T(8,128)(2,1)S(1)} %get-tuple-element.74.refs_3_.refs_1_.refs_4_, bf16[256,512]{1,0:T(8,128)(2,1)S(1)} %get-tuple-element.76.refs_2_.refs_5_, ...), custom_call_target="tpu_custom_call" | custom-call | flops 80530640 | bytes 799539 | tf_op jit(solution)/shard_map/pallas_call | solution.py:50
  137.6 1.8 %shard_map.60 = bf16[512,1024]{1,0:T(8,128)(2,1)} custom-call(bf16[512,256]{1,0:T(8,128)(2,1)S(1)} %shard_map.59.refs_0_, bf16[512,256]{1,0:T(8,128)(2,1)S(1)} %collective-permute-done.39.refs_1_, bf16[384,512]{1,0:T(8,128)(2,1)S(1)} %collective-permute-done.10.refs_1_.refs_3_.refs_5_.refs_2_, ...), custom_call_target="tpu_custom_call" | custom-call | flops 26843544 | bytes 222822 | tf_op jit(solution)/shard_map/pallas_call | solution.py:50
  (91 shorter events, 41.5 us)
Async XLA Ops:
  1.2 20.6 %collective-permute-start.6 = (bf16[768,512]{1,0:T(8,128)(2,1)S(1)}, bf16[768,512]{1,0:T(8,128)(2,1)S(1)}, u32[]{:S(2)}, u32[]{:S(2)}) collective-permute-start(bf16[768,512]{1,0:T(8,128)(2,1)S(1)} %shard_map.29.refs_1_.refs_4_.refs_3_.refs_2_), channel_id=1, source_target_pairs={{8,0},{16,8},{24,16},{28,24},{20,28},{12,20},{4,12},{0,4},{9,1},{1... | collective-permute-start | bytes 2359304 | tf_op jit(solution)/shard_map/ppermute | solution.py:115
  4.3 19.3 %collective-permute-start.3 = (bf16[768,512]{1,0:T(8,128)(2,1)S(1)}, bf16[768,512]{1,0:T(8,128)(2,1)S(1)}, u32[]{:S(2)}, u32[]{:S(2)}) collective-permute-start(bf16[768,512]{1,0:T(8,128)(2,1)S(1)} %shard_map.29.refs_1_.refs_4_.refs_3_.refs_2_), channel_id=1, source_target_pairs={{0,8},{8,16},{16,24},{24,28},{28,20},{20,12},{12,4},{4,0},{1,9},{9... | collective-permute-start | bytes 2359304 | tf_op jit(solution)/shard_map/ppermute | solution.py:112
  4.4 24.8 %collective-permute-start = (bf16[128,4096]{1,0:T(8,128)(2,1)}, bf16[128,4096]{1,0:T(8,128)(2,1)S(1)}, u32[]{:S(2)}, u32[]{:S(2)}) collective-permute-start(bf16[128,4096]{1,0:T(8,128)(2,1)} %refs_0_.3), channel_id=1, source_target_pairs={{0,2},{1,3},{2,0},{3,1},{4,6},{5,7},{6,4},{7,5},{8,10},{9,11},{10,... | collective-permute-start | bytes 3145736 | tf_op jit(solution)/shard_map/ppermute | solution.py:118
  21.9 18.7 %collective-permute-start.7 = (bf16[768,512]{1,0:T(8,128)(2,1)S(1)}, bf16[768,512]{1,0:T(8,128)(2,1)S(1)}, u32[]{:S(2)}, u32[]{:S(2)}) collective-permute-start(bf16[768,512]{1,0:T(8,128)(2,1)S(1)} %collective-permute-done.6.refs_3_.refs_2_.refs_6_.refs_1_.refs_8_), channel_id=1, source_target_pairs={{8,0},{16,8},{24,16},{28,24},{20,28},{12,20},{4,12},{0,4},{9,1},{1... | collective-permute-start | bytes 2359304 | tf_op jit(solution)/shard_map/ppermute | solution.py:115
  23.5 18.4 %collective-permute-start.4 = (bf16[768,512]{1,0:T(8,128)(2,1)S(1)}, bf16[768,512]{1,0:T(8,128)(2,1)S(1)}, u32[]{:S(2)}, u32[]{:S(2)}) collective-permute-start(bf16[768,512]{1,0:T(8,128)(2,1)S(1)} %collective-permute-done.3.refs_2_.refs_1_.refs_5_), channel_id=1, source_target_pairs={{0,8},{8,16},{16,24},{24,28},{28,20},{20,12},{12,4},{4,0},{1,9},{9... | collective-permute-start | bytes 2359304 | tf_op jit(solution)/shard_map/ppermute | solution.py:112
  23.9 21.1 %collective-permute-start.1 = (bf16[128,4096]{1,0:T(8,128)(2,1)}, bf16[128,4096]{1,0:T(8,128)(2,1)S(1)}, u32[]{:S(2)}, u32[]{:S(2)}) collective-permute-start(bf16[128,4096]{1,0:T(8,128)(2,1)} %refs_0_.3), channel_id=1, source_target_pairs={{0,1},{1,0},{2,3},{3,2},{4,5},{5,4},{6,7},{7,6},{8,9},{9,8},{10,11... | collective-permute-start | bytes 3145736 | tf_op jit(solution)/shard_map/ppermute | solution.py:121
  29.2 15.8 %collective-permute-start.2 = (bf16[128,4096]{1,0:T(8,128)(2,1)S(1)}, bf16[128,4096]{1,0:T(8,128)(2,1)S(1)}, u32[]{:S(2)}, u32[]{:S(2)}) collective-permute-start(bf16[128,4096]{1,0:T(8,128)(2,1)S(1)} %collective-permute-done.refs_1_), channel_id=1, source_target_pairs={{0,1},{1,0},{2,3},{3,2},{4,5},{5,4},{6,7},{7,6},{8,9},{9,8},{10,11... | collective-permute-start | bytes 3145736 | tf_op jit(solution)/shard_map/ppermute | solution.py:121
  40.6 17.8 %collective-permute-start.8 = (bf16[768,512]{1,0:T(8,128)(2,1)S(1)}, bf16[768,512]{1,0:T(8,128)(2,1)S(1)}, u32[]{:S(2)}, u32[]{:S(2)}) collective-permute-start(bf16[768,512]{1,0:T(8,128)(2,1)S(1)} %collective-permute-done.7.refs_5_.refs_3_.refs_6_.refs_8_), channel_id=1, source_target_pairs={{8,0},{16,8},{24,16},{28,24},{20,28},{12,20},{4,12},{0,4},{9,1},{1... | collective-permute-start | bytes 2359304 | tf_op jit(solution)/shard_map/ppermute | solution.py:115
  42.0 17.6 %collective-permute-start.5 = (bf16[768,512]{1,0:T(8,128)(2,1)S(1)}, bf16[768,512]{1,0:T(8,128)(2,1)S(1)}, u32[]{:S(2)}, u32[]{:S(2)}) collective-permute-start(bf16[768,512]{1,0:T(8,128)(2,1)S(1)} %collective-permute-done.4.refs_4_.refs_2_.refs_5_), channel_id=1, source_target_pairs={{0,8},{8,16},{16,24},{24,28},{28,20},{20,12},{12,4},{4,0},{1,9},{9... | collective-permute-start | bytes 2359304 | tf_op jit(solution)/shard_map/ppermute | solution.py:112
  70.4 13.9 %collective-permute-start.16 = (bf16[512,512]{1,0:T(8,128)(2,1)S(1)}, bf16[512,512]{1,0:T(8,128)(2,1)S(1)}, u32[]{:S(2)}, u32[]{:S(2)}) collective-permute-start(bf16[512,512]{1,0:T(8,128)(2,1)S(1)} %shard_map.43.refs_1_.refs_3_), channel_id=1, source_target_pairs={{0,8},{8,16},{16,24},{24,28},{28,20},{20,12},{12,4},{4,0},{1,9},{9... | collective-permute-start | bytes 1572872 | tf_op jit(solution)/shard_map/ppermute | solution.py:112
  71.6 13.6 %collective-permute-start.17 = (bf16[512,512]{1,0:T(8,128)(2,1)S(1)}, bf16[512,512]{1,0:T(8,128)(2,1)S(1)}, u32[]{:S(2)}, u32[]{:S(2)}) collective-permute-start(bf16[512,512]{1,0:T(8,128)(2,1)S(1)} %shard_map.43.refs_1_.refs_3_), channel_id=1, source_target_pairs={{8,0},{16,8},{24,16},{28,24},{20,28},{12,20},{4,12},{0,4},{9,1},{1... | collective-permute-start | bytes 1572872 | tf_op jit(solution)/shard_map/ppermute | solution.py:115
  75.1 12.4 %collective-permute-start.13 = (bf16[512,768]{1,0:T(8,128)(2,1)S(1)}, bf16[512,768]{1,0:T(8,128)(2,1)S(1)}, u32[]{:S(2)}, u32[]{:S(2)}) collective-permute-start(bf16[512,768]{1,0:T(8,128)(2,1)S(1)} %shard_map.38), channel_id=1, source_target_pairs={{0,1},{1,0},{2,3},{3,2},{4,5},{5,4},{6,7},{7,6},{8,9},{9,8},{10,11... | collective-permute-start | bytes 2359304 | tf_op jit(solution)/shard_map/ppermute | solution.py:121
  76.0 9.9 %collective-permute-start.14 = (bf16[512,640]{1,0:T(8,128)(2,1)S(1)}, bf16[512,640]{1,0:T(8,128)(2,1)S(1)}, u32[]{:S(2)}, u32[]{:S(2)}) collective-permute-start(bf16[512,640]{1,0:T(8,128)(2,1)S(1)} %shard_map.41), channel_id=1, source_target_pairs={{0,1},{1,0},{2,3},{3,2},{4,5},{5,4},{6,7},{7,6},{8,9},{9,8},{10,11... | collective-permute-start | bytes 1966088 | tf_op jit(solution)/shard_map/ppermute | solution.py:121
  76.5 16.7 %collective-permute-start.15 = (bf16[512,640]{1,0:T(8,128)(2,1)S(1)}, bf16[512,640]{1,0:T(8,128)(2,1)S(1)}, u32[]{:S(2)}, u32[]{:S(2)}) collective-permute-start(bf16[512,640]{1,0:T(8,128)(2,1)S(1)} %get-tuple-element.48.refs_5_.refs_4_), channel_id=1, source_target_pairs={{0,2},{1,3},{2,0},{3,1},{4,6},{5,7},{6,4},{7,5},{8,10},{9,11},{10,... | collective-permute-start | bytes 1966088 | tf_op jit(solution)/shard_map/ppermute | solution.py:118
  85.9 13.9 %collective-permute-start.23 = (bf16[512,512]{1,0:T(8,128)(2,1)S(1)}, bf16[512,512]{1,0:T(8,128)(2,1)S(1)}, u32[]{:S(2)}, u32[]{:S(2)}) collective-permute-start(bf16[512,512]{1,0:T(8,128)(2,1)S(1)} %get-tuple-element.57.refs_3_.refs_1_.refs_6_), channel_id=1, source_target_pairs={{0,8},{8,16},{16,24},{24,28},{28,20},{20,12},{12,4},{4,0},{1,9},{9... | collective-permute-start | bytes 1572872 | tf_op jit(solution)/shard_map/ppermute | solution.py:112
  87.5 13.6 %collective-permute-start.24 = (bf16[512,512]{1,0:T(8,128)(2,1)S(1)}, bf16[512,512]{1,0:T(8,128)(2,1)S(1)}, u32[]{:S(2)}, u32[]{:S(2)}) collective-permute-start(bf16[512,512]{1,0:T(8,128)(2,1)S(1)} %get-tuple-element.61.refs_3_.refs_9_), channel_id=1, source_target_pairs={{8,0},{16,8},{24,16},{28,24},{20,28},{12,20},{4,12},{0,4},{9,1},{1... | collective-permute-start | bytes 1572872 | tf_op jit(solution)/shard_map/ppermute | solution.py:115
  93.4 10.0 %collective-permute-start.20 = (bf16[512,640]{1,0:T(8,128)(2,1)S(1)}, bf16[512,640]{1,0:T(8,128)(2,1)S(1)}, u32[]{:S(2)}, u32[]{:S(2)}) collective-permute-start(bf16[512,640]{1,0:T(8,128)(2,1)S(1)} %get-tuple-element.60.refs_9_.refs_0_), channel_id=1, source_target_pairs={{0,1},{1,0},{2,3},{3,2},{4,5},{5,4},{6,7},{7,6},{8,9},{9,8},{10,11... | collective-permute-start | bytes 1966088 | tf_op jit(solution)/shard_map/ppermute | solution.py:121
  93.5 17.1 %collective-permute-start.19 = (bf16[512,640]{1,0:T(8,128)(2,1)S(1)}, bf16[512,640]{1,0:T(8,128)(2,1)S(1)}, u32[]{:S(2)}, u32[]{:S(2)}) collective-permute-start(bf16[512,640]{1,0:T(8,128)(2,1)S(1)} %get-tuple-element.59), channel_id=1, source_target_pairs={{0,2},{1,3},{2,0},{3,1},{4,6},{5,7},{6,4},{7,5},{8,10},{9,11},{10,... | collective-permute-start | bytes 1966088 | tf_op jit(solution)/shard_map/ppermute | solution.py:118
  101.2 9.7 %collective-permute-start.28 = (bf16[512,512]{1,0:T(8,128)(2,1)S(1)}, bf16[512,512]{1,0:T(8,128)(2,1)S(1)}, u32[]{:S(2)}, u32[]{:S(2)}) collective-permute-start(bf16[512,512]{1,0:T(8,128)(2,1)S(1)} %get-tuple-element.64.refs_11_.refs_1_.refs_6_), channel_id=1, source_target_pairs={{0,1},{1,0},{2,3},{3,2},{4,5},{5,4},{6,7},{7,6},{8,9},{9,8},{10,11... | collective-permute-start | bytes 1572872 | tf_op jit(solution)/shard_map/ppermute | solution.py:121
  101.2 10.9 %collective-permute-start.29 = (bf16[512,512]{1,0:T(8,128)(2,1)S(1)}, bf16[512,512]{1,0:T(8,128)(2,1)S(1)}, u32[]{:S(2)}, u32[]{:S(2)}) collective-permute-start(bf16[512,512]{1,0:T(8,128)(2,1)S(1)} %get-tuple-element.67.refs_3_.refs_9_), channel_id=1, source_target_pairs={{0,1},{1,0},{2,3},{3,2},{4,5},{5,4},{6,7},{7,6},{8,9},{9,8},{10,11... | collective-permute-start | bytes 1572872 | tf_op jit(solution)/shard_map/ppermute | solution.py:121
  101.7 13.9 %collective-permute-start.26 = (bf16[512,512]{1,0:T(8,128)(2,1)S(1)}, bf16[512,512]{1,0:T(8,128)(2,1)S(1)}, u32[]{:S(2)}, u32[]{:S(2)}) collective-permute-start(bf16[512,512]{1,0:T(8,128)(2,1)S(1)} %get-tuple-element.64.refs_11_.refs_1_.refs_6_), channel_id=1, source_target_pairs={{0,8},{8,16},{16,24},{24,28},{28,20},{20,12},{12,4},{4,0},{1,9},{9... | collective-permute-start | bytes 1572872 | tf_op jit(solution)/shard_map/ppermute | solution.py:112
  103.4 13.6 %collective-permute-start.27 = (bf16[512,512]{1,0:T(8,128)(2,1)S(1)}, bf16[512,512]{1,0:T(8,128)(2,1)S(1)}, u32[]{:S(2)}, u32[]{:S(2)}) collective-permute-start(bf16[512,512]{1,0:T(8,128)(2,1)S(1)} %get-tuple-element.67.refs_3_.refs_9_), channel_id=1, source_target_pairs={{8,0},{16,8},{24,16},{28,24},{20,28},{12,20},{4,12},{0,4},{9,1},{1... | collective-permute-start | bytes 1572872 | tf_op jit(solution)/shard_map/ppermute | solution.py:115
  110.9 14.8 %collective-permute-start.25 = (bf16[512,512]{1,0:T(8,128)(2,1)S(1)}, bf16[512,512]{1,0:T(8,128)(2,1)S(1)}, u32[]{:S(2)}, u32[]{:S(2)}) collective-permute-start(bf16[512,512]{1,0:T(8,128)(2,1)S(1)} %get-tuple-element.65), channel_id=1, source_target_pairs={{0,2},{1,3},{2,0},{3,1},{4,6},{5,7},{6,4},{7,5},{8,10},{9,11},{10,... | collective-permute-start | bytes 1572872 | tf_op jit(solution)/shard_map/ppermute | solution.py:118
  126.4 9.5 %collective-permute-start.33 = (bf16[512,256]{1,0:T(8,128)(2,1)S(1)}, bf16[512,256]{1,0:T(8,128)(2,1)S(1)}, u32[]{:S(2)}, u32[]{:S(2)}) collective-permute-start(bf16[512,256]{1,0:T(8,128)(2,1)S(1)} %get-tuple-element.75), channel_id=1, source_target_pairs={{0,2},{1,3},{2,0},{3,1},{4,6},{5,7},{6,4},{7,5},{8,10},{9,11},{10,... | collective-permute-start | bytes 786440 | tf_op jit(solution)/shard_map/ppermute | solution.py:118
  (17 other events, 153.8 us)

commit v4 on v3

--- a/solution.py
+++ b/solution.py
@@ -205,7 +205,7 @@
             total = term if total is None else total + term
         return total
 
-    sizes = [5 * half // 2, 5 * half // 2, 2 * half, half]
+    sizes = [u * half // 2 for u in (4,5,5,2)]
     starts = [sum(sizes[:g]) for g in range(len(sizes))]
 
     def spots(g):
@@ -378,23 +378,23 @@
     u, d = up(block), down(block)
     far = over_x(q0_b)
     sums = late_part([0], None, False, [q0_b])
-    ru, rd = stepped(u, d, False, [sums[0]])
+    ru, rd = stepped(u, d, False, [sums[0], give])
     v += [both([ru]), both([rd])]
     u, d = up(ru), down(rd)
     s0, nq = turned(q0, far, q1_b, [ru, q2_b])
     far = over_x(nq)
-    sums = late_part([1, 2], sums, False, [s0])
-    ru, rd = stepped(u, d, False, [sums[0]])
+    ru, rd = stepped(u, d, False, [s0])
     v += [both([ru]), both([rd])]
     u, d = up(ru), down(rd)
-    out = collect(0, [s0, over_core(s0)], None, False, [ru])
+    sums = late_part([1, 2], sums, False, [ru])
+    out = collect(0, [s0, over_core(s0)], None, False, sums[:1])
     s1, nq = turned(q1, far, q2_b, [out])
     far = over_x(nq)
-    sums = late_part([3, 4], sums, False, [s1])
-    ru, rd, a, b = stepped(u, d, True, [sums[0]])
+    ru, rd, a, b = stepped(u, d, True, [s1])
     v += [both([ru]), both([rd])]
     a, b = up(a), down(b)
-    out = collect(1, [s1, over_core(s1)], out, False, [ru])
+    sums = late_part([3, 4], sums, False, [ru])
+    out = collect(1, [s1, over_core(s1)], out, False, sums[:1])
     a, b = stepped(a, b, False, [out])
     v += [both([a, b])]
     s2, nq = turned(q2, far, q3_b, [a])

time: 140 us -> 139 us (level)
    ppermute x6, waiting for transfers between devices: 17 us -> 11.4 us  [over_x(): return lax.ppermute(v, 'tensor', [(t, t ^ 2) for t in range(4)])]
    ppermute x8, waiting for transfers between devices: 15.2 us -> 20.3 us  [up(): lax.ppermute(v, 'dp', [(ring[i], ring[(i + 1) % n]) for i in range(n)])]
  transfers between devices with their start and end apart: 40 -> 40, of which waited for: 19 -> 21; matrix products, arithmetic and copies ran while one was open for 0% -> 0% of each run, Pallas kernels for 22% -> 22%
where the time goes in v4:
time: 139 us
  waiting for transfers between devices  74.5 us (54%)
  Pallas kernels  34.7 us (25%)
  starting transfers between devices  29.2 us (21%)
    ppermute x8, waiting for transfers between devices, down(): lax.ppermute(v, 'dp', [(ring[(i + 1) % n], ring[i]) for i in range(n)])  40.8 us
    pallas_call x33, Pallas kernels, call(): pl.pallas_call(kernel, out_shape=[pltpu.VMEM(*o) if isinstance(o, tuple)...  34.7 us
    ppermute x8, waiting for transfers between devices, up(): lax.ppermute(v, 'dp', [(ring[i], ring[(i + 1) % n]) for i in range(n)])  20.3 us
    ppermute x6, waiting for transfers between devices, over_x(): return lax.ppermute(v, 'tensor', [(t, t ^ 2) for t in range(4)])  11.4 us
    ppermute x8, starting transfers between devices, down(): lax.ppermute(v, 'dp', [(ring[(i + 1) % n], ring[i]) for i in range(n)])  9.42 us
    ppermute x6, starting transfers between devices, over_x(): return lax.ppermute(v, 'tensor', [(t, t ^ 2) for t in range(4)])  8.41 us
    ppermute x8, starting transfers between devices, up(): lax.ppermute(v, 'dp', [(ring[i], ring[(i + 1) % n]) for i in range(n)])  8.11 us
    ppermute x18, starting transfers between devices, over_core(): return lax.ppermute(v, 'tensor', [(t, t ^ 1) for t in range(4)])  3.26 us
  transfers between devices with their start and end apart: 40, of which 21 were waited for; matrix products, arithmetic and copies ran while one was open for 0% of the time, Pallas kernels for 22%

profile of v4, /device:TPU:0, one launch (start us, length us, event | category | flops | bytes accessed | tf_op | source)
XLA Modules:
  0.0 138.7 jit_solution(11979158158054650688)
XLA Ops:
  1.2 3.0 %collective-permute-start.6 = (bf16[768,512]{1,0:T(8,128)(2,1)S(1)}, bf16[768,512]{1,0:T(8,128)(2,1)S(1)}, u32[]{:S(2)}, u32[]{:S(2)}) collective-permute-start(bf16[768,512]{1,0:T(8,128)(2,1)S(1)} %shard_map.29.refs_1_.refs_4_.refs_3_.refs_2_), channel_id=1, source_target_pairs={{8,0},{16,8},{24,16},{28,24},{20,28},{12,20},{4,12},{0,4},{9,1},{1... | collective-permute-start | bytes 2359304 | tf_op jit(solution)/shard_map/ppermute | solution.py:115
  4.4 1.9 %collective-permute-start = (bf16[128,4096]{1,0:T(8,128)(2,1)}, bf16[128,4096]{1,0:T(8,128)(2,1)S(1)}, u32[]{:S(2)}, u32[]{:S(2)}) collective-permute-start(bf16[128,4096]{1,0:T(8,128)(2,1)} %refs_0_.3), channel_id=1, source_target_pairs={{0,2},{1,3},{2,0},{3,1},{4,6},{5,7},{6,4},{7,5},{8,10},{9,11},{10,... | collective-permute-start | bytes 3145736 | tf_op jit(solution)/shard_map/ppermute | solution.py:118
  6.3 15.6 %collective-permute-done.6.refs_3_.refs_2_.refs_1_.refs_6_ = bf16[768,512]{1,0:T(8,128)(2,1)S(1)} collective-permute-done((bf16[768,512]{1,0:T(8,128)(2,1)S(1)}, bf16[768,512]{1,0:T(8,128)(2,1)S(1)}, u32[]{:S(2)}, u32[]{:S(2)}) %collective-permute-start.6) | collective-permute-done | bytes 786464 | tf_op jit(solution)/shard_map/ppermute | solution.py:115
  21.9 1.7 %collective-permute-start.7 = (bf16[768,512]{1,0:T(8,128)(2,1)S(1)}, bf16[768,512]{1,0:T(8,128)(2,1)S(1)}, u32[]{:S(2)}, u32[]{:S(2)}) collective-permute-start(bf16[768,512]{1,0:T(8,128)(2,1)S(1)} %collective-permute-done.6.refs_3_.refs_2_.refs_1_.refs_6_), channel_id=1, source_target_pairs={{8,0},{16,8},{24,16},{28,24},{20,28},{12,20},{4,12},{0,4},{9,1},{1... | collective-permute-start | bytes 2359304 | tf_op jit(solution)/shard_map/ppermute | solution.py:115
  23.9 5.3 %collective-permute-done.refs_1_ = bf16[128,4096]{1,0:T(8,128)(2,1)S(1)} collective-permute-done((bf16[128,4096]{1,0:T(8,128)(2,1)}, bf16[128,4096]{1,0:T(8,128)(2,1)S(1)}, u32[]{:S(2)}, u32[]{:S(2)}) %collective-permute-start) | collective-permute-done | bytes 1048608 | tf_op jit(solution)/shard_map/ppermute | solution.py:118
  29.2 11.4 %collective-permute-done.7.refs_5_.refs_1_.refs_3_.refs_6_.refs_8_.refs_2_ = bf16[768,512]{1,0:T(8,128)(2,1)S(1)} collective-permute-done((bf16[768,512]{1,0:T(8,128)(2,1)S(1)}, bf16[768,512]{1,0:T(8,128)(2,1)S(1)}, u32[]{:S(2)}, u32[]{:S(2)}) %collective-permute-start.7) | collective-permute-done | bytes 786464 | tf_op jit(solution)/shard_map/ppermute | solution.py:115
  45.3 2.2 %shard_map.30.refs_2_.refs_3_ = f32[512,768]{1,0:T(8,128)S(1)} custom-call(bf16[512,4096]{1,0:T(8,128)(2,1)S(1)} %shard_map.28.refs_0_, bf16[768,512]{1,0:T(8,128)(2,1)S(1)} %shard_map.29.refs_1_.refs_4_.refs_3_.refs_2_, bf16[768,512]{1,0:T(8,128)(2,1)S(1)} %collective-permute-done.3.refs_2_.refs_1_.refs_5_, ...), custom_call_target="tpu_custom_call" | custom-call | flops 100663296 | bytes 406323 | tf_op jit(solution)/shard_map/pallas_call | solution.py:50
  47.6 2.5 %collective-permute-done.9.refs_3_.refs_1_ = bf16[256,512]{1,0:T(8,128)(2,1)S(1)} collective-permute-done((bf16[256,512]{1,0:T(8,128)(2,1)S(1)}, bf16[256,512]{1,0:T(8,128)(2,1)S(1)}, u32[]{:S(2)}, u32[]{:S(2)}) %collective-permute-start.9) | collective-permute-done | bytes 262176 | tf_op jit(solution)/shard_map/ppermute | solution.py:118
  50.0 8.4 %collective-permute-done.8.refs_1_.refs_2_.refs_3_.refs_6_.refs_8_ = bf16[768,512]{1,0:T(8,128)(2,1)S(1)} collective-permute-done((bf16[768,512]{1,0:T(8,128)(2,1)S(1)}, bf16[768,512]{1,0:T(8,128)(2,1)S(1)}, u32[]{:S(2)}, u32[]{:S(2)}) %collective-permute-start.8) | collective-permute-done | bytes 786464 | tf_op jit(solution)/shard_map/ppermute | solution.py:115
  62.7 4.9 %collective-permute-done.10.refs_1_.refs_4_.refs_5_.refs_2_ = bf16[384,512]{1,0:T(8,128)(2,1)S(1)} collective-permute-done((bf16[384,512]{1,0:T(8,128)(2,1)S(1)}, bf16[384,512]{1,0:T(8,128)(2,1)S(1)}, u32[]{:S(2)}, u32[]{:S(2)}) %collective-permute-start.10) | collective-permute-done | bytes 393248 | tf_op jit(solution)/shard_map/ppermute | solution.py:112
  77.5 1.8 %shard_map.44 = (f32[512,1024]{1,0:T(8,128)S(1)}, f32[1024,1024]{1,0:T(8,128)S(1)}) custom-call(bf16[512,4096]{1,0:T(8,128)(2,1)S(1)} %shard_map.28.refs_0_, bf16[512,512]{1,0:T(8,128)(2,1)S(1)} %shard_map.43.refs_1_.refs_3_, bf16[512,512]{1,0:T(8,128)(2,1)S(1)} %collective-permute-done.18.refs_2_.refs_4_, ...), custom_call_target="tpu_custom_call" | custom-call | flops 80530640 | bytes 301465 | tf_op jit(solution)/shard_map/pallas_call | solution.py:50
  79.3 4.6 %collective-permute-done.16.refs_0_ = bf16[512,512]{1,0:T(8,128)(2,1)S(1)} collective-permute-done((bf16[512,512]{1,0:T(8,128)(2,1)S(1)}, bf16[512,512]{1,0:T(8,128)(2,1)S(1)}, u32[]{:S(2)}, u32[]{:S(2)}) %collective-permute-start.16) | collective-permute-done | bytes 524320 | tf_op jit(solution)/shard_map/ppermute | solution.py:112
  88.2 2.0 %collective-permute-done.15.refs_1_ = bf16[512,512]{1,0:T(8,128)(2,1)S(1)} collective-permute-done((bf16[512,512]{1,0:T(8,128)(2,1)S(1)}, bf16[512,512]{1,0:T(8,128)(2,1)S(1)}, u32[]{:S(2)}, u32[]{:S(2)}) %collective-permute-start.15) | collective-permute-done | bytes 524320 | tf_op jit(solution)/shard_map/ppermute | solution.py:118
  92.1 5.6 %collective-permute-done.23.refs_0_ = bf16[512,512]{1,0:T(8,128)(2,1)S(1)} collective-permute-done((bf16[512,512]{1,0:T(8,128)(2,1)S(1)}, bf16[512,512]{1,0:T(8,128)(2,1)S(1)}, u32[]{:S(2)}, u32[]{:S(2)}) %collective-permute-start.23) | collective-permute-done | bytes 524320 | tf_op jit(solution)/shard_map/ppermute | solution.py:112
  99.1 1.7 %collective-permute-start.26 = (bf16[512,512]{1,0:T(8,128)(2,1)S(1)}, bf16[512,512]{1,0:T(8,128)(2,1)S(1)}, u32[]{:S(2)}, u32[]{:S(2)}) collective-permute-start(bf16[512,512]{1,0:T(8,128)(2,1)S(1)} %get-tuple-element.63.refs_9_.refs_1_.refs_6_), channel_id=1, source_target_pairs={{0,8},{8,16},{16,24},{24,28},{28,20},{20,12},{12,4},{4,0},{1,9},{9... | collective-permute-start | bytes 1572872 | tf_op jit(solution)/shard_map/ppermute | solution.py:112
  101.2 3.5 %shard_map.48 = (f32[512,1024]{1,0:T(8,128)S(1)}, f32[1024,1024]{1,0:T(8,128)S(1)}) custom-call(bf16[512,4096]{1,0:T(8,128)(2,1)S(1)} %shard_map.28.refs_0_, bf16[512,512]{1,0:T(8,128)(2,1)S(1)} %get-tuple-element.57.refs_3_.refs_1_.refs_6_, bf16[512,512]{1,0:T(8,128)(2,1)S(1)} %collective-permute-done.21.refs_2_.refs_7_, ...), custom_call_target="tpu_custom_call" | custom-call | flops 161061280 | bytes 707788 | tf_op jit(solution)/shard_map/pallas_call | solution.py:50
  108.2 4.0 %collective-permute-done.26.refs_0_ = bf16[512,512]{1,0:T(8,128)(2,1)S(1)} collective-permute-done((bf16[512,512]{1,0:T(8,128)(2,1)S(1)}, bf16[512,512]{1,0:T(8,128)(2,1)S(1)}, u32[]{:S(2)}, u32[]{:S(2)}) %collective-permute-start.26) | collective-permute-done | bytes 524320 | tf_op jit(solution)/shard_map/ppermute | solution.py:112
  113.6 1.7 %collective-permute-start.28 = (bf16[256,512]{1,0:T(8,128)(2,1)S(1)}, bf16[256,512]{1,0:T(8,128)(2,1)S(1)}, u32[]{:S(2)}, u32[]{:S(2)}) collective-permute-start(bf16[256,512]{1,0:T(8,128)(2,1)S(1)} %get-tuple-element.69), channel_id=1, source_target_pairs={{0,8},{8,16},{16,24},{24,28},{28,20},{20,12},{12,4},{4,0},{1,9},{9... | collective-permute-start | bytes 786440 | tf_op jit(solution)/shard_map/ppermute | solution.py:112
  115.7 3.4 %shard_map.52 = (f32[512,1024]{1,0:T(8,128)S(1)}, f32[1024,1024]{1,0:T(8,128)S(1)}) custom-call(bf16[512,4096]{1,0:T(8,128)(2,1)S(1)} %shard_map.28.refs_0_, bf16[512,512]{1,0:T(8,128)(2,1)S(1)} %get-tuple-element.63.refs_9_.refs_1_.refs_6_, bf16[512,512]{1,0:T(8,128)(2,1)S(1)} %collective-permute-done.31.refs_2_.refs_7_, ...), custom_call_target="tpu_custom_call" | custom-call | flops 161061280 | bytes 707788 | tf_op jit(solution)/shard_map/pallas_call | solution.py:50
  119.1 1.8 %shard_map.53.refs_2_.refs_11_ = f32[512,1024]{1,0:T(8,128)S(1)} custom-call(bf16[512,640]{1,0:T(8,128)(2,1)S(1)} %get-tuple-element.68.refs_2_.refs_0_, bf16[512,640]{1,0:T(8,128)(2,1)S(1)} %collective-permute-done.30.refs_1_, bf16[768,512]{1,0:T(8,128)(2,1)S(1)} %collective-permute-done.6.refs_3_.refs_2_.refs_1_.refs_6_, ...), custom_call_target="tpu_custom_call" | custom-call | flops 67108864 | bytes 445644 | tf_op jit(solution)/shard_map/pallas_call | solution.py:50
  126.7 3.4 %shard_map.56 = (f32[512,1024]{1,0:T(8,128)S(1)}, f32[1024,1024]{1,0:T(8,128)S(1)}) custom-call(bf16[512,4096]{1,0:T(8,128)(2,1)S(1)} %shard_map.28.refs_0_, bf16[512,512]{1,0:T(8,128)(2,1)S(1)} %get-tuple-element.72.refs_9_.refs_1_.refs_6_, bf16[512,512]{1,0:T(8,128)(2,1)S(1)} %collective-permute-done.36.refs_2_.refs_7_, ...), custom_call_target="tpu_custom_call" | custom-call | flops 161061280 | bytes 707788 | tf_op jit(solution)/shard_map/pallas_call | solution.py:50
  130.2 1.8 %shard_map.57.refs_10_ = f32[512,1024]{1,0:T(8,128)S(1)} custom-call(bf16[512,640]{1,0:T(8,128)(2,1)S(1)} %get-tuple-element.79.refs_9_.refs_0_, bf16[512,640]{1,0:T(8,128)(2,1)S(1)} %collective-permute-done.38.refs_1_, bf16[768,512]{1,0:T(8,128)(2,1)S(1)} %collective-permute-done.7.refs_5_.refs_1_.refs_3_.refs_6_.refs_8_.refs_2_, ...), custom_call_target="tpu_custom_call" | custom-call | flops 67108864 | bytes 445644 | tf_op jit(solution)/shard_map/pallas_call | solution.py:50
  132.0 3.2 %shard_map.58.refs_2_.refs_8_ = f32[512,1024]{1,0:T(8,128)S(1)} custom-call(bf16[512,4096]{1,0:T(8,128)(2,1)S(1)} %shard_map.28.refs_0_, bf16[256,512]{1,0:T(8,128)(2,1)S(1)} %get-tuple-element.74.refs_3_.refs_1_.refs_4_, bf16[256,512]{1,0:T(8,128)(2,1)S(1)} %get-tuple-element.76.refs_2_.refs_5_, ...), custom_call_target="tpu_custom_call" | custom-call | flops 80530640 | bytes 799539 | tf_op jit(solution)/shard_map/pallas_call | solution.py:50
  136.9 1.8 %shard_map.60 = bf16[512,1024]{1,0:T(8,128)(2,1)} custom-call(bf16[512,256]{1,0:T(8,128)(2,1)S(1)} %shard_map.59.refs_0_, bf16[512,256]{1,0:T(8,128)(2,1)S(1)} %collective-permute-done.39.refs_1_, bf16[384,512]{1,0:T(8,128)(2,1)S(1)} %collective-permute-done.10.refs_1_.refs_4_.refs_5_.refs_2_, ...), custom_call_target="tpu_custom_call" | custom-call | flops 26843544 | bytes 222822 | tf_op jit(solution)/shard_map/pallas_call | solution.py:50
  (91 shorter events, 41.2 us)
Async XLA Ops:
  1.2 20.6 %collective-permute-start.6 = (bf16[768,512]{1,0:T(8,128)(2,1)S(1)}, bf16[768,512]{1,0:T(8,128)(2,1)S(1)}, u32[]{:S(2)}, u32[]{:S(2)}) collective-permute-start(bf16[768,512]{1,0:T(8,128)(2,1)S(1)} %shard_map.29.refs_1_.refs_4_.refs_3_.refs_2_), channel_id=1, source_target_pairs={{8,0},{16,8},{24,16},{28,24},{20,28},{12,20},{4,12},{0,4},{9,1},{1... | collective-permute-start | bytes 2359304 | tf_op jit(solution)/shard_map/ppermute | solution.py:115
  4.3 19.3 %collective-permute-start.3 = (bf16[768,512]{1,0:T(8,128)(2,1)S(1)}, bf16[768,512]{1,0:T(8,128)(2,1)S(1)}, u32[]{:S(2)}, u32[]{:S(2)}) collective-permute-start(bf16[768,512]{1,0:T(8,128)(2,1)S(1)} %shard_map.29.refs_1_.refs_4_.refs_3_.refs_2_), channel_id=1, source_target_pairs={{0,8},{8,16},{16,24},{24,28},{28,20},{20,12},{12,4},{4,0},{1,9},{9... | collective-permute-start | bytes 2359304 | tf_op jit(solution)/shard_map/ppermute | solution.py:112
  4.4 24.8 %collective-permute-start = (bf16[128,4096]{1,0:T(8,128)(2,1)}, bf16[128,4096]{1,0:T(8,128)(2,1)S(1)}, u32[]{:S(2)}, u32[]{:S(2)}) collective-permute-start(bf16[128,4096]{1,0:T(8,128)(2,1)} %refs_0_.3), channel_id=1, source_target_pairs={{0,2},{1,3},{2,0},{3,1},{4,6},{5,7},{6,4},{7,5},{8,10},{9,11},{10,... | collective-permute-start | bytes 3145736 | tf_op jit(solution)/shard_map/ppermute | solution.py:118
  21.9 18.7 %collective-permute-start.7 = (bf16[768,512]{1,0:T(8,128)(2,1)S(1)}, bf16[768,512]{1,0:T(8,128)(2,1)S(1)}, u32[]{:S(2)}, u32[]{:S(2)}) collective-permute-start(bf16[768,512]{1,0:T(8,128)(2,1)S(1)} %collective-permute-done.6.refs_3_.refs_2_.refs_1_.refs_6_), channel_id=1, source_target_pairs={{8,0},{16,8},{24,16},{28,24},{20,28},{12,20},{4,12},{0,4},{9,1},{1... | collective-permute-start | bytes 2359304 | tf_op jit(solution)/shard_map/ppermute | solution.py:115
  23.5 18.4 %collective-permute-start.4 = (bf16[768,512]{1,0:T(8,128)(2,1)S(1)}, bf16[768,512]{1,0:T(8,128)(2,1)S(1)}, u32[]{:S(2)}, u32[]{:S(2)}) collective-permute-start(bf16[768,512]{1,0:T(8,128)(2,1)S(1)} %collective-permute-done.3.refs_2_.refs_1_.refs_5_), channel_id=1, source_target_pairs={{0,8},{8,16},{16,24},{24,28},{28,20},{20,12},{12,4},{4,0},{1,9},{9... | collective-permute-start | bytes 2359304 | tf_op jit(solution)/shard_map/ppermute | solution.py:112
  23.9 21.1 %collective-permute-start.1 = (bf16[128,4096]{1,0:T(8,128)(2,1)}, bf16[128,4096]{1,0:T(8,128)(2,1)S(1)}, u32[]{:S(2)}, u32[]{:S(2)}) collective-permute-start(bf16[128,4096]{1,0:T(8,128)(2,1)} %refs_0_.3), channel_id=1, source_target_pairs={{0,1},{1,0},{2,3},{3,2},{4,5},{5,4},{6,7},{7,6},{8,9},{9,8},{10,11... | collective-permute-start | bytes 3145736 | tf_op jit(solution)/shard_map/ppermute | solution.py:121
  29.2 15.8 %collective-permute-start.2 = (bf16[128,4096]{1,0:T(8,128)(2,1)S(1)}, bf16[128,4096]{1,0:T(8,128)(2,1)S(1)}, u32[]{:S(2)}, u32[]{:S(2)}) collective-permute-start(bf16[128,4096]{1,0:T(8,128)(2,1)S(1)} %collective-permute-done.refs_1_), channel_id=1, source_target_pairs={{0,1},{1,0},{2,3},{3,2},{4,5},{5,4},{6,7},{7,6},{8,9},{9,8},{10,11... | collective-permute-start | bytes 3145736 | tf_op jit(solution)/shard_map/ppermute | solution.py:121
  40.6 17.8 %collective-permute-start.8 = (bf16[768,512]{1,0:T(8,128)(2,1)S(1)}, bf16[768,512]{1,0:T(8,128)(2,1)S(1)}, u32[]{:S(2)}, u32[]{:S(2)}) collective-permute-start(bf16[768,512]{1,0:T(8,128)(2,1)S(1)} %collective-permute-done.7.refs_5_.refs_1_.refs_3_.refs_6_.refs_8_.refs_2_), channel_id=1, source_target_pairs={{8,0},{16,8},{24,16},{28,24},{20,28},{12,20},{4,12},{0,4},{9,1},{1... | collective-permute-start | bytes 2359304 | tf_op jit(solution)/shard_map/ppermute | solution.py:115
  42.0 17.6 %collective-permute-start.5 = (bf16[768,512]{1,0:T(8,128)(2,1)S(1)}, bf16[768,512]{1,0:T(8,128)(2,1)S(1)}, u32[]{:S(2)}, u32[]{:S(2)}) collective-permute-start(bf16[768,512]{1,0:T(8,128)(2,1)S(1)} %collective-permute-done.4.refs_4_.refs_2_.refs_5_), channel_id=1, source_target_pairs={{0,8},{8,16},{16,24},{24,28},{28,20},{20,12},{12,4},{4,0},{1,9},{9... | collective-permute-start | bytes 2359304 | tf_op jit(solution)/shard_map/ppermute | solution.py:112
  70.0 13.9 %collective-permute-start.16 = (bf16[512,512]{1,0:T(8,128)(2,1)S(1)}, bf16[512,512]{1,0:T(8,128)(2,1)S(1)}, u32[]{:S(2)}, u32[]{:S(2)}) collective-permute-start(bf16[512,512]{1,0:T(8,128)(2,1)S(1)} %shard_map.43.refs_1_.refs_3_), channel_id=1, source_target_pairs={{0,8},{8,16},{16,24},{24,28},{28,20},{20,12},{12,4},{4,0},{1,9},{9... | collective-permute-start | bytes 1572872 | tf_op jit(solution)/shard_map/ppermute | solution.py:112
  71.2 13.6 %collective-permute-start.17 = (bf16[512,512]{1,0:T(8,128)(2,1)S(1)}, bf16[512,512]{1,0:T(8,128)(2,1)S(1)}, u32[]{:S(2)}, u32[]{:S(2)}) collective-permute-start(bf16[512,512]{1,0:T(8,128)(2,1)S(1)} %shard_map.43.refs_1_.refs_3_), channel_id=1, source_target_pairs={{8,0},{16,8},{24,16},{28,24},{20,28},{12,20},{4,12},{0,4},{9,1},{1... | collective-permute-start | bytes 1572872 | tf_op jit(solution)/shard_map/ppermute | solution.py:115
  74.9 13.1 %collective-permute-start.13 = (bf16[512,896]{1,0:T(8,128)(2,1)S(1)}, bf16[512,896]{1,0:T(8,128)(2,1)S(1)}, u32[]{:S(2)}, u32[]{:S(2)}) collective-permute-start(bf16[512,896]{1,0:T(8,128)(2,1)S(1)} %shard_map.38.refs_3_), channel_id=1, source_target_pairs={{0,1},{1,0},{2,3},{3,2},{4,5},{5,4},{6,7},{7,6},{8,9},{9,8},{10,11... | collective-permute-start | bytes 2752520 | tf_op jit(solution)/shard_map/ppermute | solution.py:121
  75.8 12.0 %collective-permute-start.14 = (bf16[512,640]{1,0:T(8,128)(2,1)S(1)}, bf16[512,640]{1,0:T(8,128)(2,1)S(1)}, u32[]{:S(2)}, u32[]{:S(2)}) collective-permute-start(bf16[512,640]{1,0:T(8,128)(2,1)S(1)} %shard_map.41), channel_id=1, source_target_pairs={{0,1},{1,0},{2,3},{3,2},{4,5},{5,4},{6,7},{7,6},{8,9},{9,8},{10,11... | collective-permute-start | bytes 1966088 | tf_op jit(solution)/shard_map/ppermute | solution.py:121
  76.3 13.9 %collective-permute-start.15 = (bf16[512,512]{1,0:T(8,128)(2,1)S(1)}, bf16[512,512]{1,0:T(8,128)(2,1)S(1)}, u32[]{:S(2)}, u32[]{:S(2)}) collective-permute-start(bf16[512,512]{1,0:T(8,128)(2,1)S(1)} %get-tuple-element.48.refs_6_.refs_4_), channel_id=1, source_target_pairs={{0,2},{1,3},{2,0},{3,1},{4,6},{5,7},{6,4},{7,5},{8,10},{9,11},{10,... | collective-permute-start | bytes 1572872 | tf_op jit(solution)/shard_map/ppermute | solution.py:118
  84.9 12.8 %collective-permute-start.23 = (bf16[512,512]{1,0:T(8,128)(2,1)S(1)}, bf16[512,512]{1,0:T(8,128)(2,1)S(1)}, u32[]{:S(2)}, u32[]{:S(2)}) collective-permute-start(bf16[512,512]{1,0:T(8,128)(2,1)S(1)} %get-tuple-element.57.refs_3_.refs_1_.refs_6_), channel_id=1, source_target_pairs={{0,8},{8,16},{16,24},{24,28},{28,20},{20,12},{12,4},{4,0},{1,9},{9... | collective-permute-start | bytes 1572872 | tf_op jit(solution)/shard_map/ppermute | solution.py:112
  86.6 12.5 %collective-permute-start.24 = (bf16[512,512]{1,0:T(8,128)(2,1)S(1)}, bf16[512,512]{1,0:T(8,128)(2,1)S(1)}, u32[]{:S(2)}, u32[]{:S(2)}) collective-permute-start(bf16[512,512]{1,0:T(8,128)(2,1)S(1)} %get-tuple-element.61.refs_3_), channel_id=1, source_target_pairs={{8,0},{16,8},{24,16},{28,24},{20,28},{12,20},{4,12},{0,4},{9,1},{1... | collective-permute-start | bytes 1572872 | tf_op jit(solution)/shard_map/ppermute | solution.py:115
  90.4 15.9 %collective-permute-start.19 = (bf16[512,640]{1,0:T(8,128)(2,1)S(1)}, bf16[512,640]{1,0:T(8,128)(2,1)S(1)}, u32[]{:S(2)}, u32[]{:S(2)}) collective-permute-start(bf16[512,640]{1,0:T(8,128)(2,1)S(1)} %get-tuple-element.59), channel_id=1, source_target_pairs={{0,2},{1,3},{2,0},{3,1},{4,6},{5,7},{6,4},{7,5},{8,10},{9,11},{10,... | collective-permute-start | bytes 1966088 | tf_op jit(solution)/shard_map/ppermute | solution.py:118
  91.6 9.6 %collective-permute-start.22 = (bf16[512,512]{1,0:T(8,128)(2,1)S(1)}, bf16[512,512]{1,0:T(8,128)(2,1)S(1)}, u32[]{:S(2)}, u32[]{:S(2)}) collective-permute-start(bf16[512,512]{1,0:T(8,128)(2,1)S(1)} %get-tuple-element.61.refs_3_), channel_id=1, source_target_pairs={{0,1},{1,0},{2,3},{3,2},{4,5},{5,4},{6,7},{7,6},{8,9},{9,8},{10,11... | collective-permute-start | bytes 1572872 | tf_op jit(solution)/shard_map/ppermute | solution.py:121
  99.1 13.1 %collective-permute-start.26 = (bf16[512,512]{1,0:T(8,128)(2,1)S(1)}, bf16[512,512]{1,0:T(8,128)(2,1)S(1)}, u32[]{:S(2)}, u32[]{:S(2)}) collective-permute-start(bf16[512,512]{1,0:T(8,128)(2,1)S(1)} %get-tuple-element.63.refs_9_.refs_1_.refs_6_), channel_id=1, source_target_pairs={{0,8},{8,16},{16,24},{24,28},{28,20},{20,12},{12,4},{4,0},{1,9},{9... | collective-permute-start | bytes 1572872 | tf_op jit(solution)/shard_map/ppermute | solution.py:112
  100.8 12.7 %collective-permute-start.27 = (bf16[512,512]{1,0:T(8,128)(2,1)S(1)}, bf16[512,512]{1,0:T(8,128)(2,1)S(1)}, u32[]{:S(2)}, u32[]{:S(2)}) collective-permute-start(bf16[512,512]{1,0:T(8,128)(2,1)S(1)} %get-tuple-element.67.refs_3_.refs_9_), channel_id=1, source_target_pairs={{8,0},{16,8},{24,16},{28,24},{20,28},{12,20},{4,12},{0,4},{9,1},{1... | collective-permute-start | bytes 1572872 | tf_op jit(solution)/shard_map/ppermute | solution.py:115
  101.2 14.1 %collective-permute-start.31 = (bf16[512,512]{1,0:T(8,128)(2,1)S(1)}, bf16[512,512]{1,0:T(8,128)(2,1)S(1)}, u32[]{:S(2)}, u32[]{:S(2)}) collective-permute-start(bf16[512,512]{1,0:T(8,128)(2,1)S(1)} %get-tuple-element.63.refs_9_.refs_1_.refs_6_), channel_id=1, source_target_pairs={{0,1},{1,0},{2,3},{3,2},{4,5},{5,4},{6,7},{7,6},{8,9},{9,8},{10,11... | collective-permute-start | bytes 1572872 | tf_op jit(solution)/shard_map/ppermute | solution.py:121
  106.5 12.7 %collective-permute-start.30 = (bf16[512,640]{1,0:T(8,128)(2,1)S(1)}, bf16[512,640]{1,0:T(8,128)(2,1)S(1)}, u32[]{:S(2)}, u32[]{:S(2)}) collective-permute-start(bf16[512,640]{1,0:T(8,128)(2,1)S(1)} %get-tuple-element.68.refs_2_.refs_0_), channel_id=1, source_target_pairs={{0,1},{1,0},{2,3},{3,2},{4,5},{5,4},{6,7},{7,6},{8,9},{9,8},{10,11... | collective-permute-start | bytes 1966088 | tf_op jit(solution)/shard_map/ppermute | solution.py:121
  106.7 17.0 %collective-permute-start.25 = (bf16[512,640]{1,0:T(8,128)(2,1)S(1)}, bf16[512,640]{1,0:T(8,128)(2,1)S(1)}, u32[]{:S(2)}, u32[]{:S(2)}) collective-permute-start(bf16[512,640]{1,0:T(8,128)(2,1)S(1)} %get-tuple-element.65), channel_id=1, source_target_pairs={{0,2},{1,3},{2,0},{3,1},{4,6},{5,7},{6,4},{7,5},{8,10},{9,11},{10,... | collective-permute-start | bytes 1966088 | tf_op jit(solution)/shard_map/ppermute | solution.py:118
  124.9 10.4 %collective-permute-start.33 = (bf16[512,256]{1,0:T(8,128)(2,1)S(1)}, bf16[512,256]{1,0:T(8,128)(2,1)S(1)}, u32[]{:S(2)}, u32[]{:S(2)}) collective-permute-start(bf16[512,256]{1,0:T(8,128)(2,1)S(1)} %get-tuple-element.75), channel_id=1, source_target_pairs={{0,2},{1,3},{2,0},{3,1},{4,6},{5,7},{6,4},{7,5},{8,10},{9,11},{10,... | collective-permute-start | bytes 786440 | tf_op jit(solution)/shard_map/ppermute | solution.py:118
  (17 other events, 146.8 us)

commit v5 on v4

--- a/solution.py
+++ b/solution.py
@@ -34,7 +34,7 @@
     return [slice(at, min(at + step, extent)) for at in range(0, extent, step)]
 
 
-def call(body, ins, outs, flops, after=(), leave=False, scratch=()):
+def call(body, ins, outs, flops, after=(), leave=False, scratch=(), out_left=False):
     flat, tree = jax.tree.flatten(ins)
     after = list(after)
     n_in, n_out = len(flat), len(outs)
@@ -51,7 +51,7 @@
         kernel,
         out_shape=[pltpu.VMEM(*o) if isinstance(o, tuple) else o for o in outs],
         in_specs=[HBM if leave else VMEM] * n_in + [ANY] * len(after),
-        out_specs=[VMEM] * n_out,
+        out_specs=[ANY if out_left else VMEM] * n_out,
         scratch_shapes=[pltpu.SemaphoreType.DMA((n_out,))] if leave else list(scratch),
         compiler_params=pltpu.CompilerParams(vmem_limit_bytes=16 << 20),
         cost_estimate=pl.CostEstimate(flops=flops // 20, bytes_accessed=nbytes // 20, transcendentals=0),
@@ -278,8 +278,8 @@
     keep = q_part([0], True, F32)
     give1 = q_part([1], False, BF, keep)[0]
     q0, q0_b = q_sum(keep, give)
-    keep = q_part([1], True, F32, [q0_b])
-    q1, q1_b = q_sum(keep, give1)
+    keep1 = q_part([1], True, F32, [q0_b])
+    q1, q1_b = q_sum(keep1, give1)
     keep = q_part([2, 3], True, F32, [q0_b])
     give = q_part([2, 3], False, BF, keep)[0]
     q2, q2_b, q3, q3_b = q_sum(keep, give)
@@ -325,8 +325,9 @@
         return call(body, ins, outs, flops, after, False, scratch)
 
     def collect(g, sides, out, final, after=()):
-        def body(given, outs):
+        def body(given, outs, *scratch):
             side_refs, chunks, base_ref = given
+            copies = []
             for cols in cuts([e for e, _ in chunks]) + [slice(early, rows)]:
                 term = None if out is None or final else base_ref[:, cols]
                 for (_, here, offset, size), (early_rows, late_rows) in zip(spots(g), chunks):
@@ -340,11 +341,25 @@
                         term = add_dots([(left, right)], term)
                 if final:
                     term = base_ref[:, cols] - 0.5 * term
-                outs[0][:, cols] = term.astype(outs[0].dtype)
+                if not final:
+                    outs[0][:, cols] = term
+                    continue
+                buf, sem = scratch
+                buf[:, cols] = term.astype(BF)
+                copies.append(
+                    pltpu.make_async_copy(buf.at[:, cols], outs[0].at[:, cols], sem.at[len(copies)])
+                )
+                copies[-1].start()
+            for copy in copies:
+                copy.wait()
 
         outs = [jax.ShapeDtypeStruct((count, rows), BF) if final else ((count, rows), F32)]
         ins = (sides, [(w[k], v[k]) for k, *_ in spots(g)], out)
-        return call(body, ins, outs, 4 * count * rows * sizes[g], after)[0]
+        scratch = ()
+        if final:
+            scratch = [pltpu.VMEM((count, rows), BF), pltpu.SemaphoreType.DMA((n,))]
+        flops = 4 * count * rows * sizes[g]
+        return call(body, ins, outs, flops, after, False, scratch, final)[0]
 
     def join(given, outs):
         outs[0][:LATE, :] = given[0][...]
@@ -378,7 +393,7 @@
     u, d = up(block), down(block)
     far = over_x(q0_b)
     sums = late_part([0], None, False, [q0_b])
-    ru, rd = stepped(u, d, False, [sums[0], give])
+    ru, rd = stepped(u, d, False, [sums[0], give, keep1[0]])
     v += [both([ru]), both([rd])]
     u, d = up(ru), down(rd)
     s0, nq = turned(q0, far, q1_b, [ru, q2_b])

time: 139 us -> 139 us (level)
  no operation moved by 1% of the time
where the time goes in v5:
time: 139 us
  waiting for transfers between devices  74.5 us (54%)
  Pallas kernels  34.6 us (25%)
  starting transfers between devices  29.2 us (21%)
    ppermute x8, waiting for transfers between devices, down(): lax.ppermute(v, 'dp', [(ring[(i + 1) % n], ring[i]) for i in range(n)])  40.8 us
    pallas_call x33, Pallas kernels, call(): pl.pallas_call(kernel, out_shape=[pltpu.VMEM(*o) if isinstance(o, tuple)...  34.6 us
    ppermute x8, waiting for transfers between devices, up(): lax.ppermute(v, 'dp', [(ring[i], ring[(i + 1) % n]) for i in range(n)])  19.5 us
    ppermute x6, waiting for transfers between devices, over_x(): return lax.ppermute(v, 'tensor', [(t, t ^ 2) for t in range(4)])  12.2 us
    ppermute x8, starting transfers between devices, down(): lax.ppermute(v, 'dp', [(ring[(i + 1) % n], ring[i]) for i in range(n)])  9.42 us
    ppermute x6, starting transfers between devices, over_x(): return lax.ppermute(v, 'tensor', [(t, t ^ 2) for t in range(4)])  8.41 us
    ppermute x8, starting transfers between devices, up(): lax.ppermute(v, 'dp', [(ring[i], ring[(i + 1) % n]) for i in range(n)])  8.11 us
    ppermute x18, starting transfers between devices, over_core(): return lax.ppermute(v, 'tensor', [(t, t ^ 1) for t in range(4)])  3.27 us
  transfers between devices with their start and end apart: 40, of which 21 were waited for; matrix products, arithmetic and copies ran while one was open for 0% of the time, Pallas kernels for 22%

profile of v5, /device:TPU:0, one launch (start us, length us, event | category | flops | bytes accessed | tf_op | source)
XLA Modules:
  0.0 138.8 jit_solution(11149347900375336449)
XLA Ops:
  1.2 3.0 %collective-permute-start.6 = (bf16[768,512]{1,0:T(8,128)(2,1)S(1)}, bf16[768,512]{1,0:T(8,128)(2,1)S(1)}, u32[]{:S(2)}, u32[]{:S(2)}) collective-permute-start(bf16[768,512]{1,0:T(8,128)(2,1)S(1)} %shard_map.29.refs_1_.refs_4_.refs_3_.refs_2_), channel_id=1, source_target_pairs={{8,0},{16,8},{24,16},{28,24},{20,28},{12,20},{4,12},{0,4},{9,1},{1... | collective-permute-start | bytes 2359304 | tf_op jit(solution)/shard_map/ppermute | solution.py:115
  4.4 1.9 %collective-permute-start = (bf16[128,4096]{1,0:T(8,128)(2,1)}, bf16[128,4096]{1,0:T(8,128)(2,1)S(1)}, u32[]{:S(2)}, u32[]{:S(2)}) collective-permute-start(bf16[128,4096]{1,0:T(8,128)(2,1)} %refs_0_.3), channel_id=1, source_target_pairs={{0,2},{1,3},{2,0},{3,1},{4,6},{5,7},{6,4},{7,5},{8,10},{9,11},{10,... | collective-permute-start | bytes 3145736 | tf_op jit(solution)/shard_map/ppermute | solution.py:118
  6.3 15.6 %collective-permute-done.6.refs_3_.refs_2_.refs_1_.refs_6_ = bf16[768,512]{1,0:T(8,128)(2,1)S(1)} collective-permute-done((bf16[768,512]{1,0:T(8,128)(2,1)S(1)}, bf16[768,512]{1,0:T(8,128)(2,1)S(1)}, u32[]{:S(2)}, u32[]{:S(2)}) %collective-permute-start.6) | collective-permute-done | bytes 786464 | tf_op jit(solution)/shard_map/ppermute | solution.py:115
  21.9 1.7 %collective-permute-start.7 = (bf16[768,512]{1,0:T(8,128)(2,1)S(1)}, bf16[768,512]{1,0:T(8,128)(2,1)S(1)}, u32[]{:S(2)}, u32[]{:S(2)}) collective-permute-start(bf16[768,512]{1,0:T(8,128)(2,1)S(1)} %collective-permute-done.6.refs_3_.refs_2_.refs_1_.refs_6_), channel_id=1, source_target_pairs={{8,0},{16,8},{24,16},{28,24},{20,28},{12,20},{4,12},{0,4},{9,1},{1... | collective-permute-start | bytes 2359304 | tf_op jit(solution)/shard_map/ppermute | solution.py:115
  23.9 5.3 %collective-permute-done.refs_1_ = bf16[128,4096]{1,0:T(8,128)(2,1)S(1)} collective-permute-done((bf16[128,4096]{1,0:T(8,128)(2,1)}, bf16[128,4096]{1,0:T(8,128)(2,1)S(1)}, u32[]{:S(2)}, u32[]{:S(2)}) %collective-permute-start) | collective-permute-done | bytes 1048608 | tf_op jit(solution)/shard_map/ppermute | solution.py:118
  29.2 11.4 %collective-permute-done.7.refs_5_.refs_1_.refs_3_.refs_6_.refs_8_.refs_2_ = bf16[768,512]{1,0:T(8,128)(2,1)S(1)} collective-permute-done((bf16[768,512]{1,0:T(8,128)(2,1)S(1)}, bf16[768,512]{1,0:T(8,128)(2,1)S(1)}, u32[]{:S(2)}, u32[]{:S(2)}) %collective-permute-start.7) | collective-permute-done | bytes 786464 | tf_op jit(solution)/shard_map/ppermute | solution.py:115
  45.3 2.2 %shard_map.30.refs_2_.refs_3_ = f32[512,768]{1,0:T(8,128)S(1)} custom-call(bf16[512,4096]{1,0:T(8,128)(2,1)S(1)} %shard_map.28.refs_0_, bf16[768,512]{1,0:T(8,128)(2,1)S(1)} %shard_map.29.refs_1_.refs_4_.refs_3_.refs_2_, bf16[768,512]{1,0:T(8,128)(2,1)S(1)} %collective-permute-done.3.refs_2_.refs_1_.refs_5_, ...), custom_call_target="tpu_custom_call" | custom-call | flops 100663296 | bytes 406323 | tf_op jit(solution)/shard_map/pallas_call | solution.py:50
  47.6 2.5 %collective-permute-done.9.refs_3_.refs_1_ = bf16[256,512]{1,0:T(8,128)(2,1)S(1)} collective-permute-done((bf16[256,512]{1,0:T(8,128)(2,1)S(1)}, bf16[256,512]{1,0:T(8,128)(2,1)S(1)}, u32[]{:S(2)}, u32[]{:S(2)}) %collective-permute-start.9) | collective-permute-done | bytes 262176 | tf_op jit(solution)/shard_map/ppermute | solution.py:118
  50.0 8.4 %collective-permute-done.8.refs_1_.refs_2_.refs_3_.refs_6_.refs_8_ = bf16[768,512]{1,0:T(8,128)(2,1)S(1)} collective-permute-done((bf16[768,512]{1,0:T(8,128)(2,1)S(1)}, bf16[768,512]{1,0:T(8,128)(2,1)S(1)}, u32[]{:S(2)}, u32[]{:S(2)}) %collective-permute-start.8) | collective-permute-done | bytes 786464 | tf_op jit(solution)/shard_map/ppermute | solution.py:115
  62.7 4.9 %collective-permute-done.10.refs_1_.refs_4_.refs_5_.refs_2_ = bf16[384,512]{1,0:T(8,128)(2,1)S(1)} collective-permute-done((bf16[384,512]{1,0:T(8,128)(2,1)S(1)}, bf16[384,512]{1,0:T(8,128)(2,1)S(1)}, u32[]{:S(2)}, u32[]{:S(2)}) %collective-permute-start.10) | collective-permute-done | bytes 393248 | tf_op jit(solution)/shard_map/ppermute | solution.py:112
  78.3 1.8 %shard_map.44 = (f32[512,1024]{1,0:T(8,128)S(1)}, f32[1024,1024]{1,0:T(8,128)S(1)}) custom-call(bf16[512,4096]{1,0:T(8,128)(2,1)S(1)} %shard_map.28.refs_0_, bf16[512,512]{1,0:T(8,128)(2,1)S(1)} %shard_map.43.refs_1_.refs_3_, bf16[512,512]{1,0:T(8,128)(2,1)S(1)} %collective-permute-done.18.refs_2_.refs_4_, ...), custom_call_target="tpu_custom_call" | custom-call | flops 80530640 | bytes 301465 | tf_op jit(solution)/shard_map/pallas_call | solution.py:50
  80.1 3.8 %collective-permute-done.16.refs_0_ = bf16[512,512]{1,0:T(8,128)(2,1)S(1)} collective-permute-done((bf16[512,512]{1,0:T(8,128)(2,1)S(1)}, bf16[512,512]{1,0:T(8,128)(2,1)S(1)}, u32[]{:S(2)}, u32[]{:S(2)}) %collective-permute-start.16) | collective-permute-done | bytes 524320 | tf_op jit(solution)/shard_map/ppermute | solution.py:112
  87.5 2.8 %collective-permute-done.15.refs_1_ = bf16[512,512]{1,0:T(8,128)(2,1)S(1)} collective-permute-done((bf16[512,512]{1,0:T(8,128)(2,1)S(1)}, bf16[512,512]{1,0:T(8,128)(2,1)S(1)}, u32[]{:S(2)}, u32[]{:S(2)}) %collective-permute-start.15) | collective-permute-done | bytes 524320 | tf_op jit(solution)/shard_map/ppermute | solution.py:118
  92.1 5.6 %collective-permute-done.23.refs_0_ = bf16[512,512]{1,0:T(8,128)(2,1)S(1)} collective-permute-done((bf16[512,512]{1,0:T(8,128)(2,1)S(1)}, bf16[512,512]{1,0:T(8,128)(2,1)S(1)}, u32[]{:S(2)}, u32[]{:S(2)}) %collective-permute-start.23) | collective-permute-done | bytes 524320 | tf_op jit(solution)/shard_map/ppermute | solution.py:112
  99.1 1.7 %collective-permute-start.26 = (bf16[512,512]{1,0:T(8,128)(2,1)S(1)}, bf16[512,512]{1,0:T(8,128)(2,1)S(1)}, u32[]{:S(2)}, u32[]{:S(2)}) collective-permute-start(bf16[512,512]{1,0:T(8,128)(2,1)S(1)} %get-tuple-element.63.refs_9_.refs_1_.refs_6_), channel_id=1, source_target_pairs={{0,8},{8,16},{16,24},{24,28},{28,20},{20,12},{12,4},{4,0},{1,9},{9... | collective-permute-start | bytes 1572872 | tf_op jit(solution)/shard_map/ppermute | solution.py:112
  101.2 3.5 %shard_map.48 = (f32[512,1024]{1,0:T(8,128)S(1)}, f32[1024,1024]{1,0:T(8,128)S(1)}) custom-call(bf16[512,4096]{1,0:T(8,128)(2,1)S(1)} %shard_map.28.refs_0_, bf16[512,512]{1,0:T(8,128)(2,1)S(1)} %get-tuple-element.57.refs_3_.refs_1_.refs_6_, bf16[512,512]{1,0:T(8,128)(2,1)S(1)} %collective-permute-done.21.refs_2_.refs_7_, ...), custom_call_target="tpu_custom_call" | custom-call | flops 161061280 | bytes 707788 | tf_op jit(solution)/shard_map/pallas_call | solution.py:50
  108.2 4.0 %collective-permute-done.26.refs_0_ = bf16[512,512]{1,0:T(8,128)(2,1)S(1)} collective-permute-done((bf16[512,512]{1,0:T(8,128)(2,1)S(1)}, bf16[512,512]{1,0:T(8,128)(2,1)S(1)}, u32[]{:S(2)}, u32[]{:S(2)}) %collective-permute-start.26) | collective-permute-done | bytes 524320 | tf_op jit(solution)/shard_map/ppermute | solution.py:112
  113.6 1.7 %collective-permute-start.28 = (bf16[256,512]{1,0:T(8,128)(2,1)S(1)}, bf16[256,512]{1,0:T(8,128)(2,1)S(1)}, u32[]{:S(2)}, u32[]{:S(2)}) collective-permute-start(bf16[256,512]{1,0:T(8,128)(2,1)S(1)} %get-tuple-element.69), channel_id=1, source_target_pairs={{0,8},{8,16},{16,24},{24,28},{28,20},{20,12},{12,4},{4,0},{1,9},{9... | collective-permute-start | bytes 786440 | tf_op jit(solution)/shard_map/ppermute | solution.py:112
  115.7 3.4 %shard_map.52 = (f32[512,1024]{1,0:T(8,128)S(1)}, f32[1024,1024]{1,0:T(8,128)S(1)}) custom-call(bf16[512,4096]{1,0:T(8,128)(2,1)S(1)} %shard_map.28.refs_0_, bf16[512,512]{1,0:T(8,128)(2,1)S(1)} %get-tuple-element.63.refs_9_.refs_1_.refs_6_, bf16[512,512]{1,0:T(8,128)(2,1)S(1)} %collective-permute-done.31.refs_2_.refs_7_, ...), custom_call_target="tpu_custom_call" | custom-call | flops 161061280 | bytes 707788 | tf_op jit(solution)/shard_map/pallas_call | solution.py:50
  119.1 1.8 %shard_map.53.refs_2_.refs_11_ = f32[512,1024]{1,0:T(8,128)S(1)} custom-call(bf16[512,640]{1,0:T(8,128)(2,1)S(1)} %get-tuple-element.68.refs_2_.refs_0_, bf16[512,640]{1,0:T(8,128)(2,1)S(1)} %collective-permute-done.30.refs_1_, bf16[768,512]{1,0:T(8,128)(2,1)S(1)} %collective-permute-done.6.refs_3_.refs_2_.refs_1_.refs_6_, ...), custom_call_target="tpu_custom_call" | custom-call | flops 67108864 | bytes 445644 | tf_op jit(solution)/shard_map/pallas_call | solution.py:50
  126.7 3.4 %shard_map.56 = (f32[512,1024]{1,0:T(8,128)S(1)}, f32[1024,1024]{1,0:T(8,128)S(1)}) custom-call(bf16[512,4096]{1,0:T(8,128)(2,1)S(1)} %shard_map.28.refs_0_, bf16[512,512]{1,0:T(8,128)(2,1)S(1)} %get-tuple-element.72.refs_9_.refs_1_.refs_6_, bf16[512,512]{1,0:T(8,128)(2,1)S(1)} %collective-permute-done.36.refs_2_.refs_7_, ...), custom_call_target="tpu_custom_call" | custom-call | flops 161061280 | bytes 707788 | tf_op jit(solution)/shard_map/pallas_call | solution.py:50
  130.2 1.8 %shard_map.57.refs_10_ = f32[512,1024]{1,0:T(8,128)S(1)} custom-call(bf16[512,640]{1,0:T(8,128)(2,1)S(1)} %get-tuple-element.79.refs_9_.refs_0_, bf16[512,640]{1,0:T(8,128)(2,1)S(1)} %collective-permute-done.38.refs_1_, bf16[768,512]{1,0:T(8,128)(2,1)S(1)} %collective-permute-done.7.refs_5_.refs_1_.refs_3_.refs_6_.refs_8_.refs_2_, ...), custom_call_target="tpu_custom_call" | custom-call | flops 67108864 | bytes 445644 | tf_op jit(solution)/shard_map/pallas_call | solution.py:50
  132.0 3.2 %shard_map.58.refs_2_.refs_8_ = f32[512,1024]{1,0:T(8,128)S(1)} custom-call(bf16[512,4096]{1,0:T(8,128)(2,1)S(1)} %shard_map.28.refs_0_, bf16[256,512]{1,0:T(8,128)(2,1)S(1)} %get-tuple-element.74.refs_3_.refs_1_.refs_4_, bf16[256,512]{1,0:T(8,128)(2,1)S(1)} %get-tuple-element.76.refs_2_.refs_5_, ...), custom_call_target="tpu_custom_call" | custom-call | flops 80530640 | bytes 799539 | tf_op jit(solution)/shard_map/pallas_call | solution.py:50
  136.9 1.7 %shard_map.60 = bf16[512,1024]{1,0:T(8,128)(2,1)} custom-call(bf16[512,256]{1,0:T(8,128)(2,1)S(1)} %shard_map.59.refs_0_, bf16[512,256]{1,0:T(8,128)(2,1)S(1)} %collective-permute-done.39.refs_1_, bf16[384,512]{1,0:T(8,128)(2,1)S(1)} %collective-permute-done.10.refs_1_.refs_4_.refs_5_.refs_2_, ...), custom_call_target="tpu_custom_call" | custom-call | flops 26843544 | bytes 222822 | tf_op jit(solution)/shard_map/pallas_call | solution.py:50
  (91 shorter events, 41.2 us)
Async XLA Ops:
  1.2 20.6 %collective-permute-start.6 = (bf16[768,512]{1,0:T(8,128)(2,1)S(1)}, bf16[768,512]{1,0:T(8,128)(2,1)S(1)}, u32[]{:S(2)}, u32[]{:S(2)}) collective-permute-start(bf16[768,512]{1,0:T(8,128)(2,1)S(1)} %shard_map.29.refs_1_.refs_4_.refs_3_.refs_2_), channel_id=1, source_target_pairs={{8,0},{16,8},{24,16},{28,24},{20,28},{12,20},{4,12},{0,4},{9,1},{1... | collective-permute-start | bytes 2359304 | tf_op jit(solution)/shard_map/ppermute | solution.py:115
  4.3 19.3 %collective-permute-start.3 = (bf16[768,512]{1,0:T(8,128)(2,1)S(1)}, bf16[768,512]{1,0:T(8,128)(2,1)S(1)}, u32[]{:S(2)}, u32[]{:S(2)}) collective-permute-start(bf16[768,512]{1,0:T(8,128)(2,1)S(1)} %shard_map.29.refs_1_.refs_4_.refs_3_.refs_2_), channel_id=1, source_target_pairs={{0,8},{8,16},{16,24},{24,28},{28,20},{20,12},{12,4},{4,0},{1,9},{9... | collective-permute-start | bytes 2359304 | tf_op jit(solution)/shard_map/ppermute | solution.py:112
  4.4 24.8 %collective-permute-start = (bf16[128,4096]{1,0:T(8,128)(2,1)}, bf16[128,4096]{1,0:T(8,128)(2,1)S(1)}, u32[]{:S(2)}, u32[]{:S(2)}) collective-permute-start(bf16[128,4096]{1,0:T(8,128)(2,1)} %refs_0_.3), channel_id=1, source_target_pairs={{0,2},{1,3},{2,0},{3,1},{4,6},{5,7},{6,4},{7,5},{8,10},{9,11},{10,... | collective-permute-start | bytes 3145736 | tf_op jit(solution)/shard_map/ppermute | solution.py:118
  21.9 18.7 %collective-permute-start.7 = (bf16[768,512]{1,0:T(8,128)(2,1)S(1)}, bf16[768,512]{1,0:T(8,128)(2,1)S(1)}, u32[]{:S(2)}, u32[]{:S(2)}) collective-permute-start(bf16[768,512]{1,0:T(8,128)(2,1)S(1)} %collective-permute-done.6.refs_3_.refs_2_.refs_1_.refs_6_), channel_id=1, source_target_pairs={{8,0},{16,8},{24,16},{28,24},{20,28},{12,20},{4,12},{0,4},{9,1},{1... | collective-permute-start | bytes 2359304 | tf_op jit(solution)/shard_map/ppermute | solution.py:115
  23.5 18.4 %collective-permute-start.4 = (bf16[768,512]{1,0:T(8,128)(2,1)S(1)}, bf16[768,512]{1,0:T(8,128)(2,1)S(1)}, u32[]{:S(2)}, u32[]{:S(2)}) collective-permute-start(bf16[768,512]{1,0:T(8,128)(2,1)S(1)} %collective-permute-done.3.refs_2_.refs_1_.refs_5_), channel_id=1, source_target_pairs={{0,8},{8,16},{16,24},{24,28},{28,20},{20,12},{12,4},{4,0},{1,9},{9... | collective-permute-start | bytes 2359304 | tf_op jit(solution)/shard_map/ppermute | solution.py:112
  23.9 21.1 %collective-permute-start.1 = (bf16[128,4096]{1,0:T(8,128)(2,1)}, bf16[128,4096]{1,0:T(8,128)(2,1)S(1)}, u32[]{:S(2)}, u32[]{:S(2)}) collective-permute-start(bf16[128,4096]{1,0:T(8,128)(2,1)} %refs_0_.3), channel_id=1, source_target_pairs={{0,1},{1,0},{2,3},{3,2},{4,5},{5,4},{6,7},{7,6},{8,9},{9,8},{10,11... | collective-permute-start | bytes 3145736 | tf_op jit(solution)/shard_map/ppermute | solution.py:121
  29.2 15.8 %collective-permute-start.2 = (bf16[128,4096]{1,0:T(8,128)(2,1)S(1)}, bf16[128,4096]{1,0:T(8,128)(2,1)S(1)}, u32[]{:S(2)}, u32[]{:S(2)}) collective-permute-start(bf16[128,4096]{1,0:T(8,128)(2,1)S(1)} %collective-permute-done.refs_1_), channel_id=1, source_target_pairs={{0,1},{1,0},{2,3},{3,2},{4,5},{5,4},{6,7},{7,6},{8,9},{9,8},{10,11... | collective-permute-start | bytes 3145736 | tf_op jit(solution)/shard_map/ppermute | solution.py:121
  40.6 17.8 %collective-permute-start.8 = (bf16[768,512]{1,0:T(8,128)(2,1)S(1)}, bf16[768,512]{1,0:T(8,128)(2,1)S(1)}, u32[]{:S(2)}, u32[]{:S(2)}) collective-permute-start(bf16[768,512]{1,0:T(8,128)(2,1)S(1)} %collective-permute-done.7.refs_5_.refs_1_.refs_3_.refs_6_.refs_8_.refs_2_), channel_id=1, source_target_pairs={{8,0},{16,8},{24,16},{28,24},{20,28},{12,20},{4,12},{0,4},{9,1},{1... | collective-permute-start | bytes 2359304 | tf_op jit(solution)/shard_map/ppermute | solution.py:115
  42.0 17.6 %collective-permute-start.5 = (bf16[768,512]{1,0:T(8,128)(2,1)S(1)}, bf16[768,512]{1,0:T(8,128)(2,1)S(1)}, u32[]{:S(2)}, u32[]{:S(2)}) collective-permute-start(bf16[768,512]{1,0:T(8,128)(2,1)S(1)} %collective-permute-done.4.refs_4_.refs_2_.refs_5_), channel_id=1, source_target_pairs={{0,8},{8,16},{16,24},{24,28},{28,20},{20,12},{12,4},{4,0},{1,9},{9... | collective-permute-start | bytes 2359304 | tf_op jit(solution)/shard_map/ppermute | solution.py:112
  70.0 13.9 %collective-permute-start.16 = (bf16[512,512]{1,0:T(8,128)(2,1)S(1)}, bf16[512,512]{1,0:T(8,128)(2,1)S(1)}, u32[]{:S(2)}, u32[]{:S(2)}) collective-permute-start(bf16[512,512]{1,0:T(8,128)(2,1)S(1)} %shard_map.43.refs_1_.refs_3_), channel_id=1, source_target_pairs={{0,8},{8,16},{16,24},{24,28},{28,20},{20,12},{12,4},{4,0},{1,9},{9... | collective-permute-start | bytes 1572872 | tf_op jit(solution)/shard_map/ppermute | solution.py:112
  71.2 13.6 %collective-permute-start.17 = (bf16[512,512]{1,0:T(8,128)(2,1)S(1)}, bf16[512,512]{1,0:T(8,128)(2,1)S(1)}, u32[]{:S(2)}, u32[]{:S(2)}) collective-permute-start(bf16[512,512]{1,0:T(8,128)(2,1)S(1)} %shard_map.43.refs_1_.refs_3_), channel_id=1, source_target_pairs={{8,0},{16,8},{24,16},{28,24},{20,28},{12,20},{4,12},{0,4},{9,1},{1... | collective-permute-start | bytes 1572872 | tf_op jit(solution)/shard_map/ppermute | solution.py:115
  74.9 12.3 %collective-permute-start.13 = (bf16[512,896]{1,0:T(8,128)(2,1)S(1)}, bf16[512,896]{1,0:T(8,128)(2,1)S(1)}, u32[]{:S(2)}, u32[]{:S(2)}) collective-permute-start(bf16[512,896]{1,0:T(8,128)(2,1)S(1)} %shard_map.38.refs_3_), channel_id=1, source_target_pairs={{0,1},{1,0},{2,3},{3,2},{4,5},{5,4},{6,7},{7,6},{8,9},{9,8},{10,11... | collective-permute-start | bytes 2752520 | tf_op jit(solution)/shard_map/ppermute | solution.py:121
  75.8 11.3 %collective-permute-start.14 = (bf16[512,640]{1,0:T(8,128)(2,1)S(1)}, bf16[512,640]{1,0:T(8,128)(2,1)S(1)}, u32[]{:S(2)}, u32[]{:S(2)}) collective-permute-start(bf16[512,640]{1,0:T(8,128)(2,1)S(1)} %shard_map.41), channel_id=1, source_target_pairs={{0,1},{1,0},{2,3},{3,2},{4,5},{5,4},{6,7},{7,6},{8,9},{9,8},{10,11... | collective-permute-start | bytes 1966088 | tf_op jit(solution)/shard_map/ppermute | solution.py:121
  76.3 13.9 %collective-permute-start.15 = (bf16[512,512]{1,0:T(8,128)(2,1)S(1)}, bf16[512,512]{1,0:T(8,128)(2,1)S(1)}, u32[]{:S(2)}, u32[]{:S(2)}) collective-permute-start(bf16[512,512]{1,0:T(8,128)(2,1)S(1)} %get-tuple-element.48.refs_6_.refs_4_), channel_id=1, source_target_pairs={{0,2},{1,3},{2,0},{3,1},{4,6},{5,7},{6,4},{7,5},{8,10},{9,11},{10,... | collective-permute-start | bytes 1572872 | tf_op jit(solution)/shard_map/ppermute | solution.py:118
  84.9 12.8 %collective-permute-start.23 = (bf16[512,512]{1,0:T(8,128)(2,1)S(1)}, bf16[512,512]{1,0:T(8,128)(2,1)S(1)}, u32[]{:S(2)}, u32[]{:S(2)}) collective-permute-start(bf16[512,512]{1,0:T(8,128)(2,1)S(1)} %get-tuple-element.57.refs_3_.refs_1_.refs_6_), channel_id=1, source_target_pairs={{0,8},{8,16},{16,24},{24,28},{28,20},{20,12},{12,4},{4,0},{1,9},{9... | collective-permute-start | bytes 1572872 | tf_op jit(solution)/shard_map/ppermute | solution.py:112
  86.6 12.5 %collective-permute-start.24 = (bf16[512,512]{1,0:T(8,128)(2,1)S(1)}, bf16[512,512]{1,0:T(8,128)(2,1)S(1)}, u32[]{:S(2)}, u32[]{:S(2)}) collective-permute-start(bf16[512,512]{1,0:T(8,128)(2,1)S(1)} %get-tuple-element.61.refs_3_), channel_id=1, source_target_pairs={{8,0},{16,8},{24,16},{28,24},{20,28},{12,20},{4,12},{0,4},{9,1},{1... | collective-permute-start | bytes 1572872 | tf_op jit(solution)/shard_map/ppermute | solution.py:115
  90.4 15.9 %collective-permute-start.19 = (bf16[512,640]{1,0:T(8,128)(2,1)S(1)}, bf16[512,640]{1,0:T(8,128)(2,1)S(1)}, u32[]{:S(2)}, u32[]{:S(2)}) collective-permute-start(bf16[512,640]{1,0:T(8,128)(2,1)S(1)} %get-tuple-element.59), channel_id=1, source_target_pairs={{0,2},{1,3},{2,0},{3,1},{4,6},{5,7},{6,4},{7,5},{8,10},{9,11},{10,... | collective-permute-start | bytes 1966088 | tf_op jit(solution)/shard_map/ppermute | solution.py:118
  91.6 9.6 %collective-permute-start.22 = (bf16[512,512]{1,0:T(8,128)(2,1)S(1)}, bf16[512,512]{1,0:T(8,128)(2,1)S(1)}, u32[]{:S(2)}, u32[]{:S(2)}) collective-permute-start(bf16[512,512]{1,0:T(8,128)(2,1)S(1)} %get-tuple-element.61.refs_3_), channel_id=1, source_target_pairs={{0,1},{1,0},{2,3},{3,2},{4,5},{5,4},{6,7},{7,6},{8,9},{9,8},{10,11... | collective-permute-start | bytes 1572872 | tf_op jit(solution)/shard_map/ppermute | solution.py:121
  99.1 13.1 %collective-permute-start.26 = (bf16[512,512]{1,0:T(8,128)(2,1)S(1)}, bf16[512,512]{1,0:T(8,128)(2,1)S(1)}, u32[]{:S(2)}, u32[]{:S(2)}) collective-permute-start(bf16[512,512]{1,0:T(8,128)(2,1)S(1)} %get-tuple-element.63.refs_9_.refs_1_.refs_6_), channel_id=1, source_target_pairs={{0,8},{8,16},{16,24},{24,28},{28,20},{20,12},{12,4},{4,0},{1,9},{9... | collective-permute-start | bytes 1572872 | tf_op jit(solution)/shard_map/ppermute | solution.py:112
  100.8 12.7 %collective-permute-start.27 = (bf16[512,512]{1,0:T(8,128)(2,1)S(1)}, bf16[512,512]{1,0:T(8,128)(2,1)S(1)}, u32[]{:S(2)}, u32[]{:S(2)}) collective-permute-start(bf16[512,512]{1,0:T(8,128)(2,1)S(1)} %get-tuple-element.67.refs_3_.refs_9_), channel_id=1, source_target_pairs={{8,0},{16,8},{24,16},{28,24},{20,28},{12,20},{4,12},{0,4},{9,1},{1... | collective-permute-start | bytes 1572872 | tf_op jit(solution)/shard_map/ppermute | solution.py:115
  101.2 14.1 %collective-permute-start.31 = (bf16[512,512]{1,0:T(8,128)(2,1)S(1)}, bf16[512,512]{1,0:T(8,128)(2,1)S(1)}, u32[]{:S(2)}, u32[]{:S(2)}) collective-permute-start(bf16[512,512]{1,0:T(8,128)(2,1)S(1)} %get-tuple-element.63.refs_9_.refs_1_.refs_6_), channel_id=1, source_target_pairs={{0,1},{1,0},{2,3},{3,2},{4,5},{5,4},{6,7},{7,6},{8,9},{9,8},{10,11... | collective-permute-start | bytes 1572872 | tf_op jit(solution)/shard_map/ppermute | solution.py:121
  106.5 12.7 %collective-permute-start.30 = (bf16[512,640]{1,0:T(8,128)(2,1)S(1)}, bf16[512,640]{1,0:T(8,128)(2,1)S(1)}, u32[]{:S(2)}, u32[]{:S(2)}) collective-permute-start(bf16[512,640]{1,0:T(8,128)(2,1)S(1)} %get-tuple-element.68.refs_2_.refs_0_), channel_id=1, source_target_pairs={{0,1},{1,0},{2,3},{3,2},{4,5},{5,4},{6,7},{7,6},{8,9},{9,8},{10,11... | collective-permute-start | bytes 1966088 | tf_op jit(solution)/shard_map/ppermute | solution.py:121
  106.7 17.0 %collective-permute-start.25 = (bf16[512,640]{1,0:T(8,128)(2,1)S(1)}, bf16[512,640]{1,0:T(8,128)(2,1)S(1)}, u32[]{:S(2)}, u32[]{:S(2)}) collective-permute-start(bf16[512,640]{1,0:T(8,128)(2,1)S(1)} %get-tuple-element.65), channel_id=1, source_target_pairs={{0,2},{1,3},{2,0},{3,1},{4,6},{5,7},{6,4},{7,5},{8,10},{9,11},{10,... | collective-permute-start | bytes 1966088 | tf_op jit(solution)/shard_map/ppermute | solution.py:118
  124.9 10.4 %collective-permute-start.33 = (bf16[512,256]{1,0:T(8,128)(2,1)S(1)}, bf16[512,256]{1,0:T(8,128)(2,1)S(1)}, u32[]{:S(2)}, u32[]{:S(2)}) collective-permute-start(bf16[512,256]{1,0:T(8,128)(2,1)S(1)} %get-tuple-element.75), channel_id=1, source_target_pairs={{0,2},{1,3},{2,0},{3,1},{4,6},{5,7},{6,4},{7,5},{8,10},{9,11},{10,... | collective-permute-start | bytes 786440 | tf_op jit(solution)/shard_map/ppermute | solution.py:118
  (17 other events, 146.8 us)

commit v6 on v4

--- a/solution.py
+++ b/solution.py
@@ -401,8 +401,8 @@
     far = over_x(nq)
     sums = late_part([5, 6], sums, False, [s2])
     out = collect(2, [s2, over_core(s2)], out, False, sums[:1])
-    out = late_part([n - 1], sums, True, [], [p, out])[0]
     s3 = turned(q3, far, None, [out])[0]
+    out = late_part([n - 1], sums, True, [s3], [p, out])[0]
     return collect(3, [s3, over_core(s3)], out, True)
 
 

time: 139 us -> 139 us (level)
  transfers between devices with their start and end apart: 40 -> 40, of which waited for: 21 -> 22; matrix products, arithmetic and copies ran while one was open for 0% -> 0% of each run, Pallas kernels for 22% -> 22%
where the time goes in v6:
time: 139 us; the launch traced here: 138 us
  waiting for transfers between devices  74.3 us (53%)
  Pallas kernels  34.7 us (25%)
  starting transfers between devices  28.9 us (21%)
    ppermute x8, waiting for transfers between devices, down(): lax.ppermute(v, 'dp', [(ring[(i + 1) % n], ring[i]) for i in range(n)])  40.8 us
    pallas_call x33, Pallas kernels, call(): pl.pallas_call(kernel, out_shape=[pltpu.VMEM(*o) if isinstance(o, tuple)...  34.7 us
    ppermute x8, waiting for transfers between devices, up(): lax.ppermute(v, 'dp', [(ring[i], ring[(i + 1) % n]) for i in range(n)])  20.3 us
    ppermute x6, waiting for transfers between devices, over_x(): return lax.ppermute(v, 'tensor', [(t, t ^ 2) for t in range(4)])  11.8 us
    ppermute x8, starting transfers between devices, down(): lax.ppermute(v, 'dp', [(ring[(i + 1) % n], ring[i]) for i in range(n)])  9.42 us
    ppermute x6, starting transfers between devices, over_x(): return lax.ppermute(v, 'tensor', [(t, t ^ 2) for t in range(4)])  8.41 us
    ppermute x8, starting transfers between devices, up(): lax.ppermute(v, 'dp', [(ring[i], ring[(i + 1) % n]) for i in range(n)])  8.11 us
    ppermute x18, starting transfers between devices, over_core(): return lax.ppermute(v, 'tensor', [(t, t ^ 1) for t in range(4)])  3.01 us
  transfers between devices with their start and end apart: 40, of which 22 were waited for; matrix products, arithmetic and copies ran while one was open for 0% of the time, Pallas kernels for 22%

profile of v6, /device:TPU:0, one launch (start us, length us, event | category | flops | bytes accessed | tf_op | source)
XLA Modules:
  0.0 138.3 jit_solution(9196164857685756725)
XLA Ops:
  1.2 3.0 %collective-permute-start.6 = (bf16[768,512]{1,0:T(8,128)(2,1)S(1)}, bf16[768,512]{1,0:T(8,128)(2,1)S(1)}, u32[]{:S(2)}, u32[]{:S(2)}) collective-permute-start(bf16[768,512]{1,0:T(8,128)(2,1)S(1)} %shard_map.29.refs_1_.refs_4_.refs_3_.refs_2_), channel_id=1, source_target_pairs={{8,0},{16,8},{24,16},{28,24},{20,28},{12,20},{4,12},{0,4},{9,1},{1... | collective-permute-start | bytes 2359304 | tf_op jit(solution)/shard_map/ppermute | solution.py:115
  4.4 1.9 %collective-permute-start = (bf16[128,4096]{1,0:T(8,128)(2,1)}, bf16[128,4096]{1,0:T(8,128)(2,1)S(1)}, u32[]{:S(2)}, u32[]{:S(2)}) collective-permute-start(bf16[128,4096]{1,0:T(8,128)(2,1)} %refs_0_.3), channel_id=1, source_target_pairs={{0,2},{1,3},{2,0},{3,1},{4,6},{5,7},{6,4},{7,5},{8,10},{9,11},{10,... | collective-permute-start | bytes 3145736 | tf_op jit(solution)/shard_map/ppermute | solution.py:118
  6.3 15.6 %collective-permute-done.6.refs_3_.refs_2_.refs_1_.refs_6_ = bf16[768,512]{1,0:T(8,128)(2,1)S(1)} collective-permute-done((bf16[768,512]{1,0:T(8,128)(2,1)S(1)}, bf16[768,512]{1,0:T(8,128)(2,1)S(1)}, u32[]{:S(2)}, u32[]{:S(2)}) %collective-permute-start.6) | collective-permute-done | bytes 786464 | tf_op jit(solution)/shard_map/ppermute | solution.py:115
  21.9 1.7 %collective-permute-start.7 = (bf16[768,512]{1,0:T(8,128)(2,1)S(1)}, bf16[768,512]{1,0:T(8,128)(2,1)S(1)}, u32[]{:S(2)}, u32[]{:S(2)}) collective-permute-start(bf16[768,512]{1,0:T(8,128)(2,1)S(1)} %collective-permute-done.6.refs_3_.refs_2_.refs_1_.refs_6_), channel_id=1, source_target_pairs={{8,0},{16,8},{24,16},{28,24},{20,28},{12,20},{4,12},{0,4},{9,1},{1... | collective-permute-start | bytes 2359304 | tf_op jit(solution)/shard_map/ppermute | solution.py:115
  23.9 5.3 %collective-permute-done.refs_1_ = bf16[128,4096]{1,0:T(8,128)(2,1)S(1)} collective-permute-done((bf16[128,4096]{1,0:T(8,128)(2,1)}, bf16[128,4096]{1,0:T(8,128)(2,1)S(1)}, u32[]{:S(2)}, u32[]{:S(2)}) %collective-permute-start) | collective-permute-done | bytes 1048608 | tf_op jit(solution)/shard_map/ppermute | solution.py:118
  29.2 11.4 %collective-permute-done.7.refs_5_.refs_1_.refs_3_.refs_6_.refs_8_.refs_2_ = bf16[768,512]{1,0:T(8,128)(2,1)S(1)} collective-permute-done((bf16[768,512]{1,0:T(8,128)(2,1)S(1)}, bf16[768,512]{1,0:T(8,128)(2,1)S(1)}, u32[]{:S(2)}, u32[]{:S(2)}) %collective-permute-start.7) | collective-permute-done | bytes 786464 | tf_op jit(solution)/shard_map/ppermute | solution.py:115
  45.3 2.2 %shard_map.30.refs_2_.refs_3_ = f32[512,768]{1,0:T(8,128)S(1)} custom-call(bf16[512,4096]{1,0:T(8,128)(2,1)S(1)} %shard_map.28.refs_0_, bf16[768,512]{1,0:T(8,128)(2,1)S(1)} %shard_map.29.refs_1_.refs_4_.refs_3_.refs_2_, bf16[768,512]{1,0:T(8,128)(2,1)S(1)} %collective-permute-done.3.refs_2_.refs_1_.refs_5_, ...), custom_call_target="tpu_custom_call" | custom-call | flops 100663296 | bytes 406323 | tf_op jit(solution)/shard_map/pallas_call | solution.py:50
  47.6 2.5 %collective-permute-done.9.refs_3_.refs_1_ = bf16[256,512]{1,0:T(8,128)(2,1)S(1)} collective-permute-done((bf16[256,512]{1,0:T(8,128)(2,1)S(1)}, bf16[256,512]{1,0:T(8,128)(2,1)S(1)}, u32[]{:S(2)}, u32[]{:S(2)}) %collective-permute-start.9) | collective-permute-done | bytes 262176 | tf_op jit(solution)/shard_map/ppermute | solution.py:118
  50.0 8.4 %collective-permute-done.8.refs_1_.refs_2_.refs_3_.refs_6_.refs_8_ = bf16[768,512]{1,0:T(8,128)(2,1)S(1)} collective-permute-done((bf16[768,512]{1,0:T(8,128)(2,1)S(1)}, bf16[768,512]{1,0:T(8,128)(2,1)S(1)}, u32[]{:S(2)}, u32[]{:S(2)}) %collective-permute-start.8) | collective-permute-done | bytes 786464 | tf_op jit(solution)/shard_map/ppermute | solution.py:115
  62.7 4.9 %collective-permute-done.10.refs_1_.refs_4_.refs_5_.refs_2_ = bf16[384,512]{1,0:T(8,128)(2,1)S(1)} collective-permute-done((bf16[384,512]{1,0:T(8,128)(2,1)S(1)}, bf16[384,512]{1,0:T(8,128)(2,1)S(1)}, u32[]{:S(2)}, u32[]{:S(2)}) %collective-permute-start.10) | collective-permute-done | bytes 393248 | tf_op jit(solution)/shard_map/ppermute | solution.py:112
  77.5 1.8 %shard_map.44 = (f32[512,1024]{1,0:T(8,128)S(1)}, f32[1024,1024]{1,0:T(8,128)S(1)}) custom-call(bf16[512,4096]{1,0:T(8,128)(2,1)S(1)} %shard_map.28.refs_0_, bf16[512,512]{1,0:T(8,128)(2,1)S(1)} %shard_map.43.refs_1_.refs_3_, bf16[512,512]{1,0:T(8,128)(2,1)S(1)} %collective-permute-done.18.refs_2_.refs_4_, ...), custom_call_target="tpu_custom_call" | custom-call | flops 80530640 | bytes 301465 | tf_op jit(solution)/shard_map/pallas_call | solution.py:50
  79.3 4.6 %collective-permute-done.16.refs_0_ = bf16[512,512]{1,0:T(8,128)(2,1)S(1)} collective-permute-done((bf16[512,512]{1,0:T(8,128)(2,1)S(1)}, bf16[512,512]{1,0:T(8,128)(2,1)S(1)}, u32[]{:S(2)}, u32[]{:S(2)}) %collective-permute-start.16) | collective-permute-done | bytes 524320 | tf_op jit(solution)/shard_map/ppermute | solution.py:112
  88.2 2.0 %collective-permute-done.15.refs_1_ = bf16[512,512]{1,0:T(8,128)(2,1)S(1)} collective-permute-done((bf16[512,512]{1,0:T(8,128)(2,1)S(1)}, bf16[512,512]{1,0:T(8,128)(2,1)S(1)}, u32[]{:S(2)}, u32[]{:S(2)}) %collective-permute-start.15) | collective-permute-done | bytes 524320 | tf_op jit(solution)/shard_map/ppermute | solution.py:118
  92.1 5.6 %collective-permute-done.23.refs_0_ = bf16[512,512]{1,0:T(8,128)(2,1)S(1)} collective-permute-done((bf16[512,512]{1,0:T(8,128)(2,1)S(1)}, bf16[512,512]{1,0:T(8,128)(2,1)S(1)}, u32[]{:S(2)}, u32[]{:S(2)}) %collective-permute-start.23) | collective-permute-done | bytes 524320 | tf_op jit(solution)/shard_map/ppermute | solution.py:112
  99.1 1.7 %collective-permute-start.26 = (bf16[512,512]{1,0:T(8,128)(2,1)S(1)}, bf16[512,512]{1,0:T(8,128)(2,1)S(1)}, u32[]{:S(2)}, u32[]{:S(2)}) collective-permute-start(bf16[512,512]{1,0:T(8,128)(2,1)S(1)} %get-tuple-element.63.refs_9_.refs_1_.refs_6_), channel_id=1, source_target_pairs={{0,8},{8,16},{16,24},{24,28},{28,20},{20,12},{12,4},{4,0},{1,9},{9... | collective-permute-start | bytes 1572872 | tf_op jit(solution)/shard_map/ppermute | solution.py:112
  101.2 3.5 %shard_map.48 = (f32[512,1024]{1,0:T(8,128)S(1)}, f32[1024,1024]{1,0:T(8,128)S(1)}) custom-call(bf16[512,4096]{1,0:T(8,128)(2,1)S(1)} %shard_map.28.refs_0_, bf16[512,512]{1,0:T(8,128)(2,1)S(1)} %get-tuple-element.57.refs_3_.refs_1_.refs_6_, bf16[512,512]{1,0:T(8,128)(2,1)S(1)} %collective-permute-done.21.refs_2_.refs_7_, ...), custom_call_target="tpu_custom_call" | custom-call | flops 161061280 | bytes 707788 | tf_op jit(solution)/shard_map/pallas_call | solution.py:50
  108.2 4.0 %collective-permute-done.26.refs_0_ = bf16[512,512]{1,0:T(8,128)(2,1)S(1)} collective-permute-done((bf16[512,512]{1,0:T(8,128)(2,1)S(1)}, bf16[512,512]{1,0:T(8,128)(2,1)S(1)}, u32[]{:S(2)}, u32[]{:S(2)}) %collective-permute-start.26) | collective-permute-done | bytes 524320 | tf_op jit(solution)/shard_map/ppermute | solution.py:112
  113.6 1.7 %collective-permute-start.28 = (bf16[256,512]{1,0:T(8,128)(2,1)S(1)}, bf16[256,512]{1,0:T(8,128)(2,1)S(1)}, u32[]{:S(2)}, u32[]{:S(2)}) collective-permute-start(bf16[256,512]{1,0:T(8,128)(2,1)S(1)} %get-tuple-element.69), channel_id=1, source_target_pairs={{0,8},{8,16},{16,24},{24,28},{28,20},{20,12},{12,4},{4,0},{1,9},{9... | collective-permute-start | bytes 786440 | tf_op jit(solution)/shard_map/ppermute | solution.py:112
  115.7 3.4 %shard_map.52 = (f32[512,1024]{1,0:T(8,128)S(1)}, f32[1024,1024]{1,0:T(8,128)S(1)}) custom-call(bf16[512,4096]{1,0:T(8,128)(2,1)S(1)} %shard_map.28.refs_0_, bf16[512,512]{1,0:T(8,128)(2,1)S(1)} %get-tuple-element.63.refs_9_.refs_1_.refs_6_, bf16[512,512]{1,0:T(8,128)(2,1)S(1)} %collective-permute-done.31.refs_2_.refs_7_, ...), custom_call_target="tpu_custom_call" | custom-call | flops 161061280 | bytes 707788 | tf_op jit(solution)/shard_map/pallas_call | solution.py:50
  119.1 1.8 %shard_map.53.refs_2_.refs_11_ = f32[512,1024]{1,0:T(8,128)S(1)} custom-call(bf16[512,640]{1,0:T(8,128)(2,1)S(1)} %get-tuple-element.68.refs_2_.refs_0_, bf16[512,640]{1,0:T(8,128)(2,1)S(1)} %collective-permute-done.30.refs_1_, bf16[768,512]{1,0:T(8,128)(2,1)S(1)} %collective-permute-done.6.refs_3_.refs_2_.refs_1_.refs_6_, ...), custom_call_target="tpu_custom_call" | custom-call | flops 67108864 | bytes 445644 | tf_op jit(solution)/shard_map/pallas_call | solution.py:50
  127.5 3.4 %shard_map.56 = (f32[512,1024]{1,0:T(8,128)S(1)}, f32[1024,1024]{1,0:T(8,128)S(1)}) custom-call(bf16[512,4096]{1,0:T(8,128)(2,1)S(1)} %shard_map.28.refs_0_, bf16[512,512]{1,0:T(8,128)(2,1)S(1)} %get-tuple-element.72.refs_9_.refs_1_.refs_6_, bf16[512,512]{1,0:T(8,128)(2,1)S(1)} %collective-permute-done.35.refs_2_.refs_7_, ...), custom_call_target="tpu_custom_call" | custom-call | flops 161061280 | bytes 707788 | tf_op jit(solution)/shard_map/pallas_call | solution.py:50
  130.9 1.8 %shard_map.57.refs_2_.refs_10_ = f32[512,1024]{1,0:T(8,128)S(1)} custom-call(bf16[512,640]{1,0:T(8,128)(2,1)S(1)} %get-tuple-element.76.refs_9_.refs_0_, bf16[512,640]{1,0:T(8,128)(2,1)S(1)} %collective-permute-done.34.refs_1_, bf16[768,512]{1,0:T(8,128)(2,1)S(1)} %collective-permute-done.7.refs_5_.refs_1_.refs_3_.refs_6_.refs_8_.refs_2_, ...), custom_call_target="tpu_custom_call" | custom-call | flops 67108864 | bytes 445644 | tf_op jit(solution)/shard_map/pallas_call | solution.py:50
  133.3 3.2 %shard_map.59.refs_8_ = f32[512,1024]{1,0:T(8,128)S(1)} custom-call(bf16[512,4096]{1,0:T(8,128)(2,1)S(1)} %shard_map.28.refs_0_, bf16[256,512]{1,0:T(8,128)(2,1)S(1)} %get-tuple-element.74.refs_3_.refs_1_.refs_4_, bf16[256,512]{1,0:T(8,128)(2,1)S(1)} %get-tuple-element.80.refs_2_.refs_5_, bf16[256,512]{1,0:T(8,128)(2,1)S(1)} %collective-permute-done.38.refs_3_.refs_6_, ...), custom_call_target="tpu_custom_call" | custom-call | flops 80530640 | bytes 799539 | tf_op jit(solution)/shard_map/pallas_call | solution.py:50
  136.5 1.8 %shard_map.60 = bf16[512,1024]{1,0:T(8,128)(2,1)} custom-call(bf16[512,256]{1,0:T(8,128)(2,1)S(1)} %shard_map.58.refs_11_.refs_0_, bf16[512,256]{1,0:T(8,128)(2,1)S(1)} %collective-permute-done.37.refs_1_, bf16[384,512]{1,0:T(8,128)(2,1)S(1)} %collective-permute-done.10.refs_1_.refs_4_.refs_5_.refs_2_, ...), custom_call_target="tpu_custom_call" | custom-call | flops 26843544 | bytes 222822 | tf_op jit(solution)/shard_map/pallas_call | solution.py:50
  (91 shorter events, 40.8 us)
Async XLA Ops:
  1.2 20.6 %collective-permute-start.6 = (bf16[768,512]{1,0:T(8,128)(2,1)S(1)}, bf16[768,512]{1,0:T(8,128)(2,1)S(1)}, u32[]{:S(2)}, u32[]{:S(2)}) collective-permute-start(bf16[768,512]{1,0:T(8,128)(2,1)S(1)} %shard_map.29.refs_1_.refs_4_.refs_3_.refs_2_), channel_id=1, source_target_pairs={{8,0},{16,8},{24,16},{28,24},{20,28},{12,20},{4,12},{0,4},{9,1},{1... | collective-permute-start | bytes 2359304 | tf_op jit(solution)/shard_map/ppermute | solution.py:115
  4.3 19.3 %collective-permute-start.3 = (bf16[768,512]{1,0:T(8,128)(2,1)S(1)}, bf16[768,512]{1,0:T(8,128)(2,1)S(1)}, u32[]{:S(2)}, u32[]{:S(2)}) collective-permute-start(bf16[768,512]{1,0:T(8,128)(2,1)S(1)} %shard_map.29.refs_1_.refs_4_.refs_3_.refs_2_), channel_id=1, source_target_pairs={{0,8},{8,16},{16,24},{24,28},{28,20},{20,12},{12,4},{4,0},{1,9},{9... | collective-permute-start | bytes 2359304 | tf_op jit(solution)/shard_map/ppermute | solution.py:112
  4.4 24.8 %collective-permute-start = (bf16[128,4096]{1,0:T(8,128)(2,1)}, bf16[128,4096]{1,0:T(8,128)(2,1)S(1)}, u32[]{:S(2)}, u32[]{:S(2)}) collective-permute-start(bf16[128,4096]{1,0:T(8,128)(2,1)} %refs_0_.3), channel_id=1, source_target_pairs={{0,2},{1,3},{2,0},{3,1},{4,6},{5,7},{6,4},{7,5},{8,10},{9,11},{10,... | collective-permute-start | bytes 3145736 | tf_op jit(solution)/shard_map/ppermute | solution.py:118
  21.9 18.7 %collective-permute-start.7 = (bf16[768,512]{1,0:T(8,128)(2,1)S(1)}, bf16[768,512]{1,0:T(8,128)(2,1)S(1)}, u32[]{:S(2)}, u32[]{:S(2)}) collective-permute-start(bf16[768,512]{1,0:T(8,128)(2,1)S(1)} %collective-permute-done.6.refs_3_.refs_2_.refs_1_.refs_6_), channel_id=1, source_target_pairs={{8,0},{16,8},{24,16},{28,24},{20,28},{12,20},{4,12},{0,4},{9,1},{1... | collective-permute-start | bytes 2359304 | tf_op jit(solution)/shard_map/ppermute | solution.py:115
  23.5 18.4 %collective-permute-start.4 = (bf16[768,512]{1,0:T(8,128)(2,1)S(1)}, bf16[768,512]{1,0:T(8,128)(2,1)S(1)}, u32[]{:S(2)}, u32[]{:S(2)}) collective-permute-start(bf16[768,512]{1,0:T(8,128)(2,1)S(1)} %collective-permute-done.3.refs_2_.refs_1_.refs_5_), channel_id=1, source_target_pairs={{0,8},{8,16},{16,24},{24,28},{28,20},{20,12},{12,4},{4,0},{1,9},{9... | collective-permute-start | bytes 2359304 | tf_op jit(solution)/shard_map/ppermute | solution.py:112
  23.9 21.1 %collective-permute-start.1 = (bf16[128,4096]{1,0:T(8,128)(2,1)}, bf16[128,4096]{1,0:T(8,128)(2,1)S(1)}, u32[]{:S(2)}, u32[]{:S(2)}) collective-permute-start(bf16[128,4096]{1,0:T(8,128)(2,1)} %refs_0_.3), channel_id=1, source_target_pairs={{0,1},{1,0},{2,3},{3,2},{4,5},{5,4},{6,7},{7,6},{8,9},{9,8},{10,11... | collective-permute-start | bytes 3145736 | tf_op jit(solution)/shard_map/ppermute | solution.py:121
  29.2 15.8 %collective-permute-start.2 = (bf16[128,4096]{1,0:T(8,128)(2,1)S(1)}, bf16[128,4096]{1,0:T(8,128)(2,1)S(1)}, u32[]{:S(2)}, u32[]{:S(2)}) collective-permute-start(bf16[128,4096]{1,0:T(8,128)(2,1)S(1)} %collective-permute-done.refs_1_), channel_id=1, source_target_pairs={{0,1},{1,0},{2,3},{3,2},{4,5},{5,4},{6,7},{7,6},{8,9},{9,8},{10,11... | collective-permute-start | bytes 3145736 | tf_op jit(solution)/shard_map/ppermute | solution.py:121
  40.6 17.8 %collective-permute-start.8 = (bf16[768,512]{1,0:T(8,128)(2,1)S(1)}, bf16[768,512]{1,0:T(8,128)(2,1)S(1)}, u32[]{:S(2)}, u32[]{:S(2)}) collective-permute-start(bf16[768,512]{1,0:T(8,128)(2,1)S(1)} %collective-permute-done.7.refs_5_.refs_1_.refs_3_.refs_6_.refs_8_.refs_2_), channel_id=1, source_target_pairs={{8,0},{16,8},{24,16},{28,24},{20,28},{12,20},{4,12},{0,4},{9,1},{1... | collective-permute-start | bytes 2359304 | tf_op jit(solution)/shard_map/ppermute | solution.py:115
  42.0 17.6 %collective-permute-start.5 = (bf16[768,512]{1,0:T(8,128)(2,1)S(1)}, bf16[768,512]{1,0:T(8,128)(2,1)S(1)}, u32[]{:S(2)}, u32[]{:S(2)}) collective-permute-start(bf16[768,512]{1,0:T(8,128)(2,1)S(1)} %collective-permute-done.4.refs_4_.refs_2_.refs_5_), channel_id=1, source_target_pairs={{0,8},{8,16},{16,24},{24,28},{28,20},{20,12},{12,4},{4,0},{1,9},{9... | collective-permute-start | bytes 2359304 | tf_op jit(solution)/shard_map/ppermute | solution.py:112
  70.0 13.9 %collective-permute-start.16 = (bf16[512,512]{1,0:T(8,128)(2,1)S(1)}, bf16[512,512]{1,0:T(8,128)(2,1)S(1)}, u32[]{:S(2)}, u32[]{:S(2)}) collective-permute-start(bf16[512,512]{1,0:T(8,128)(2,1)S(1)} %shard_map.43.refs_1_.refs_3_), channel_id=1, source_target_pairs={{0,8},{8,16},{16,24},{24,28},{28,20},{20,12},{12,4},{4,0},{1,9},{9... | collective-permute-start | bytes 1572872 | tf_op jit(solution)/shard_map/ppermute | solution.py:112
  71.2 13.6 %collective-permute-start.17 = (bf16[512,512]{1,0:T(8,128)(2,1)S(1)}, bf16[512,512]{1,0:T(8,128)(2,1)S(1)}, u32[]{:S(2)}, u32[]{:S(2)}) collective-permute-start(bf16[512,512]{1,0:T(8,128)(2,1)S(1)} %shard_map.43.refs_1_.refs_3_), channel_id=1, source_target_pairs={{8,0},{16,8},{24,16},{28,24},{20,28},{12,20},{4,12},{0,4},{9,1},{1... | collective-permute-start | bytes 1572872 | tf_op jit(solution)/shard_map/ppermute | solution.py:115
  74.9 13.1 %collective-permute-start.13 = (bf16[512,896]{1,0:T(8,128)(2,1)S(1)}, bf16[512,896]{1,0:T(8,128)(2,1)S(1)}, u32[]{:S(2)}, u32[]{:S(2)}) collective-permute-start(bf16[512,896]{1,0:T(8,128)(2,1)S(1)} %shard_map.38.refs_3_), channel_id=1, source_target_pairs={{0,1},{1,0},{2,3},{3,2},{4,5},{5,4},{6,7},{7,6},{8,9},{9,8},{10,11... | collective-permute-start | bytes 2752520 | tf_op jit(solution)/shard_map/ppermute | solution.py:121
  75.8 12.0 %collective-permute-start.14 = (bf16[512,640]{1,0:T(8,128)(2,1)S(1)}, bf16[512,640]{1,0:T(8,128)(2,1)S(1)}, u32[]{:S(2)}, u32[]{:S(2)}) collective-permute-start(bf16[512,640]{1,0:T(8,128)(2,1)S(1)} %shard_map.41), channel_id=1, source_target_pairs={{0,1},{1,0},{2,3},{3,2},{4,5},{5,4},{6,7},{7,6},{8,9},{9,8},{10,11... | collective-permute-start | bytes 1966088 | tf_op jit(solution)/shard_map/ppermute | solution.py:121
  76.3 13.9 %collective-permute-start.15 = (bf16[512,512]{1,0:T(8,128)(2,1)S(1)}, bf16[512,512]{1,0:T(8,128)(2,1)S(1)}, u32[]{:S(2)}, u32[]{:S(2)}) collective-permute-start(bf16[512,512]{1,0:T(8,128)(2,1)S(1)} %get-tuple-element.48.refs_6_.refs_4_), channel_id=1, source_target_pairs={{0,2},{1,3},{2,0},{3,1},{4,6},{5,7},{6,4},{7,5},{8,10},{9,11},{10,... | collective-permute-start | bytes 1572872 | tf_op jit(solution)/shard_map/ppermute | solution.py:118
  84.9 12.8 %collective-permute-start.23 = (bf16[512,512]{1,0:T(8,128)(2,1)S(1)}, bf16[512,512]{1,0:T(8,128)(2,1)S(1)}, u32[]{:S(2)}, u32[]{:S(2)}) collective-permute-start(bf16[512,512]{1,0:T(8,128)(2,1)S(1)} %get-tuple-element.57.refs_3_.refs_1_.refs_6_), channel_id=1, source_target_pairs={{0,8},{8,16},{16,24},{24,28},{28,20},{20,12},{12,4},{4,0},{1,9},{9... | collective-permute-start | bytes 1572872 | tf_op jit(solution)/shard_map/ppermute | solution.py:112
  86.6 12.5 %collective-permute-start.24 = (bf16[512,512]{1,0:T(8,128)(2,1)S(1)}, bf16[512,512]{1,0:T(8,128)(2,1)S(1)}, u32[]{:S(2)}, u32[]{:S(2)}) collective-permute-start(bf16[512,512]{1,0:T(8,128)(2,1)S(1)} %get-tuple-element.61.refs_3_), channel_id=1, source_target_pairs={{8,0},{16,8},{24,16},{28,24},{20,28},{12,20},{4,12},{0,4},{9,1},{1... | collective-permute-start | bytes 1572872 | tf_op jit(solution)/shard_map/ppermute | solution.py:115
  90.4 15.9 %collective-permute-start.19 = (bf16[512,640]{1,0:T(8,128)(2,1)S(1)}, bf16[512,640]{1,0:T(8,128)(2,1)S(1)}, u32[]{:S(2)}, u32[]{:S(2)}) collective-permute-start(bf16[512,640]{1,0:T(8,128)(2,1)S(1)} %get-tuple-element.59), channel_id=1, source_target_pairs={{0,2},{1,3},{2,0},{3,1},{4,6},{5,7},{6,4},{7,5},{8,10},{9,11},{10,... | collective-permute-start | bytes 1966088 | tf_op jit(solution)/shard_map/ppermute | solution.py:118
  91.6 9.2 %collective-permute-start.21 = (bf16[512,512]{1,0:T(8,128)(2,1)S(1)}, bf16[512,512]{1,0:T(8,128)(2,1)S(1)}, u32[]{:S(2)}, u32[]{:S(2)}) collective-permute-start(bf16[512,512]{1,0:T(8,128)(2,1)S(1)} %get-tuple-element.57.refs_3_.refs_1_.refs_6_), channel_id=1, source_target_pairs={{0,1},{1,0},{2,3},{3,2},{4,5},{5,4},{6,7},{7,6},{8,9},{9,8},{10,11... | collective-permute-start | bytes 1572872 | tf_op jit(solution)/shard_map/ppermute | solution.py:121
  91.6 9.6 %collective-permute-start.22 = (bf16[512,512]{1,0:T(8,128)(2,1)S(1)}, bf16[512,512]{1,0:T(8,128)(2,1)S(1)}, u32[]{:S(2)}, u32[]{:S(2)}) collective-permute-start(bf16[512,512]{1,0:T(8,128)(2,1)S(1)} %get-tuple-element.61.refs_3_), channel_id=1, source_target_pairs={{0,1},{1,0},{2,3},{3,2},{4,5},{5,4},{6,7},{7,6},{8,9},{9,8},{10,11... | collective-permute-start | bytes 1572872 | tf_op jit(solution)/shard_map/ppermute | solution.py:121
  99.1 13.1 %collective-permute-start.26 = (bf16[512,512]{1,0:T(8,128)(2,1)S(1)}, bf16[512,512]{1,0:T(8,128)(2,1)S(1)}, u32[]{:S(2)}, u32[]{:S(2)}) collective-permute-start(bf16[512,512]{1,0:T(8,128)(2,1)S(1)} %get-tuple-element.63.refs_9_.refs_1_.refs_6_), channel_id=1, source_target_pairs={{0,8},{8,16},{16,24},{24,28},{28,20},{20,12},{12,4},{4,0},{1,9},{9... | collective-permute-start | bytes 1572872 | tf_op jit(solution)/shard_map/ppermute | solution.py:112
  100.8 12.7 %collective-permute-start.27 = (bf16[512,512]{1,0:T(8,128)(2,1)S(1)}, bf16[512,512]{1,0:T(8,128)(2,1)S(1)}, u32[]{:S(2)}, u32[]{:S(2)}) collective-permute-start(bf16[512,512]{1,0:T(8,128)(2,1)S(1)} %get-tuple-element.67.refs_3_.refs_9_), channel_id=1, source_target_pairs={{8,0},{16,8},{24,16},{28,24},{20,28},{12,20},{4,12},{0,4},{9,1},{1... | collective-permute-start | bytes 1572872 | tf_op jit(solution)/shard_map/ppermute | solution.py:115
  101.2 14.1 %collective-permute-start.31 = (bf16[512,512]{1,0:T(8,128)(2,1)S(1)}, bf16[512,512]{1,0:T(8,128)(2,1)S(1)}, u32[]{:S(2)}, u32[]{:S(2)}) collective-permute-start(bf16[512,512]{1,0:T(8,128)(2,1)S(1)} %get-tuple-element.63.refs_9_.refs_1_.refs_6_), channel_id=1, source_target_pairs={{0,1},{1,0},{2,3},{3,2},{4,5},{5,4},{6,7},{7,6},{8,9},{9,8},{10,11... | collective-permute-start | bytes 1572872 | tf_op jit(solution)/shard_map/ppermute | solution.py:121
  106.5 12.7 %collective-permute-start.30 = (bf16[512,640]{1,0:T(8,128)(2,1)S(1)}, bf16[512,640]{1,0:T(8,128)(2,1)S(1)}, u32[]{:S(2)}, u32[]{:S(2)}) collective-permute-start(bf16[512,640]{1,0:T(8,128)(2,1)S(1)} %get-tuple-element.68.refs_2_.refs_0_), channel_id=1, source_target_pairs={{0,1},{1,0},{2,3},{3,2},{4,5},{5,4},{6,7},{7,6},{8,9},{9,8},{10,11... | collective-permute-start | bytes 1966088 | tf_op jit(solution)/shard_map/ppermute | solution.py:121
  106.7 17.0 %collective-permute-start.25 = (bf16[512,640]{1,0:T(8,128)(2,1)S(1)}, bf16[512,640]{1,0:T(8,128)(2,1)S(1)}, u32[]{:S(2)}, u32[]{:S(2)}) collective-permute-start(bf16[512,640]{1,0:T(8,128)(2,1)S(1)} %get-tuple-element.65), channel_id=1, source_target_pairs={{0,2},{1,3},{2,0},{3,1},{4,6},{5,7},{6,4},{7,5},{8,10},{9,11},{10,... | collective-permute-start | bytes 1966088 | tf_op jit(solution)/shard_map/ppermute | solution.py:118
  (17 other events, 141.5 us)
